TPU v7x, 32 devices: a whole 2x2x4 slice. The times are simulated.
32 devices in a mesh: grp: 2 (over y), vec: 4 (over z), wlk: 4 (over x, core).
Axes of the slice: x: 2, y: 2, z: 4, core: 2. Of those that a mesh axis runs over, the one named last changes fastest.
Arguments:
- cholesky: bfloat16 [48, 64, 512], P(('grp', 'vec')), parts along dimension 0
- orbitals: float32 [32, 64, 512], P(('grp', 'vec', 'wlk')), parts along dimension 0, may hold values from -6 to 6
- log_weights: float32 [32], P(('grp', 'vec', 'wlk')), parts along dimension 0, may hold values from -6 to 6
- parents: int32 [32], P(('grp', 'vec', 'wlk')), parts along dimension 0, may hold values from 0 to 3
- propagator: float32 [1024, 512], P('grp'), parts along dimension 0
Outputs:
- new_orbitals: float32 [32, 64, 512], P(('grp', 'vec', 'wlk')), parts along dimension 0
- new_log_weights: float32 [32], P(('grp', 'vec', 'wlk')), parts along dimension 0
There are 2 independent parts, one for each index of `grp`. A program takes and returns all parts, laid end to end along the dimension named above; each array names one. Nothing has to cross between parts.
Inputs may be any that keep to these rules, and one draw needn't show every extreme that they name: parents[w] counts within the aligned block of 4 consecutive walkers that holds w.
All inputs are finite; a program needn't handle non-finite values.
Results may differ from a plain program's by a relative error of at most 0.02.
Values may be sent and summed in bfloat16 or wider, within the bound.
No kernel may reach another device: no remote copies, remote signals or barrier semaphores. Data moves between devices by JAX's collectives and lax.ppermute only.
A program may use at most 64 MiB of HBM per device.

v0:
```python
import math

import jax
import jax.numpy as jnp
from jax import lax
from jax.sharding import PartitionSpec as P

NS_ITERS = 2


gradient_step = 0.25
energy_step = 0.002
epsilon = 1e-06


def local(cholesky, orbitals, log_weights, parents, propagator):
    walker_count, occupied, basis = orbitals.shape
    vectors_here = cholesky.shape[0]
    norm_scale = 1.0 / math.sqrt(vectors_here * lax.axis_size("vec"))
    chol_flat = cholesky.reshape(vectors_here * occupied, basis)
    theta = orbitals.astype(jnp.bfloat16)
    gathered = lax.all_gather(theta, "vec", axis=0, tiled=True)
    row_count = gathered.shape[0]
    flattened = gathered.reshape(row_count * occupied, basis)
    product = lax.dot_general(
        flattened, chol_flat, (((1,), (1,)), ((), ())), preferred_element_type=jnp.float32
    )
    rotated = product.astype(jnp.bfloat16).reshape(row_count, occupied, vectors_here * occupied)
    group_count = rotated.shape[0]
    blocks = rotated.reshape(group_count, occupied, vectors_here, occupied).astype(jnp.float32)
    identity = jnp.eye(occupied, dtype=jnp.float32)
    traces = jnp.sum(blocks * identity[None, :, None, :], axis=(1, 3))
    swapped = jnp.transpose(blocks, (0, 3, 2, 1))
    exchange_sum = jnp.sum(blocks * swapped, axis=(1, 3))
    energy_part = 0.5 * norm_scale * jnp.sum(traces * traces - exchange_sum, axis=1)
    adjoint = norm_scale * (traces[:, None, :, None] * identity[None, :, None, :] - swapped)
    adjoint = adjoint.astype(jnp.bfloat16).reshape(group_count, occupied, vectors_here * occupied)
    energy = lax.psum_scatter(energy_part, "vec", scatter_dimension=0, tiled=True)
    row_count = lax.axis_size("vec") * walker_count
    flattened = adjoint.reshape(row_count * occupied, vectors_here * occupied)
    gradient_part = jnp.dot(flattened, chol_flat, preferred_element_type=jnp.float32)
    gradient = lax.psum_scatter(
        gradient_part.reshape(row_count, occupied, basis), "vec", scatter_dimension=0, tiled=True
    )
    stepped = orbitals - gradient_step * gradient
    shifted = log_weights - energy_step * energy
    row_block = lax.all_gather(stepped, "wlk", axis=0, tiled=True)
    log_block = lax.all_gather(shifted, "wlk", axis=0, tiled=True)
    row_count = row_block.shape[0]
    candidates = jnp.arange(row_count, dtype=jnp.int32)
    selector = (parents[:, None] == candidates[None, :]).astype(jnp.float32)
    picked = jnp.einsum("km,mjp->kjp", selector, row_block, precision=lax.Precision.HIGHEST)
    picked_logs = jnp.dot(selector, log_block, precision=lax.Precision.HIGHEST)
    propagated = lax.dot_general(
        picked, propagator, (((2,), (1,)), ((), ())), precision=lax.Precision.HIGHEST
    )
    mean_square = jnp.mean(propagated * propagated, axis=(1, 2))
    current = propagated / jnp.sqrt(mean_square + epsilon)[:, None, None]
    for repeat_index in range(NS_ITERS):
        intersection = (
            jnp.einsum("wjp,wkp->wjk", current, current, precision=lax.Precision.HIGHEST) / basis
        )
        current = 0.5 * (
            3.0 * current
            - jnp.einsum("wjk,wkp->wjp", intersection, current, precision=lax.Precision.HIGHEST)
        )
    return (current, picked_logs)


def solution(mesh):
    placed = (
        P(("grp", "vec"), None, None),
        P(("grp", "vec", "wlk"), None, None),
        P(("grp", "vec", "wlk")),
        P(("grp", "vec", "wlk")),
        P("grp", None),
    )
    return jax.shard_map(
        local,
        mesh=mesh,
        in_specs=placed,
        out_specs=(P(("grp", "vec", "wlk"), None, None), P(("grp", "vec", "wlk"))),
        check_vma=False,
    )
```

profile of v0, /device:TPU:0, one launch (start us, length us, event | category | flops | bytes accessed | tf_op | source)
XLA Modules:
  0.0 71.3 jit_solution(4510532308159012636)
XLA Ops:
  7.2 0.0 copy-start
  7.2 0.0 copy-start.1
  7.2 0.0 reduce-scatter.2.cloned.1.call-start
  7.2 1.0 %convert_element_type.25 = bf16[1,64,512]{2,1,0:T(8,128)(2,1)S(1)} convert(f32[1,64,512]{2,1,0:T(8,128)} %param.6) | non-fusion elementwise | flops 32768 | bytes 196608 | tf_op jit(solution)/shard_map/convert_element_type | solution.py:21
  8.3 15.6 %all_gather.9 = bf16[4,64,512]{2,1,0:T(8,128)(2,1)S(1)} all-gather(bf16[1,64,512]{2,1,0:T(8,128)(2,1)S(1)} %convert_element_type.25), channel_id=1, replica_groups=mesh['grp'=2,'vec'=4,'wlk'=4] {'vec'}, dimensions={0}, use_global_device_ids=true | all-gather | bytes 327680 | tf_op jit(solution)/shard_map/all_gather | solution.py:22
  23.9 0.0 copy-done.1
  23.9 0.3 fusion
  24.2 0.2 copy.10
  24.4 0.3 reshape.80
  24.8 0.3 copy.11
  25.1 0.5 fusion.5
  25.6 0.3 fusion.4
  25.9 1.1 %convolution_bitcast_fusion = f32[4,64,512]{2,1,0:T(8,128)} fusion(bf16[6,64,512]{2,1,0:T(8,128)(2,1)S(1)} %copy-done.1, bf16[4,64,6,64]{1,0,3,2:T(4,128)(2,1)S(1)} %fusion.4), kind=kOutput, calls=%fused_computation | convolution fusion | flops 100663296 | bytes 1114112 | tf_op jit(solution)/shard_map/dot_general | solution.py:41
  27.0 0.0 copy-start.2
  27.0 0.0 reduce-scatter.2.cloned.1.call-update
  27.1 12.3 %all-reduce.1 = f32[4]{0:T(128)S(1)} all-reduce(f32[4]{0:T(128)S(1)} %broadcast_multiply_fusion), channel_id=3, replica_groups=mesh['grp'=2,'vec'=4,'wlk'=4] {'vec'}, use_global_device_ids=true, to_apply=%region_5.0.clone | all-reduce | flops 4 | bytes 32
  40.0 0.0 copy-start.4
  40.0 0.6 copy-done.4
  40.6 0.6 dynamic-slice.1
  41.2 0.0 copy-start.3
  41.2 0.7 copy-done.3
  41.9 0.6 dynamic-slice
  42.5 1.5 %fusion.23 = f32[4]{0:T(128)S(1)} fusion(f32[4]{0:T(128)S(1)} %broadcast.34, u32[]{:T(128)} %bitcast.10, f32[1]{0:T(128)S(6)} %copy.29, f32[4]{0:T(128)S(1)} %all-reduce.1, u32[]{:T(128)} %bitcast.12), kind=kLoop, calls=%fused_computation.39 | loop fusion | flops 2 | bytes 540
  43.9 6.0 %all-reduce = f32[4]{0:T(128)S(1)} all-reduce(f32[4]{0:T(128)S(1)} %fusion.23), channel_id=1, replica_groups=mesh['grp'=2,'vec'=4,'wlk'=4] {'wlk'}, use_global_device_ids=true, to_apply=%add | all-reduce | flops 4 | bytes 32
  50.6 0.6 fusion.21
  51.2 0.0 reduce-scatter.2.cloned.1.call-done
  51.2 0.0 copy-done.2
  51.2 0.9 %multiply_subtract_fusion = f32[1,64,512]{2,1,0:T(8,128)S(1)} fusion(f32[1,64,512]{2,1,0:T(8,128)S(1)} %copy-done.2, f32[1,64,512]{2,1,0:T(8,128)} %reduce-scatter.2.cloned.1.call-done), kind=kLoop, calls=%fused_computation.23 | loop fusion | flops 65536 | bytes 393216 | tf_op jit(solution)/shard_map/sub | solution.py:45
  52.1 7.2 %all_gather.10 = f32[4,64,512]{2,1,0:T(8,128)S(1)} all-gather(f32[1,64,512]{2,1,0:T(8,128)S(1)} %multiply_subtract_fusion), channel_id=1, replica_groups=mesh['grp'=2,'vec'=4,'wlk'=4] {'wlk'}, dimensions={0}, use_global_device_ids=true | all-gather | bytes 655360 | tf_op jit(solution)/shard_map/all_gather | solution.py:47
  59.3 0.9 %fusion.6 = f32[1,64,512]{2,0,1:T(1,128)S(1)} fusion(f32[4,64,512]{2,1,0:T(8,128)S(1)} %all_gather.10, s32[]{:T(128)} %bitcast.38), kind=kOutput, calls=%fused_computation.15 | convolution fusion | flops 1572868 | bytes 655364 | tf_op jit(solution)/shard_map/km,mjp->kjp/dot_general | solution.py:52
  60.2 0.0 copy-done
  60.2 1.7 %multiply_reduce_fusion.1 = (f32[]{:T(128)}, f32[64,512]{1,0:T(8,128)S(1)}) fusion(f32[512,512]{1,0:T(8,128)S(1)} %copy-done, f32[1,64,512]{2,0,1:T(1,128)S(1)} %fusion.6), kind=kOutput, calls=%fused_computation.22 | convolution fusion | flops 201392128 | bytes 1310724 | tf_op jit(solution)/shard_map/dot_general | solution.py:54
  62.7 0.3 convolution_multiply_fusion.1
  62.9 0.3 convolution_subtract_fusion.1
  63.2 0.3 convolution_multiply_fusion
  63.5 0.9 %fusion.2 = f32[1,64,512]{2,1,0:T(8,128)} fusion(f32[64,64]{1,0:T(8,128)S(1)} %convolution_multiply_fusion, f32[64,512]{1,0:T(8,128)S(1)} %convolution_subtract_fusion.1), kind=kOutput, calls=%fused_computation.6 | convolution fusion | flops 25296896 | bytes 278528 | tf_op jit(solution)/shard_map/wjk,wkp->wjp/dot_general | solution.py:65
  (4 shorter events, 0.0 us)
Async XLA Ops:
  7.2 53.1 %copy-start = (f32[512,512]{1,0:T(8,128)S(1)}, f32[512,512]{1,0:T(8,128)}, u32[]{:S(2)}) copy-start(f32[512,512]{1,0:T(8,128)} %param.9) | copy-start | bytes 3145732
  7.2 16.7 %copy-start.1 = (bf16[6,64,512]{2,1,0:T(8,128)(2,1)S(1)}, bf16[6,64,512]{2,1,0:T(8,128)(2,1)}, u32[]{:S(2)}) copy-start(bf16[6,64,512]{2,1,0:T(8,128)(2,1)} %param.5) | copy-start | bytes 1179652
  7.2 44.0 %reduce-scatter.2.cloned.1.call-start = ((), (), s32[]{:S(2)}) async-start(), calls=%async_computation.1 | async-start | bytes 655360 | tf_op jit(solution)/shard_map/reduce_scatter | solution.py:42
  27.0 24.2 %copy-start.2 = (f32[1,64,512]{2,1,0:T(8,128)S(1)}, f32[1,64,512]{2,1,0:T(8,128)}, u32[]{:S(2)}) copy-start(f32[1,64,512]{2,1,0:T(8,128)} %param.6) | copy-start | bytes 393220
  40.0 0.7 copy-start.4
  41.2 0.7 copy-start.3
Sparse Core Ops, SparseCore 0:
  27.2 23.2 reduce-scatter.1
where the time goes:
time: 71.5 us; the launch traced here: 71.3 us
  blocking collectives  41.1 us (57%)
  between operations  16.1 us (23%)
  matrix products  5.77 us (8%)
  other arithmetic  4.87 us (7%)
  local copies, waits for them, and re-layouts  3.31 us (5%)
    unnamed x2, blocking collectives  18.3 us
    all_gather x1, blocking collectives, local(): gathered = lax.all_gather(theta, 'vec', axis=0, tiled=True)  15.6 us
    all_gather x1, blocking collectives, local(): row_block = lax.all_gather(stepped, 'wlk', axis=0, tiled=True)  7.18 us
    unnamed x13, local copies, waits for them, and re-layouts  2.49 us
    dot_general x1, matrix products, local(): lax.dot_general(picked, propagator, (((2,), (1,)), ((), ())), precision=l...  1.74 us
    unnamed x1, other arithmetic  1.46 us
  transfers between devices with their start and end apart: 1, of which 0 were waited for; matrix products, arithmetic and copies ran while one was open for 5% of the time, Pallas kernels for 0%

commit v1 on v0

v1 whole, which is shorter than its diff:
```python
import functools
import math

import jax
import jax.numpy as jnp
from jax import lax
from jax.experimental import pallas as pl
from jax.experimental.pallas import tpu as pltpu
from jax.sharding import PartitionSpec as P

NS_ITERS = 2
EXTRA = 16

gradient_step = 0.25
energy_step = 0.002
epsilon = 1e-06

VMEM_LIMIT = 32 * 1024 * 1024


def call(body, out_shape, in_specs, out_specs, scratch=()):
    return pl.pallas_call(
        body,
        out_shape=out_shape,
        in_specs=in_specs,
        out_specs=out_specs,
        scratch_shapes=list(scratch),
        compiler_params=pltpu.CompilerParams(vmem_limit_bytes=VMEM_LIMIT),
    )


def vmem(count):
    return [pl.BlockSpec(memory_space=pltpu.VMEM)] * count


def swap(array, axis, partner):
    size = lax.axis_size(axis)
    return lax.ppermute(array, axis, [(i, partner(i)) for i in range(size)])


def select_kernel(parent_ref, *refs):
    *row_refs, theta_ref, extra_ref = refs
    occupied = theta_ref.shape[0]
    place = jnp.bitwise_xor(parent_ref[0], lax.axis_index("wlk"))
    for index, ref in enumerate(row_refs):

        @pl.when(place == index)
        def _():
            theta_ref[...] = ref[:occupied, :]
            extra_ref[...] = ref[occupied:, :]


def gradient_kernel(norm_scale, blocks, summands, theta_ref, *refs):
    chol_refs = refs[:blocks]
    sum_refs = refs[blocks : blocks + summands]
    out_ref, adjoint = refs[blocks + summands :]
    occupied = theta_ref.shape[0]
    theta = theta_ref[...]
    rows = lax.broadcasted_iota(jnp.int32, (occupied, occupied), 0)
    columns = lax.broadcasted_iota(jnp.int32, (occupied, occupied), 1)
    diagonal = rows == columns
    total = None
    for ref in sum_refs:
        term = ref[...].astype(jnp.float32)
        total = term if total is None else total + term
    for ref in chol_refs:
        vectors, _, basis = ref.shape
        chol = ref[...].reshape(vectors * occupied, basis)
        turned = lax.dot_general(
            chol, theta, (((1,), (1,)), ((), ())), preferred_element_type=jnp.float32
        )
        turned = turned.astype(jnp.bfloat16).astype(jnp.float32)
        for g in range(vectors):
            block = turned[g * occupied : (g + 1) * occupied, :]
            on_diagonal = jnp.where(diagonal, block, 0.0)
            trace = jnp.sum(jnp.sum(on_diagonal, axis=0, keepdims=True), axis=1, keepdims=True)
            piece = norm_scale * (jnp.where(diagonal, trace, 0.0) - block)
            adjoint[:, g * occupied : (g + 1) * occupied] = piece.astype(jnp.bfloat16)
        term = jnp.dot(
            adjoint[:, : vectors * occupied], chol, preferred_element_type=jnp.float32
        )
        total = term if total is None else total + term
    out_ref[...] = total.astype(out_ref.dtype)


def partial_gradient(norm_scale, theta, chols, summands, dtype):
    occupied, basis = theta.shape
    most = max(c.shape[0] for c in chols)
    return call(
        functools.partial(gradient_kernel, norm_scale, len(chols), len(summands)),
        jax.ShapeDtypeStruct((occupied, basis), dtype),
        vmem(1 + len(chols) + len(summands)),
        pl.BlockSpec(memory_space=pltpu.VMEM),
        [pltpu.VMEM((occupied, most * occupied), jnp.bfloat16)],
    )(theta, *chols, *summands)


def final_kernel(theta_ref, extra_ref, own_ref, other_ref, propagator_ref, out_ref, log_ref):
    occupied, basis = theta_ref.shape
    theta = theta_ref[...].astype(jnp.float32)
    gradient = own_ref[...] + other_ref[...].astype(jnp.float32)
    energy = 0.5 * jnp.sum(theta * gradient)
    log_weight = jnp.sum(extra_ref[...].astype(jnp.float32))
    log_ref[0] = log_weight - energy_step * energy
    stepped = (theta - gradient_step * gradient).astype(jnp.bfloat16)
    propagated = lax.dot_general(
        stepped, propagator_ref[...], (((1,), (1,)), ((), ())), preferred_element_type=jnp.float32
    )
    mean_square = jnp.sum(propagated * propagated, keepdims=True) / (occupied * basis)
    current = propagated * lax.rsqrt(mean_square + epsilon)
    for _ in range(NS_ITERS):
        narrow = current.astype(jnp.bfloat16)
        overlap = lax.dot_general(
            narrow, narrow, (((1,), (1,)), ((), ())), preferred_element_type=jnp.float32
        )
        overlap = (overlap * (0.5 / basis)).astype(jnp.bfloat16)
        current = 1.5 * current - jnp.dot(overlap, narrow, preferred_element_type=jnp.float32)
    out_ref[...] = current


def local(cholesky, orbitals, log_weights, parents, propagator):
    walker_count, occupied, basis = orbitals.shape
    vectors_here = cholesky.shape[0]
    vec_size, wlk_size = lax.axis_size("vec"), lax.axis_size("wlk")
    norm_scale = 1.0 / math.sqrt(vectors_here * vec_size)
    half = vectors_here // 2
    core = lax.axis_index("wlk") % 2

    mine = lax.dynamic_slice_in_dim(cholesky, core * half, half, 0)
    cross = [
        lax.ppermute(mine, "vec", [(i, (i + 2 * m) % vec_size) for i in range(vec_size)])
        for m in range(1, vec_size // 2)
    ]

    theta = orbitals[0].astype(jnp.bfloat16)
    high = log_weights.astype(jnp.bfloat16)
    rest = log_weights - high.astype(jnp.float32)
    middle = rest.astype(jnp.bfloat16)
    low = (rest - middle.astype(jnp.float32)).astype(jnp.bfloat16)
    extra = jnp.concatenate([high, middle, low]).reshape(1, 3)
    extra = jnp.pad(extra, ((0, EXTRA - 1), (0, basis - 3)))
    payload = jnp.concatenate([theta, extra], axis=0)

    row = [payload] + [swap(payload, "wlk", lambda i, m=m: i ^ (2 * m)) for m in range(1, wlk_size // 2)]
    across = swap(jnp.stack(row), "wlk", lambda i: i ^ 1)
    row = [r for m in range(wlk_size // 2) for r in (row[m], across[m])]

    smem = pl.BlockSpec(memory_space=pltpu.SMEM)
    chosen, chosen_extra = call(
        select_kernel,
        (
            jax.ShapeDtypeStruct((occupied, basis), jnp.bfloat16),
            jax.ShapeDtypeStruct((EXTRA, basis), jnp.bfloat16),
        ),
        [smem] + vmem(wlk_size),
        vmem(2),
    )(parents, *row)
    neighbour = swap(chosen, "vec", lambda i: i ^ 1)

    other = [swap(c, "wlk", lambda i: i ^ 1) for c in cross]
    own_part = partial_gradient(norm_scale, chosen, [cholesky], [], jnp.float32)
    to_send = partial_gradient(norm_scale, neighbour, [cholesky, *cross], [], jnp.float32)
    to_send = partial_gradient(norm_scale, neighbour, other, [to_send], jnp.bfloat16)
    received = swap(to_send, "vec", lambda i: i ^ 1)
    own_part = partial_gradient(norm_scale, chosen, [*cross, *other], [own_part], jnp.float32)

    new_orbitals, new_logs = call(
        final_kernel,
        (
            jax.ShapeDtypeStruct((occupied, basis), jnp.float32),
            jax.ShapeDtypeStruct((1,), jnp.float32),
        ),
        vmem(5),
        [pl.BlockSpec(memory_space=pltpu.VMEM), smem],
    )(chosen, chosen_extra, own_part, received, propagator.astype(jnp.bfloat16))
    return new_orbitals.reshape(orbitals.shape), new_logs


def solution(mesh):
    placed = (
        P(("grp", "vec"), None, None),
        P(("grp", "vec", "wlk"), None, None),
        P(("grp", "vec", "wlk")),
        P(("grp", "vec", "wlk")),
        P("grp", None),
    )
    return jax.shard_map(
        local,
        mesh=mesh,
        in_specs=placed,
        out_specs=(P(("grp", "vec", "wlk"), None, None), P(("grp", "vec", "wlk"))),
        check_vma=False,
    )
```

time: 71.5 us -> 29 us (0.41)
  blocking collectives: 41.1 us -> 0 us
  between operations: 16.1 us -> 2.16 us
  waiting for transfers between devices: 0.02 us -> 13.9 us
  starting transfers between devices: 0.04 us -> 7.21 us
  matrix products: 5.77 us -> 0 us
  Pallas kernels: 0 us -> 4.52 us
  other arithmetic: 4.87 us -> 1.09 us
  local copies, waits for them, and re-layouts: 3.31 us -> 0.03 us
    all_gather x2 -> x0, blocking collectives: 22.8 us -> none  [the longest x1 15.6 us: local(): gathered = lax.all_gather(theta, 'vec', axis=0, tiled=True)]
    unnamed x2 -> x0, blocking collectives: 18.3 us -> none
    ppermute x0 -> x6, waiting for transfers between devices: none -> 13.9 us  [the longest x1 8.06 us: local(): lax.ppermute(mine, 'vec', [(i, (i + 2 * m) % vec_size) for i in range(vec...]
    ppermute x0 -> x6, starting transfers between devices: none -> 7.21 us  [the longest x5 4.56 us: swap(): return lax.ppermute(array, axis, [(i, partner(i)) for i in range(size)])]
    dot_general x8 -> x0, matrix products: 5.77 us -> none  [the longest x1 1.74 us: local(): lax.dot_general(picked, propagator, (((2,), (1,)), ((), ())), precision=l...]
    pallas_call x0 -> x6, Pallas kernels: none -> 4.52 us  [the longest x4 2.82 us: partial_gradient(): call(functools.partial(gradient_kernel, norm_scale, len(chols), len(summa...]
    unnamed x13 -> x4, local copies, waits for them, and re-layouts: 2.49 us -> 0.01 us
    unnamed x1 -> x0, other arithmetic: 1.46 us -> none
  transfers between devices with their start and end apart: 1 -> 6, of which waited for: 0 -> 3; matrix products, arithmetic and copies ran while one was open for 5% -> 0% of each run, Pallas kernels for 0% -> 8%
where the time goes in v1:
time: 29 us; the launch traced here: 28.9 us
  waiting for transfers between devices  13.9 us (48%)
  starting transfers between devices  7.21 us (25%)
  Pallas kernels  4.52 us (16%)
  between operations  2.16 us (7%)
  other arithmetic  1.09 us (4%)
    ppermute x1, waiting for transfers between devices, local(): lax.ppermute(mine, 'vec', [(i, (i + 2 * m) % vec_size) for i in range(vec...  8.06 us
    ppermute x5, waiting for transfers between devices, swap(): return lax.ppermute(array, axis, [(i, partner(i)) for i in range(size)])  5.8 us
    ppermute x5, starting transfers between devices, swap(): return lax.ppermute(array, axis, [(i, partner(i)) for i in range(size)])  4.56 us
    pallas_call x4, Pallas kernels, partial_gradient(): call(functools.partial(gradient_kernel, norm_scale, len(chols), len(summa...  2.82 us
    ppermute x1, starting transfers between devices, local(): lax.ppermute(mine, 'vec', [(i, (i + 2 * m) % vec_size) for i in range(vec...  2.65 us
    pallas_call x1, Pallas kernels, local(): call(final_kernel, (jax.ShapeDtypeStruct((occupied, basis), jnp.float32),...  1.67 us
    convert_element_type x1, other arithmetic, local(): theta = orbitals[0].astype(jnp.bfloat16)  0.92 us
  transfers between devices with their start and end apart: 6, of which 3 were waited for; matrix products, arithmetic and copies ran while one was open for 0% of the time, Pallas kernels for 8%

profile of v1, /device:TPU:0, one launch (start us, length us, event | category | flops | bytes accessed | tf_op | source)
XLA Modules:
  0.0 28.9 jit_solution(14877678891454159308)
XLA Ops:
  0.6 0.0 copy-start
  1.4 0.1 maximum_bitcast_fusion
  1.4 0.9 %convert_bitcast_fusion = bf16[64,512]{1,0:T(8,128)(2,1)S(1)} fusion(f32[1,64,512]{2,1,0:T(8,128)} %param.6), kind=kLoop, calls=%fused_computation.6 | loop fusion | flops 32768 | bytes 196608 | tf_op jit(solution)/shard_map/convert_element_type | solution.py:135
  2.4 3.0 %collective-permute-start = (bf16[80,512]{1,0:T(8,128)(2,1)S(1)}, bf16[80,512]{1,0:T(8,128)(2,1)S(1)}, u32[]{:S(2)}, u32[]{:S(2)}) collective-permute-start(bf16[80,512]{1,0:T(8,128)(2,1)S(1)} %get-tuple-element.13.refs_0_), channel_id=1, source_target_pairs={{0,2},{1,3},{2,0},{3,1},{4,6},{5,7},{6,4},{7,5},{8,10},{9,11},{10,... | collective-permute-start | bytes 245768 | tf_op jit(solution)/shard_map/ppermute | solution.py:38
  5.4 0.0 copy-done
  5.4 2.7 %collective-permute-start.2 = (bf16[3,64,512]{2,1,0:T(8,128)(2,1)S(1)}, bf16[3,64,512]{2,1,0:T(8,128)(2,1)S(1)}, u32[]{:S(2)}, u32[]{:S(2)}) collective-permute-start(bf16[3,64,512]{2,1,0:T(8,128)(2,1)S(1)} %constant_dynamic-slice_fusion), channel_id=1, source_target_pairs={{0,8},{4,12},{8,0},{12,4},{1,9},{5,13},{9,1},{13,5},{2,10},{6,14},... | collective-permute-start | bytes 589832 | tf_op jit(solution)/shard_map/ppermute | solution.py:131
  8.1 0.0 collective-permute-done.refs_2_
  8.1 0.0 copy-start.1
  8.1 0.1 collective-permute-start.1
  8.9 8.1 %collective-permute-done.2.refs_0_.refs_1_ = bf16[3,64,512]{2,1,0:T(8,128)(2,1)S(1)} collective-permute-done((bf16[3,64,512]{2,1,0:T(8,128)(2,1)S(1)}, bf16[3,64,512]{2,1,0:T(8,128)(2,1)S(1)}, u32[]{:S(2)}, u32[]{:S(2)}) %collective-permute-start.2) | collective-permute-done | bytes 196640 | tf_op jit(solution)/shard_map/ppermute | solution.py:131
  16.9 0.0 collective-permute-start.3
  16.9 0.0 collective-permute-done.1
  17.0 0.8 %collective-permute-start.4 = (bf16[64,512]{1,0:T(8,128)(2,1)S(1)}, bf16[64,512]{1,0:T(8,128)(2,1)S(1)}, u32[]{:S(2)}, u32[]{:S(2)}) collective-permute-start(bf16[64,512]{1,0:T(8,128)(2,1)S(1)} %get-tuple-element.6.theta_ref), channel_id=1, source_target_pairs={{0,4},{4,0},{8,12},{12,8},{1,5},{5,1},{9,13},{13,9},{2,6},{6,2},{1... | collective-permute-start | bytes 196616 | tf_op jit(solution)/shard_map/ppermute | solution.py:38
  17.8 3.8 %collective-permute-done.4.theta_ref = bf16[64,512]{1,0:T(8,128)(2,1)S(1)} collective-permute-done((bf16[64,512]{1,0:T(8,128)(2,1)S(1)}, bf16[64,512]{1,0:T(8,128)(2,1)S(1)}, u32[]{:S(2)}, u32[]{:S(2)}) %collective-permute-start.4) | collective-permute-done | bytes 65568 | tf_op jit(solution)/shard_map/ppermute | solution.py:38
  21.6 0.8 %shard_map.71.refs_1_ = f32[64,512]{1,0:T(8,128)S(1)} custom-call(bf16[64,512]{1,0:T(8,128)(2,1)S(1)} %collective-permute-done.4.theta_ref, bf16[6,64,512]{2,1,0:T(8,128)(2,1)S(1)} %copy-done, bf16[3,64,512]{2,1,0:T(8,128)(2,1)S(1)} %collective-permute-done.2.refs_0_.refs_1_), custom_call_target="tpu_custom_call" | custom-call | tf_op jit(solution)/shard_map/pallas_call | solution.py:89
  22.3 0.0 collective-permute-done.3.refs_1_.refs_0_
  22.4 0.5 %shard_map.72 = bf16[64,512]{1,0:T(8,128)(2,1)S(1)} custom-call(bf16[64,512]{1,0:T(8,128)(2,1)S(1)} %collective-permute-done.4.theta_ref, bf16[3,64,512]{2,1,0:T(8,128)(2,1)S(1)} %collective-permute-done.3.refs_1_.refs_0_, f32[64,512]{1,0:T(8,128)S(1)} %shard_map.71.refs_1_), custom_call_target="tpu_custom_call" | custom-call | tf_op jit(solution)/shard_map/pallas_call | solution.py:89
  22.9 0.7 %collective-permute-start.5 = (bf16[64,512]{1,0:T(8,128)(2,1)S(1)}, bf16[64,512]{1,0:T(8,128)(2,1)S(1)}, u32[]{:S(2)}, u32[]{:S(2)}) collective-permute-start(bf16[64,512]{1,0:T(8,128)(2,1)S(1)} %shard_map.72), channel_id=1, source_target_pairs={{0,4},{4,0},{8,12},{12,8},{1,5},{5,1},{9,13},{13,9},{2,6},{6,2},{1... | collective-permute-start | bytes 196616 | tf_op jit(solution)/shard_map/ppermute | solution.py:38
  23.6 0.0 copy-done.1
  23.6 0.1 convert_element_type.33.propagator_ref
  23.7 0.6 %shard_map.69.refs_2_ = f32[64,512]{1,0:T(8,128)S(1)} custom-call(bf16[64,512]{1,0:T(8,128)(2,1)S(1)} %get-tuple-element.6.theta_ref, bf16[6,64,512]{2,1,0:T(8,128)(2,1)S(1)} %copy-done), custom_call_target="tpu_custom_call" | custom-call | tf_op jit(solution)/shard_map/pallas_call | solution.py:89
  24.3 0.9 %shard_map.70.own_ref = f32[64,512]{1,0:T(8,128)S(1)} custom-call(bf16[64,512]{1,0:T(8,128)(2,1)S(1)} %get-tuple-element.6.theta_ref, bf16[3,64,512]{2,1,0:T(8,128)(2,1)S(1)} %collective-permute-done.2.refs_0_.refs_1_, bf16[3,64,512]{2,1,0:T(8,128)(2,1)S(1)} %collective-permute-done.3.refs_1_.refs_0_, f32[64,512]{1,0:T(8,128)S(1)} %shard_map.69.refs_2_), custom_call_target="tpu_custom_call" | custom-call | tf_op jit(solution)/shard_map/pallas_call | solution.py:89
  25.2 2.0 %collective-permute-done.5.other_ref = bf16[64,512]{1,0:T(8,128)(2,1)S(1)} collective-permute-done((bf16[64,512]{1,0:T(8,128)(2,1)S(1)}, bf16[64,512]{1,0:T(8,128)(2,1)S(1)}, u32[]{:S(2)}, u32[]{:S(2)}) %collective-permute-start.5) | collective-permute-done | bytes 65568 | tf_op jit(solution)/shard_map/ppermute | solution.py:38
  27.2 1.7 %shard_map.73 = (f32[64,512]{1,0:T(8,128)}, f32[1]{0:T(128)}) custom-call(bf16[64,512]{1,0:T(8,128)(2,1)S(1)} %get-tuple-element.6.theta_ref, bf16[16,512]{1,0:T(8,128)(2,1)S(1)} %get-tuple-element.7.extra_ref, f32[64,512]{1,0:T(8,128)S(1)} %shard_map.70.own_ref, bf16[64,512]{1,0:T(8,128)(2,1)S(1)} %collective-permute-done.5.other_ref, ...), custom_call_target="tpu_custom_call" | custom-call | tf_op jit(solution)/shard_map/pallas_call | solution.py:167
  (5 shorter events, 0.1 us)
Async XLA Ops:
  0.6 4.8 %copy-start = (bf16[6,64,512]{2,1,0:T(8,128)(2,1)S(1)}, bf16[6,64,512]{2,1,0:T(8,128)(2,1)}, u32[]{:S(2)}) copy-start(bf16[6,64,512]{2,1,0:T(8,128)(2,1)} %refs_0_.3) | copy-start | bytes 1179652
  2.4 5.7 %collective-permute-start = (bf16[80,512]{1,0:T(8,128)(2,1)S(1)}, bf16[80,512]{1,0:T(8,128)(2,1)S(1)}, u32[]{:S(2)}, u32[]{:S(2)}) collective-permute-start(bf16[80,512]{1,0:T(8,128)(2,1)S(1)} %get-tuple-element.13.refs_0_), channel_id=1, source_target_pairs={{0,2},{1,3},{2,0},{3,1},{4,6},{5,7},{6,4},{7,5},{8,10},{9,11},{10,... | collective-permute-start | bytes 245768 | tf_op jit(solution)/shard_map/ppermute | solution.py:38
  5.4 11.5 %collective-permute-start.2 = (bf16[3,64,512]{2,1,0:T(8,128)(2,1)S(1)}, bf16[3,64,512]{2,1,0:T(8,128)(2,1)S(1)}, u32[]{:S(2)}, u32[]{:S(2)}) collective-permute-start(bf16[3,64,512]{2,1,0:T(8,128)(2,1)S(1)} %constant_dynamic-slice_fusion), channel_id=1, source_target_pairs={{0,8},{4,12},{8,0},{12,4},{1,9},{5,13},{9,1},{13,5},{2,10},{6,14},... | collective-permute-start | bytes 589832 | tf_op jit(solution)/shard_map/ppermute | solution.py:131
  8.1 15.6 %copy-start.1 = (f32[512,512]{1,0:T(8,128)S(1)}, f32[512,512]{1,0:T(8,128)}, u32[]{:S(2)}) copy-start(f32[512,512]{1,0:T(8,128)} %param.9) | copy-start | bytes 3145732
  8.1 8.9 %collective-permute-start.1 = (bf16[2,80,512]{2,1,0:T(8,128)(2,1)S(1)}, bf16[2,80,512]{2,1,0:T(8,128)(2,1)S(1)}, u32[]{:S(2)}, u32[]{:S(2)}) collective-permute-start(bf16[2,80,512]{2,1,0:T(8,128)(2,1)S(1)} %pad_maximum_fusion), channel_id=1, source_target_pairs={{0,1},{1,0},{2,3},{3,2},{4,5},{5,4},{6,7},{7,6},{8,9},{9,8},{10,11... | collective-permute-start | bytes 491528 | tf_op jit(solution)/shard_map/ppermute | solution.py:38
  16.9 5.4 %collective-permute-start.3 = (bf16[3,64,512]{2,1,0:T(8,128)(2,1)S(1)}, bf16[3,64,512]{2,1,0:T(8,128)(2,1)S(1)}, u32[]{:S(2)}, u32[]{:S(2)}) collective-permute-start(bf16[3,64,512]{2,1,0:T(8,128)(2,1)S(1)} %collective-permute-done.2.refs_0_.refs_1_), channel_id=1, source_target_pairs={{0,1},{1,0},{2,3},{3,2},{4,5},{5,4},{6,7},{7,6},{8,9},{9,8},{10,11... | collective-permute-start | bytes 589832 | tf_op jit(solution)/shard_map/ppermute | solution.py:38
  17.0 4.6 %collective-permute-start.4 = (bf16[64,512]{1,0:T(8,128)(2,1)S(1)}, bf16[64,512]{1,0:T(8,128)(2,1)S(1)}, u32[]{:S(2)}, u32[]{:S(2)}) collective-permute-start(bf16[64,512]{1,0:T(8,128)(2,1)S(1)} %get-tuple-element.6.theta_ref), channel_id=1, source_target_pairs={{0,4},{4,0},{8,12},{12,8},{1,5},{5,1},{9,13},{13,9},{2,6},{6,2},{1... | collective-permute-start | bytes 196616 | tf_op jit(solution)/shard_map/ppermute | solution.py:38
  22.9 4.3 %collective-permute-start.5 = (bf16[64,512]{1,0:T(8,128)(2,1)S(1)}, bf16[64,512]{1,0:T(8,128)(2,1)S(1)}, u32[]{:S(2)}, u32[]{:S(2)}) collective-permute-start(bf16[64,512]{1,0:T(8,128)(2,1)S(1)} %shard_map.72), channel_id=1, source_target_pairs={{0,4},{4,0},{8,12},{12,8},{1,5},{5,1},{9,13},{13,9},{2,6},{6,2},{1... | collective-permute-start | bytes 196616 | tf_op jit(solution)/shard_map/ppermute | solution.py:38

commit v2 on v1

--- a/solution.py
+++ b/solution.py
@@ -38,16 +38,32 @@
     return lax.ppermute(array, axis, [(i, partner(i)) for i in range(size)])
 
 
-def select_kernel(parent_ref, *refs):
+def payload_kernel(log_ref, parent_ref, orbitals_ref, payload_ref, place_ref):
+    occupied, basis = orbitals_ref.shape[1:]
+    parent = jnp.broadcast_to(parent_ref[...].reshape(1, 1), place_ref.shape)
+    place_ref[...] = parent
+    value = jnp.broadcast_to(log_ref[...].reshape(1, 1), (EXTRA, basis))
+    high = value.astype(jnp.bfloat16).astype(jnp.float32)
+    middle = (value - high).astype(jnp.bfloat16).astype(jnp.float32)
+    low = value - high - middle
+    rows = lax.broadcasted_iota(jnp.int32, (EXTRA, basis), 0)
+    lanes = lax.broadcasted_iota(jnp.int32, (EXTRA, basis), 1)
+    pieces = jnp.where(rows == 0, high, jnp.where(rows == 1, middle, jnp.where(rows == 2, low, 0.0)))
+    payload_ref[occupied:, :] = jnp.where(lanes == 0, pieces, 0.0).astype(jnp.bfloat16)
+    payload_ref[:occupied, :] = orbitals_ref[0].astype(jnp.bfloat16)
+
+
+def select_kernel(place_ref, *refs):
     *row_refs, theta_ref, extra_ref = refs
-    occupied = theta_ref.shape[0]
-    place = jnp.bitwise_xor(parent_ref[0], lax.axis_index("wlk"))
-    for index, ref in enumerate(row_refs):
-
-        @pl.when(place == index)
-        def _():
-            theta_ref[...] = ref[:occupied, :]
-            extra_ref[...] = ref[occupied:, :]
+    occupied, basis = theta_ref.shape
+    whole = (occupied + EXTRA, basis)
+    place = jnp.broadcast_to(place_ref[:1, :1], whole)
+    picked = row_refs[0][...].astype(jnp.float32)
+    for index, ref in enumerate(row_refs[1:]):
+        picked = jnp.where(place == index + 1, ref[...].astype(jnp.float32), picked)
+    picked = picked.astype(jnp.bfloat16)
+    theta_ref[...] = picked[:occupied]
+    extra_ref[...] = picked[occupied:]
 
 
 def gradient_kernel(norm_scale, blocks, summands, theta_ref, *refs):
@@ -124,39 +140,42 @@
     vec_size, wlk_size = lax.axis_size("vec"), lax.axis_size("wlk")
     norm_scale = 1.0 / math.sqrt(vectors_here * vec_size)
     half = vectors_here // 2
-    core = lax.axis_index("wlk") % 2
-
-    mine = lax.dynamic_slice_in_dim(cholesky, core * half, half, 0)
+    smem = pl.BlockSpec(memory_space=pltpu.SMEM)
+
+    here = lax.axis_index("wlk")
+    mine = lax.dynamic_slice_in_dim(cholesky, here % 2 * half, half, 0)
+
     cross = [
         lax.ppermute(mine, "vec", [(i, (i + 2 * m) % vec_size) for i in range(vec_size)])
         for m in range(1, vec_size // 2)
     ]
 
-    theta = orbitals[0].astype(jnp.bfloat16)
-    high = log_weights.astype(jnp.bfloat16)
-    rest = log_weights - high.astype(jnp.float32)
-    middle = rest.astype(jnp.bfloat16)
-    low = (rest - middle.astype(jnp.float32)).astype(jnp.bfloat16)
-    extra = jnp.concatenate([high, middle, low]).reshape(1, 3)
-    extra = jnp.pad(extra, ((0, EXTRA - 1), (0, basis - 3)))
-    payload = jnp.concatenate([theta, extra], axis=0)
-
-    row = [payload] + [swap(payload, "wlk", lambda i, m=m: i ^ (2 * m)) for m in range(1, wlk_size // 2)]
-    across = swap(jnp.stack(row), "wlk", lambda i: i ^ 1)
-    row = [r for m in range(wlk_size // 2) for r in (row[m], across[m])]
-
-    smem = pl.BlockSpec(memory_space=pltpu.SMEM)
-    chosen, chosen_extra = call(
-        select_kernel,
-        (
-            jax.ShapeDtypeStruct((occupied, basis), jnp.bfloat16),
-            jax.ShapeDtypeStruct((EXTRA, basis), jnp.bfloat16),
-        ),
-        [smem] + vmem(wlk_size),
-        vmem(2),
-    )(parents, *row)
-    neighbour = swap(chosen, "vec", lambda i: i ^ 1)
-
+
+    def walkers(orbitals, log_weights, parents):
+        payload, place = call(
+            payload_kernel,
+            (
+                jax.ShapeDtypeStruct((occupied + EXTRA, basis), jnp.bfloat16),
+                jax.ShapeDtypeStruct((8, 128), jnp.int32),
+            ),
+            vmem(3),
+            vmem(2),
+        )(log_weights, parents, orbitals)
+        gathered = lax.all_gather(payload, "wlk", axis=0)
+        row = [gathered[m] for m in range(wlk_size)]
+        chosen, chosen_extra = call(
+            select_kernel,
+            (
+                jax.ShapeDtypeStruct((occupied, basis), jnp.bfloat16),
+                jax.ShapeDtypeStruct((EXTRA, basis), jnp.bfloat16),
+            ),
+            vmem(1 + wlk_size),
+            vmem(2),
+        )(place, *row)
+        return chosen, chosen_extra, swap(chosen, "vec", lambda i: i ^ 1)
+
+    chosen, chosen_extra, neighbour = walkers(orbitals, log_weights, parents)
+    *cross, neighbour = lax.optimization_barrier((*cross, neighbour))
     other = [swap(c, "wlk", lambda i: i ^ 1) for c in cross]
     own_part = partial_gradient(norm_scale, chosen, [cholesky], [], jnp.float32)
     to_send = partial_gradient(norm_scale, neighbour, [cholesky, *cross], [], jnp.float32)

time: 29 us -> 25.9 us (0.89)
  waiting for transfers between devices: 13.9 us -> 4.49 us
  blocking collectives: 0 us -> 6.09 us
  other arithmetic: 1.09 us -> 0.07 us
  local copies, waits for them, and re-layouts: 0.03 us -> 1.02 us
    ppermute x1, waiting for transfers between devices: 8.06 us -> 0.01 us  [local(): lax.ppermute(mine, 'vec', [(i, (i + 2 * m) % vec_size) for i in range(vec...]
    all_gather x0 -> x1, blocking collectives: none -> 6.09 us  [walkers(): gathered = lax.all_gather(payload, 'wlk', axis=0)]
    ppermute x1, starting transfers between devices: 2.65 us -> 4.1 us  [local(): lax.ppermute(mine, 'vec', [(i, (i + 2 * m) % vec_size) for i in range(vec...]
    ppermute x5 -> x3, waiting for transfers between devices: 5.8 us -> 4.49 us  [swap(): return lax.ppermute(array, axis, [(i, partner(i)) for i in range(size)])]
    ppermute x5 -> x3, starting transfers between devices: 4.56 us -> 3.29 us  [swap(): return lax.ppermute(array, axis, [(i, partner(i)) for i in range(size)])]
    dynamic_slice x1, local copies, waits for them, and re-layouts: 0.01 us -> 0.98 us  [local(): mine = lax.dynamic_slice_in_dim(cholesky, here % 2 * half, half, 0)]
    convert_element_type x1 -> x0, other arithmetic: 0.92 us -> none  [local(): theta = orbitals[0].astype(jnp.bfloat16)]
  transfers between devices with their start and end apart: 6 -> 4, of which waited for: 3 -> 3; matrix products, arithmetic and copies ran while one was open for 0% -> 0% of each run, Pallas kernels for 8% -> 10%
where the time goes in v2:
time: 25.9 us; the launch traced here: 25.7 us
  starting transfers between devices  7.39 us (29%)
  blocking collectives  6.09 us (24%)
  Pallas kernels  4.65 us (18%)
  waiting for transfers between devices  4.49 us (17%)
  between operations  2.03 us (8%)
  local copies, waits for them, and re-layouts  1.02 us (4%)
    all_gather x1, blocking collectives, walkers(): gathered = lax.all_gather(payload, 'wlk', axis=0)  6.09 us
    ppermute x3, waiting for transfers between devices, swap(): return lax.ppermute(array, axis, [(i, partner(i)) for i in range(size)])  4.49 us
    ppermute x1, starting transfers between devices, local(): lax.ppermute(mine, 'vec', [(i, (i + 2 * m) % vec_size) for i in range(vec...  4.1 us
    ppermute x3, starting transfers between devices, swap(): return lax.ppermute(array, axis, [(i, partner(i)) for i in range(size)])  3.29 us
    pallas_call x4, Pallas kernels, partial_gradient(): call(functools.partial(gradient_kernel, norm_scale, len(chols), len(summa...  2.81 us
    pallas_call x1, Pallas kernels, local(): call(final_kernel, (jax.ShapeDtypeStruct((occupied, basis), jnp.float32),...  1.67 us
    dynamic_slice x1, local copies, waits for them, and re-layouts, local(): mine = lax.dynamic_slice_in_dim(cholesky, here % 2 * half, half, 0)  0.98 us
  transfers between devices with their start and end apart: 4, of which 3 were waited for; matrix products, arithmetic and copies ran while one was open for 0% of the time, Pallas kernels for 10%

profile of v2, /device:TPU:0, one launch (start us, length us, event | category | flops | bytes accessed | tf_op | source)
XLA Modules:
  0.0 25.7 jit_solution(2412647764948042257)
XLA Ops:
  0.6 0.0 copy-start.1
  0.7 1.0 %constant_dynamic-slice_fusion = bf16[3,64,512]{2,1,0:T(8,128)(2,1)S(1)} fusion(bf16[6,64,512]{2,1,0:T(8,128)(2,1)} %refs_0_.3, s32[]{:T(128)S(6)} %select_n.11), kind=kLoop, calls=%fused_computation | loop fusion | bytes 393220 | tf_op jit(solution)/shard_map/dynamic_slice | solution.py:146
  1.6 4.1 %collective-permute-start = (bf16[3,64,512]{2,1,0:T(8,128)(2,1)S(1)}, bf16[3,64,512]{2,1,0:T(8,128)(2,1)S(1)}, u32[]{:S(2)}, u32[]{:S(2)}) collective-permute-start(bf16[3,64,512]{2,1,0:T(8,128)(2,1)S(1)} %constant_dynamic-slice_fusion), channel_id=1, source_target_pairs={{0,8},{4,12},{8,0},{12,4},{1,9},{5,13},{9,1},{13,5},{2,10},{6,14},... | collective-permute-start | bytes 589832 | tf_op jit(solution)/shard_map/ppermute | solution.py:149
  7.0 0.0 copy-done.1
  7.0 0.1 shard_map.68
  7.1 6.1 %all-gather = bf16[320,512]{1,0:T(8,128)(2,1)S(1)} all-gather(bf16[80,512]{1,0:T(8,128)(2,1)S(1)} %get-tuple-element.11), channel_id=2, replica_groups=mesh['grp'=2,'vec'=4,'wlk'=4] {'wlk'}, dimensions={0}, use_global_device_ids=true | all-gather | bytes 409600 | tf_op jit(solution)/shard_map/all_gather | solution.py:164
  13.2 0.0 copy-start
  13.2 0.0 copy-start.2
  13.3 0.1 shard_map.69
  13.3 1.6 %collective-permute-start.1 = (bf16[64,512]{1,0:T(8,128)(2,1)S(1)}, bf16[64,512]{1,0:T(8,128)(2,1)S(1)}, u32[]{:S(2)}, u32[]{:S(2)}) collective-permute-start(bf16[64,512]{1,0:T(8,128)(2,1)S(1)} %get-tuple-element.12.theta_ref), channel_id=1, source_target_pairs={{0,4},{4,0},{8,12},{12,8},{1,5},{5,1},{9,13},{13,9},{2,6},{6,2},{1... | collective-permute-start | bytes 196616 | tf_op jit(solution)/shard_map/ppermute | solution.py:38
  15.0 2.8 %collective-permute-done.1.theta_ref = bf16[64,512]{1,0:T(8,128)(2,1)S(1)} collective-permute-done((bf16[64,512]{1,0:T(8,128)(2,1)S(1)}, bf16[64,512]{1,0:T(8,128)(2,1)S(1)}, u32[]{:S(2)}, u32[]{:S(2)}) %collective-permute-start.1) | collective-permute-done | bytes 65568 | tf_op jit(solution)/shard_map/ppermute | solution.py:38
  17.8 0.0 collective-permute-done.refs_0_.refs_1_
  17.8 0.0 collective-permute-start.2
  17.8 0.0 copy-done
  17.8 0.8 %shard_map.72.refs_1_ = f32[64,512]{1,0:T(8,128)S(1)} custom-call(bf16[64,512]{1,0:T(8,128)(2,1)S(1)} %collective-permute-done.1.theta_ref, bf16[6,64,512]{2,1,0:T(8,128)(2,1)S(1)} %copy-done, bf16[3,64,512]{2,1,0:T(8,128)(2,1)S(1)} %collective-permute-done.refs_0_.refs_1_), custom_call_target="tpu_custom_call" | custom-call | tf_op jit(solution)/shard_map/pallas_call | solution.py:105
  18.5 0.7 %collective-permute-done.2.refs_1_.refs_0_ = bf16[3,64,512]{2,1,0:T(8,128)(2,1)S(1)} collective-permute-done((bf16[3,64,512]{2,1,0:T(8,128)(2,1)S(1)}, bf16[3,64,512]{2,1,0:T(8,128)(2,1)S(1)}, u32[]{:S(2)}, u32[]{:S(2)}) %collective-permute-start.2) | collective-permute-done | bytes 196640 | tf_op jit(solution)/shard_map/ppermute | solution.py:38
  19.2 0.5 %shard_map.73 = bf16[64,512]{1,0:T(8,128)(2,1)S(1)} custom-call(bf16[64,512]{1,0:T(8,128)(2,1)S(1)} %collective-permute-done.1.theta_ref, bf16[3,64,512]{2,1,0:T(8,128)(2,1)S(1)} %collective-permute-done.2.refs_1_.refs_0_, f32[64,512]{1,0:T(8,128)S(1)} %shard_map.72.refs_1_), custom_call_target="tpu_custom_call" | custom-call | tf_op jit(solution)/shard_map/pallas_call | solution.py:105
  19.7 1.6 %collective-permute-start.3 = (bf16[64,512]{1,0:T(8,128)(2,1)S(1)}, bf16[64,512]{1,0:T(8,128)(2,1)S(1)}, u32[]{:S(2)}, u32[]{:S(2)}) collective-permute-start(bf16[64,512]{1,0:T(8,128)(2,1)S(1)} %shard_map.73), channel_id=1, source_target_pairs={{0,4},{4,0},{8,12},{12,8},{1,5},{5,1},{9,13},{13,9},{2,6},{6,2},{1... | collective-permute-start | bytes 196616 | tf_op jit(solution)/shard_map/ppermute | solution.py:38
  21.4 0.6 %shard_map.70.refs_2_ = f32[64,512]{1,0:T(8,128)S(1)} custom-call(bf16[64,512]{1,0:T(8,128)(2,1)S(1)} %get-tuple-element.12.theta_ref, bf16[6,64,512]{2,1,0:T(8,128)(2,1)S(1)} %copy-done), custom_call_target="tpu_custom_call" | custom-call | tf_op jit(solution)/shard_map/pallas_call | solution.py:105
  22.0 0.0 copy-done.2
  22.0 0.1 convert_element_type.3.propagator_ref
  22.1 0.9 %shard_map.71.own_ref = f32[64,512]{1,0:T(8,128)S(1)} custom-call(bf16[64,512]{1,0:T(8,128)(2,1)S(1)} %get-tuple-element.12.theta_ref, bf16[3,64,512]{2,1,0:T(8,128)(2,1)S(1)} %collective-permute-done.refs_0_.refs_1_, bf16[3,64,512]{2,1,0:T(8,128)(2,1)S(1)} %collective-permute-done.2.refs_1_.refs_0_, f32[64,512]{1,0:T(8,128)S(1)} %shard_map.70.refs_2_), custom_call_target="tpu_custom_call" | custom-call | tf_op jit(solution)/shard_map/pallas_call | solution.py:105
  23.0 1.1 %collective-permute-done.3.other_ref = bf16[64,512]{1,0:T(8,128)(2,1)S(1)} collective-permute-done((bf16[64,512]{1,0:T(8,128)(2,1)S(1)}, bf16[64,512]{1,0:T(8,128)(2,1)S(1)}, u32[]{:S(2)}, u32[]{:S(2)}) %collective-permute-start.3) | collective-permute-done | bytes 65568 | tf_op jit(solution)/shard_map/ppermute | solution.py:38
  24.1 1.7 %shard_map.74 = (f32[64,512]{1,0:T(8,128)}, f32[1]{0:T(128)}) custom-call(bf16[64,512]{1,0:T(8,128)(2,1)S(1)} %get-tuple-element.12.theta_ref, bf16[16,512]{1,0:T(8,128)(2,1)S(1)} %get-tuple-element.13.extra_ref, f32[64,512]{1,0:T(8,128)S(1)} %shard_map.71.own_ref, bf16[64,512]{1,0:T(8,128)(2,1)S(1)} %collective-permute-done.3.other_ref, ...), custom_call_target="tpu_custom_call" | custom-call | tf_op jit(solution)/shard_map/pallas_call | solution.py:186
  (1 shorter events, 0.0 us)
Async XLA Ops:
  0.6 6.4 %copy-start.1 = (f32[1,64,512]{2,1,0:T(8,128)S(1)}, f32[1,64,512]{2,1,0:T(8,128)}, u32[]{:S(2)}) copy-start(f32[1,64,512]{2,1,0:T(8,128)} %orbitals_ref.1) | copy-start | bytes 393220
  1.6 16.1 %collective-permute-start = (bf16[3,64,512]{2,1,0:T(8,128)(2,1)S(1)}, bf16[3,64,512]{2,1,0:T(8,128)(2,1)S(1)}, u32[]{:S(2)}, u32[]{:S(2)}) collective-permute-start(bf16[3,64,512]{2,1,0:T(8,128)(2,1)S(1)} %constant_dynamic-slice_fusion), channel_id=1, source_target_pairs={{0,8},{4,12},{8,0},{12,4},{1,9},{5,13},{9,1},{13,5},{2,10},{6,14},... | collective-permute-start | bytes 589832 | tf_op jit(solution)/shard_map/ppermute | solution.py:149
  13.2 4.5 %copy-start = (bf16[6,64,512]{2,1,0:T(8,128)(2,1)S(1)}, bf16[6,64,512]{2,1,0:T(8,128)(2,1)}, u32[]{:S(2)}) copy-start(bf16[6,64,512]{2,1,0:T(8,128)(2,1)} %refs_0_.3) | copy-start | bytes 1179652
  13.2 8.8 %copy-start.2 = (f32[512,512]{1,0:T(8,128)S(1)}, f32[512,512]{1,0:T(8,128)}, u32[]{:S(2)}) copy-start(f32[512,512]{1,0:T(8,128)} %param.9) | copy-start | bytes 3145732
  13.3 4.4 %collective-permute-start.1 = (bf16[64,512]{1,0:T(8,128)(2,1)S(1)}, bf16[64,512]{1,0:T(8,128)(2,1)S(1)}, u32[]{:S(2)}, u32[]{:S(2)}) collective-permute-start(bf16[64,512]{1,0:T(8,128)(2,1)S(1)} %get-tuple-element.12.theta_ref), channel_id=1, source_target_pairs={{0,4},{4,0},{8,12},{12,8},{1,5},{5,1},{9,13},{13,9},{2,6},{6,2},{1... | collective-permute-start | bytes 196616 | tf_op jit(solution)/shard_map/ppermute | solution.py:38
  17.8 1.4 %collective-permute-start.2 = (bf16[3,64,512]{2,1,0:T(8,128)(2,1)S(1)}, bf16[3,64,512]{2,1,0:T(8,128)(2,1)S(1)}, u32[]{:S(2)}, u32[]{:S(2)}) collective-permute-start(bf16[3,64,512]{2,1,0:T(8,128)(2,1)S(1)} %collective-permute-done.refs_0_.refs_1_), channel_id=1, source_target_pairs={{0,1},{1,0},{2,3},{3,2},{4,5},{5,4},{6,7},{7,6},{8,9},{9,8},{10,11... | collective-permute-start | bytes 589832 | tf_op jit(solution)/shard_map/ppermute | solution.py:38
  19.7 4.3 %collective-permute-start.3 = (bf16[64,512]{1,0:T(8,128)(2,1)S(1)}, bf16[64,512]{1,0:T(8,128)(2,1)S(1)}, u32[]{:S(2)}, u32[]{:S(2)}) collective-permute-start(bf16[64,512]{1,0:T(8,128)(2,1)S(1)} %shard_map.73), channel_id=1, source_target_pairs={{0,4},{4,0},{8,12},{12,8},{1,5},{5,1},{9,13},{13,9},{2,6},{6,2},{1... | collective-permute-start | bytes 196616 | tf_op jit(solution)/shard_map/ppermute | solution.py:38

commit v3 on v2

--- a/solution.py
+++ b/solution.py
@@ -18,13 +18,14 @@
 VMEM_LIMIT = 32 * 1024 * 1024
 
 
-def call(body, out_shape, in_specs, out_specs, scratch=()):
+def call(body, out_shape, in_specs, out_specs, scratch=(), cost=None):
     return pl.pallas_call(
         body,
         out_shape=out_shape,
         in_specs=in_specs,
         out_specs=out_specs,
         scratch_shapes=list(scratch),
+        cost_estimate=cost,
         compiler_params=pltpu.CompilerParams(vmem_limit_bytes=VMEM_LIMIT),
     )
 
@@ -38,26 +39,38 @@
     return lax.ppermute(array, axis, [(i, partner(i)) for i in range(size)])
 
 
-def payload_kernel(log_ref, parent_ref, orbitals_ref, payload_ref, place_ref):
-    occupied, basis = orbitals_ref.shape[1:]
-    parent = jnp.broadcast_to(parent_ref[...].reshape(1, 1), place_ref.shape)
-    place_ref[...] = parent
-    value = jnp.broadcast_to(log_ref[...].reshape(1, 1), (EXTRA, basis))
+def blank_kernel(out_ref):
+    out_ref[...] = jnp.zeros(out_ref.shape, out_ref.dtype)
+
+
+def tile_kernel(log_ref, parent_ref, blank_ref, out_ref):
+    rows = lax.broadcasted_iota(jnp.int32, out_ref.shape, 0)
+    out_ref[...] = jnp.where(rows == 0, log_ref[0], parent_ref[0].astype(jnp.float32))
+
+
+def half_kernel(tile_ref, chol_ref, out_ref):
+    half = out_ref.shape[0]
+    out_ref[...] = chol_ref[pl.ds(lax.rem(lax.axis_index("wlk"), 2) * half, half)]
+
+
+def payload_kernel(tile_ref, orbitals_ref, payload_ref):
+    occupied = orbitals_ref.shape[1]
+    payload_ref[:occupied, :] = orbitals_ref[0].astype(jnp.bfloat16)
+    value = jnp.broadcast_to(tile_ref[0:1, :], payload_ref[occupied:, :].shape)
     high = value.astype(jnp.bfloat16).astype(jnp.float32)
     middle = (value - high).astype(jnp.bfloat16).astype(jnp.float32)
     low = value - high - middle
-    rows = lax.broadcasted_iota(jnp.int32, (EXTRA, basis), 0)
-    lanes = lax.broadcasted_iota(jnp.int32, (EXTRA, basis), 1)
+    rows = lax.broadcasted_iota(jnp.int32, value.shape, 0)
+    lanes = lax.broadcasted_iota(jnp.int32, value.shape, 1)
     pieces = jnp.where(rows == 0, high, jnp.where(rows == 1, middle, jnp.where(rows == 2, low, 0.0)))
     payload_ref[occupied:, :] = jnp.where(lanes == 0, pieces, 0.0).astype(jnp.bfloat16)
-    payload_ref[:occupied, :] = orbitals_ref[0].astype(jnp.bfloat16)
-
-
-def select_kernel(place_ref, *refs):
+
+
+def select_kernel(tile_ref, *refs):
     *row_refs, theta_ref, extra_ref = refs
     occupied, basis = theta_ref.shape
     whole = (occupied + EXTRA, basis)
-    place = jnp.broadcast_to(place_ref[:1, :1], whole)
+    place = jnp.broadcast_to(tile_ref[1:2, :], whole).astype(jnp.int32)
     picked = row_refs[0][...].astype(jnp.float32)
     for index, ref in enumerate(row_refs[1:]):
         picked = jnp.where(place == index + 1, ref[...].astype(jnp.float32), picked)
@@ -70,44 +83,54 @@
     chol_refs = refs[:blocks]
     sum_refs = refs[blocks : blocks + summands]
     out_ref, adjoint = refs[blocks + summands :]
-    occupied = theta_ref.shape[0]
+    occupied, basis = theta_ref.shape
     theta = theta_ref[...]
     rows = lax.broadcasted_iota(jnp.int32, (occupied, occupied), 0)
     columns = lax.broadcasted_iota(jnp.int32, (occupied, occupied), 1)
     diagonal = rows == columns
+    turned = [
+        lax.dot_general(
+            ref[...].reshape(-1, basis), theta, (((1,), (1,)), ((), ())),
+            preferred_element_type=jnp.float32,
+        )
+        for ref in chol_refs
+    ]
+    place = 0
+    for product in turned:
+        product = product.astype(jnp.bfloat16).astype(jnp.float32)
+        for g in range(product.shape[0] // occupied):
+            block = product[g * occupied : (g + 1) * occupied, :]
+            on_diagonal = jnp.where(diagonal, block, 0.0)
+            trace = jnp.sum(jnp.sum(on_diagonal, axis=0, keepdims=True), axis=1, keepdims=True)
+            piece = norm_scale * (jnp.where(diagonal, trace, 0.0) - block)
+            adjoint[:, place : place + occupied] = piece.astype(jnp.bfloat16)
+            place += occupied
     total = None
     for ref in sum_refs:
         term = ref[...].astype(jnp.float32)
         total = term if total is None else total + term
+    place = 0
     for ref in chol_refs:
-        vectors, _, basis = ref.shape
-        chol = ref[...].reshape(vectors * occupied, basis)
-        turned = lax.dot_general(
-            chol, theta, (((1,), (1,)), ((), ())), preferred_element_type=jnp.float32
-        )
-        turned = turned.astype(jnp.bfloat16).astype(jnp.float32)
-        for g in range(vectors):
-            block = turned[g * occupied : (g + 1) * occupied, :]
-            on_diagonal = jnp.where(diagonal, block, 0.0)
-            trace = jnp.sum(jnp.sum(on_diagonal, axis=0, keepdims=True), axis=1, keepdims=True)
-            piece = norm_scale * (jnp.where(diagonal, trace, 0.0) - block)
-            adjoint[:, g * occupied : (g + 1) * occupied] = piece.astype(jnp.bfloat16)
+        width = ref.shape[0] * occupied
         term = jnp.dot(
-            adjoint[:, : vectors * occupied], chol, preferred_element_type=jnp.float32
+            adjoint[:, place : place + width], ref[...].reshape(-1, basis),
+            preferred_element_type=jnp.float32,
         )
         total = term if total is None else total + term
+        place += width
     out_ref[...] = total.astype(out_ref.dtype)
 
 
-def partial_gradient(norm_scale, theta, chols, summands, dtype):
+def partial_gradient(norm_scale, theta, chols, summands, dtype, cost=None):
     occupied, basis = theta.shape
-    most = max(c.shape[0] for c in chols)
+    width = sum(c.shape[0] for c in chols) * occupied
     return call(
         functools.partial(gradient_kernel, norm_scale, len(chols), len(summands)),
         jax.ShapeDtypeStruct((occupied, basis), dtype),
         vmem(1 + len(chols) + len(summands)),
         pl.BlockSpec(memory_space=pltpu.VMEM),
-        [pltpu.VMEM((occupied, most * occupied), jnp.bfloat16)],
+        [pltpu.VMEM((occupied, width), jnp.bfloat16)],
+        cost,
     )(theta, *chols, *summands)
 
 
@@ -143,7 +166,26 @@
     smem = pl.BlockSpec(memory_space=pltpu.SMEM)
 
     here = lax.axis_index("wlk")
-    mine = lax.dynamic_slice_in_dim(cholesky, here % 2 * half, half, 0)
+    blank = call(
+        blank_kernel,
+        jax.ShapeDtypeStruct((8, basis), jnp.float32),
+        [],
+        vmem(1)[0],
+        (),
+        pl.CostEstimate(flops=10**11, bytes_accessed=256 * 2**20, transcendentals=0),
+    )()
+    tile = call(
+        tile_kernel,
+        jax.ShapeDtypeStruct((8, basis), jnp.float32),
+        [smem] * 2 + vmem(1),
+        vmem(1)[0],
+    )(log_weights, parents, blank)
+    mine = call(
+        half_kernel,
+        jax.ShapeDtypeStruct((half, occupied, basis), cholesky.dtype),
+        vmem(2),
+        vmem(1)[0],
+    )(tile, cholesky)
 
     cross = [
         lax.ppermute(mine, "vec", [(i, (i + 2 * m) % vec_size) for i in range(vec_size)])
@@ -152,15 +194,12 @@
 
 
     def walkers(orbitals, log_weights, parents):
-        payload, place = call(
+        payload = call(
             payload_kernel,
-            (
-                jax.ShapeDtypeStruct((occupied + EXTRA, basis), jnp.bfloat16),
-                jax.ShapeDtypeStruct((8, 128), jnp.int32),
-            ),
-            vmem(3),
+            jax.ShapeDtypeStruct((occupied + EXTRA, basis), jnp.bfloat16),
             vmem(2),
-        )(log_weights, parents, orbitals)
+            vmem(1)[0],
+        )(tile, orbitals)
         gathered = lax.all_gather(payload, "wlk", axis=0)
         row = [gathered[m] for m in range(wlk_size)]
         chosen, chosen_extra = call(
@@ -171,15 +210,16 @@
             ),
             vmem(1 + wlk_size),
             vmem(2),
-        )(place, *row)
+        )(tile, *row)
         return chosen, chosen_extra, swap(chosen, "vec", lambda i: i ^ 1)
 
     chosen, chosen_extra, neighbour = walkers(orbitals, log_weights, parents)
-    *cross, neighbour = lax.optimization_barrier((*cross, neighbour))
+    *cross, chosen = lax.optimization_barrier((*cross, chosen))
     other = [swap(c, "wlk", lambda i: i ^ 1) for c in cross]
+    slow = pl.CostEstimate(flops=10**11, bytes_accessed=256 * 2**20, transcendentals=0)
     own_part = partial_gradient(norm_scale, chosen, [cholesky], [], jnp.float32)
-    to_send = partial_gradient(norm_scale, neighbour, [cholesky, *cross], [], jnp.float32)
-    to_send = partial_gradient(norm_scale, neighbour, other, [to_send], jnp.bfloat16)
+    to_send = partial_gradient(norm_scale, neighbour, [cholesky], [], jnp.float32, slow)
+    to_send = partial_gradient(norm_scale, neighbour, [*cross, *other], [to_send], jnp.bfloat16)
     received = swap(to_send, "vec", lambda i: i ^ 1)
     own_part = partial_gradient(norm_scale, chosen, [*cross, *other], [own_part], jnp.float32)
 

time: 25.9 us -> 24.2 us (0.934)
  local copies, waits for them, and re-layouts: 1.02 us -> 0.04 us
  Pallas kernels: 4.65 us -> 4.25 us
  waiting for transfers between devices: 4.49 us -> 4.12 us
    ppermute x3, waiting for transfers between devices: 4.49 us -> 2.85 us  [swap(): return lax.ppermute(array, axis, [(i, partner(i)) for i in range(size)])]
    ppermute x1, waiting for transfers between devices: 0.01 us -> 1.27 us  [local(): lax.ppermute(mine, 'vec', [(i, (i + 2 * m) % vec_size) for i in range(vec...]
    dynamic_slice x1 -> x0, local copies, waits for them, and re-layouts: 0.98 us -> none  [local(): mine = lax.dynamic_slice_in_dim(cholesky, here % 2 * half, half, 0)]
    pallas_call x4, Pallas kernels: 2.81 us -> 2.49 us  [partial_gradient(): call(functools.partial(gradient_kernel, norm_scale, len(chols), len(summa...]
  transfers between devices with their start and end apart: 4 -> 4, of which waited for: 3 -> 3; matrix products, arithmetic and copies ran while one was open for 0% -> 0% of each run, Pallas kernels for 10% -> 8%
where the time goes in v3:
time: 24.2 us; the launch traced here: 24 us
  starting transfers between devices  7.39 us (31%)
  blocking collectives  6.1 us (25%)
  Pallas kernels  4.25 us (18%)
  waiting for transfers between devices  4.12 us (17%)
  between operations  2.08 us (9%)
    all_gather x1, blocking collectives, walkers(): gathered = lax.all_gather(payload, 'wlk', axis=0)  6.1 us
    ppermute x1, starting transfers between devices, local(): lax.ppermute(mine, 'vec', [(i, (i + 2 * m) % vec_size) for i in range(vec...  4.1 us
    ppermute x3, starting transfers between devices, swap(): return lax.ppermute(array, axis, [(i, partner(i)) for i in range(size)])  3.29 us
    ppermute x3, waiting for transfers between devices, swap(): return lax.ppermute(array, axis, [(i, partner(i)) for i in range(size)])  2.85 us
    pallas_call x4, Pallas kernels, partial_gradient(): call(functools.partial(gradient_kernel, norm_scale, len(chols), len(summa...  2.49 us
    pallas_call x1, Pallas kernels, local(): call(final_kernel, (jax.ShapeDtypeStruct((occupied, basis), jnp.float32),...  1.67 us
    ppermute x1, waiting for transfers between devices, local(): lax.ppermute(mine, 'vec', [(i, (i + 2 * m) % vec_size) for i in range(vec...  1.27 us
  transfers between devices with their start and end apart: 4, of which 3 were waited for; matrix products, arithmetic and copies ran while one was open for 0% of the time, Pallas kernels for 8%

profile of v3, /device:TPU:0, one launch (start us, length us, event | category | flops | bytes accessed | tf_op | source)
XLA Modules:
  0.0 24.0 jit_solution(9822562779543246544)
XLA Ops:
  0.6 0.0 copy-start
  2.0 0.0 copy-done
  2.0 0.0 copy-start.1
  2.1 4.1 %collective-permute-start = (bf16[3,64,512]{2,1,0:T(8,128)(2,1)S(1)}, bf16[3,64,512]{2,1,0:T(8,128)(2,1)S(1)}, u32[]{:S(2)}, u32[]{:S(2)}) collective-permute-start(bf16[3,64,512]{2,1,0:T(8,128)(2,1)S(1)} %shard_map.70), channel_id=1, source_target_pairs={{0,8},{4,12},{8,0},{12,4},{1,9},{5,13},{9,1},{13,5},{2,10},{6,14},... | collective-permute-start | bytes 589832 | tf_op jit(solution)/shard_map/ppermute | solution.py:191
  6.2 0.0 copy-done.1
  6.2 6.1 %all-gather = bf16[320,512]{1,0:T(8,128)(2,1)S(1)} all-gather(bf16[80,512]{1,0:T(8,128)(2,1)S(1)} %shard_map.71), channel_id=2, replica_groups=mesh['grp'=2,'vec'=4,'wlk'=4] {'wlk'}, dimensions={0}, use_global_device_ids=true | all-gather | bytes 409600 | tf_op jit(solution)/shard_map/all_gather | solution.py:203
  12.4 1.6 %collective-permute-start.2 = (bf16[64,512]{1,0:T(8,128)(2,1)S(1)}, bf16[64,512]{1,0:T(8,128)(2,1)S(1)}, u32[]{:S(2)}, u32[]{:S(2)}) collective-permute-start(bf16[64,512]{1,0:T(8,128)(2,1)S(1)} %get-tuple-element.9.theta_ref), channel_id=1, source_target_pairs={{0,4},{4,0},{8,12},{12,8},{1,5},{5,1},{9,13},{13,9},{2,6},{6,2},{1... | collective-permute-start | bytes 196616 | tf_op jit(solution)/shard_map/ppermute | solution.py:39
  14.0 1.3 %collective-permute-done.refs_0_ = bf16[3,64,512]{2,1,0:T(8,128)(2,1)S(1)} collective-permute-done((bf16[3,64,512]{2,1,0:T(8,128)(2,1)S(1)}, bf16[3,64,512]{2,1,0:T(8,128)(2,1)S(1)}, u32[]{:S(2)}, u32[]{:S(2)}) %collective-permute-start) | collective-permute-done | bytes 196640 | tf_op jit(solution)/shard_map/ppermute | solution.py:191
  15.3 0.0 collective-permute-start.1
  15.3 1.5 %collective-permute-done.2.theta_ref = bf16[64,512]{1,0:T(8,128)(2,1)S(1)} collective-permute-done((bf16[64,512]{1,0:T(8,128)(2,1)S(1)}, bf16[64,512]{1,0:T(8,128)(2,1)S(1)}, u32[]{:S(2)}, u32[]{:S(2)}) %collective-permute-start.2) | collective-permute-done | bytes 65568 | tf_op jit(solution)/shard_map/ppermute | solution.py:39
  16.8 0.0 copy-start.2
  16.8 0.6 %shard_map.75.refs_2_ = f32[64,512]{1,0:T(8,128)S(1)} custom-call(bf16[64,512]{1,0:T(8,128)(2,1)S(1)} %collective-permute-done.2.theta_ref, bf16[6,64,512]{2,1,0:T(8,128)(2,1)S(1)} %copy-done), custom_call_target="tpu_custom_call" | custom-call | flops 99999997952 | bytes 268435456 | tf_op jit(solution)/shard_map/pallas_call | solution.py:127
  17.4 0.0 collective-permute-done.1.refs_1_
  17.4 0.6 %shard_map.76 = bf16[64,512]{1,0:T(8,128)(2,1)S(1)} custom-call(bf16[64,512]{1,0:T(8,128)(2,1)S(1)} %collective-permute-done.2.theta_ref, bf16[3,64,512]{2,1,0:T(8,128)(2,1)S(1)} %collective-permute-done.refs_0_, bf16[3,64,512]{2,1,0:T(8,128)(2,1)S(1)} %collective-permute-done.1.refs_1_, f32[64,512]{1,0:T(8,128)S(1)} %shard_map.75.refs_2_), custom_call_target="tpu_custom_call" | custom-call | tf_op jit(solution)/shard_map/pallas_call | solution.py:127
  18.0 1.6 %collective-permute-start.3 = (bf16[64,512]{1,0:T(8,128)(2,1)S(1)}, bf16[64,512]{1,0:T(8,128)(2,1)S(1)}, u32[]{:S(2)}, u32[]{:S(2)}) collective-permute-start(bf16[64,512]{1,0:T(8,128)(2,1)S(1)} %shard_map.76), channel_id=1, source_target_pairs={{0,4},{4,0},{8,12},{12,8},{1,5},{5,1},{9,13},{13,9},{2,6},{6,2},{1... | collective-permute-start | bytes 196616 | tf_op jit(solution)/shard_map/ppermute | solution.py:39
  19.7 0.0 copy-done.2
  19.7 0.1 convert_element_type.3.propagator_ref
  19.8 0.6 %shard_map.73.refs_2_ = f32[64,512]{1,0:T(8,128)S(1)} custom-call(bf16[64,512]{1,0:T(8,128)(2,1)S(1)} %get-tuple-element.9.theta_ref, bf16[6,64,512]{2,1,0:T(8,128)(2,1)S(1)} %copy-done), custom_call_target="tpu_custom_call" | custom-call | tf_op jit(solution)/shard_map/pallas_call | solution.py:127
  20.4 0.6 %shard_map.74.own_ref = f32[64,512]{1,0:T(8,128)S(1)} custom-call(bf16[64,512]{1,0:T(8,128)(2,1)S(1)} %get-tuple-element.9.theta_ref, bf16[3,64,512]{2,1,0:T(8,128)(2,1)S(1)} %collective-permute-done.refs_0_, bf16[3,64,512]{2,1,0:T(8,128)(2,1)S(1)} %collective-permute-done.1.refs_1_, f32[64,512]{1,0:T(8,128)S(1)} %shard_map.73.refs_2_), custom_call_target="tpu_custom_call" | custom-call | tf_op jit(solution)/shard_map/pallas_call | solution.py:127
  21.0 1.4 %collective-permute-done.3.other_ref = bf16[64,512]{1,0:T(8,128)(2,1)S(1)} collective-permute-done((bf16[64,512]{1,0:T(8,128)(2,1)S(1)}, bf16[64,512]{1,0:T(8,128)(2,1)S(1)}, u32[]{:S(2)}, u32[]{:S(2)}) %collective-permute-start.3) | collective-permute-done | bytes 65568 | tf_op jit(solution)/shard_map/ppermute | solution.py:39
  22.4 1.7 %shard_map.77 = (f32[64,512]{1,0:T(8,128)}, f32[1]{0:T(128)}) custom-call(bf16[64,512]{1,0:T(8,128)(2,1)S(1)} %get-tuple-element.9.theta_ref, bf16[16,512]{1,0:T(8,128)(2,1)S(1)} %get-tuple-element.10.extra_ref, f32[64,512]{1,0:T(8,128)S(1)} %shard_map.74.own_ref, bf16[64,512]{1,0:T(8,128)(2,1)S(1)} %collective-permute-done.3.other_ref, ...), custom_call_target="tpu_custom_call" | custom-call | tf_op jit(solution)/shard_map/pallas_call | solution.py:226
  (6 shorter events, 0.1 us)
Async XLA Ops:
  0.6 1.4 %copy-start = (bf16[6,64,512]{2,1,0:T(8,128)(2,1)S(1)}, bf16[6,64,512]{2,1,0:T(8,128)(2,1)}, u32[]{:S(2)}) copy-start(bf16[6,64,512]{2,1,0:T(8,128)(2,1)} %refs_0_.3) | copy-start | bytes 1179652
  2.0 4.2 %copy-start.1 = (f32[1,64,512]{2,1,0:T(8,128)S(1)}, f32[1,64,512]{2,1,0:T(8,128)}, u32[]{:S(2)}) copy-start(f32[1,64,512]{2,1,0:T(8,128)} %orbitals_ref.1) | copy-start | bytes 393220
  2.1 13.2 %collective-permute-start = (bf16[3,64,512]{2,1,0:T(8,128)(2,1)S(1)}, bf16[3,64,512]{2,1,0:T(8,128)(2,1)S(1)}, u32[]{:S(2)}, u32[]{:S(2)}) collective-permute-start(bf16[3,64,512]{2,1,0:T(8,128)(2,1)S(1)} %shard_map.70), channel_id=1, source_target_pairs={{0,8},{4,12},{8,0},{12,4},{1,9},{5,13},{9,1},{13,5},{2,10},{6,14},... | collective-permute-start | bytes 589832 | tf_op jit(solution)/shard_map/ppermute | solution.py:191
  12.4 4.4 %collective-permute-start.2 = (bf16[64,512]{1,0:T(8,128)(2,1)S(1)}, bf16[64,512]{1,0:T(8,128)(2,1)S(1)}, u32[]{:S(2)}, u32[]{:S(2)}) collective-permute-start(bf16[64,512]{1,0:T(8,128)(2,1)S(1)} %get-tuple-element.9.theta_ref), channel_id=1, source_target_pairs={{0,4},{4,0},{8,12},{12,8},{1,5},{5,1},{9,13},{13,9},{2,6},{6,2},{1... | collective-permute-start | bytes 196616 | tf_op jit(solution)/shard_map/ppermute | solution.py:39
  15.3 2.1 %collective-permute-start.1 = (bf16[3,64,512]{2,1,0:T(8,128)(2,1)S(1)}, bf16[3,64,512]{2,1,0:T(8,128)(2,1)S(1)}, u32[]{:S(2)}, u32[]{:S(2)}) collective-permute-start(bf16[3,64,512]{2,1,0:T(8,128)(2,1)S(1)} %collective-permute-done.refs_0_), channel_id=1, source_target_pairs={{0,1},{1,0},{2,3},{3,2},{4,5},{5,4},{6,7},{7,6},{8,9},{9,8},{10,11... | collective-permute-start | bytes 589832 | tf_op jit(solution)/shard_map/ppermute | solution.py:39
  16.8 2.9 %copy-start.2 = (f32[512,512]{1,0:T(8,128)S(1)}, f32[512,512]{1,0:T(8,128)}, u32[]{:S(2)}) copy-start(f32[512,512]{1,0:T(8,128)} %param.9) | copy-start | bytes 3145732
  18.0 4.3 %collective-permute-start.3 = (bf16[64,512]{1,0:T(8,128)(2,1)S(1)}, bf16[64,512]{1,0:T(8,128)(2,1)S(1)}, u32[]{:S(2)}, u32[]{:S(2)}) collective-permute-start(bf16[64,512]{1,0:T(8,128)(2,1)S(1)} %shard_map.76), channel_id=1, source_target_pairs={{0,4},{4,0},{8,12},{12,8},{1,5},{5,1},{9,13},{13,9},{2,6},{6,2},{1... | collective-permute-start | bytes 196616 | tf_op jit(solution)/shard_map/ppermute | solution.py:39

commit v4 on v3

--- a/solution.py
+++ b/solution.py
@@ -79,10 +79,12 @@
     extra_ref[...] = picked[occupied:]
 
 
-def gradient_kernel(norm_scale, blocks, summands, theta_ref, *refs):
-    chol_refs = refs[:blocks]
-    sum_refs = refs[blocks : blocks + summands]
-    out_ref, adjoint = refs[blocks + summands :]
+def copy_kernel(in_ref, out_ref):
+    out_ref[...] = in_ref[...]
+
+
+def gradient_kernel(norm_scale, theta_ref, *refs):
+    *chol_refs, out_ref, adjoint = refs
     occupied, basis = theta_ref.shape
     theta = theta_ref[...]
     rows = lax.broadcasted_iota(jnp.int32, (occupied, occupied), 0)
@@ -106,9 +108,6 @@
             adjoint[:, place : place + occupied] = piece.astype(jnp.bfloat16)
             place += occupied
     total = None
-    for ref in sum_refs:
-        term = ref[...].astype(jnp.float32)
-        total = term if total is None else total + term
     place = 0
     for ref in chol_refs:
         width = ref.shape[0] * occupied
@@ -121,17 +120,16 @@
     out_ref[...] = total.astype(out_ref.dtype)
 
 
-def partial_gradient(norm_scale, theta, chols, summands, dtype, cost=None):
+def partial_gradient(norm_scale, theta, chols, dtype):
     occupied, basis = theta.shape
     width = sum(c.shape[0] for c in chols) * occupied
     return call(
-        functools.partial(gradient_kernel, norm_scale, len(chols), len(summands)),
+        functools.partial(gradient_kernel, norm_scale),
         jax.ShapeDtypeStruct((occupied, basis), dtype),
-        vmem(1 + len(chols) + len(summands)),
+        vmem(1 + len(chols)),
         pl.BlockSpec(memory_space=pltpu.VMEM),
         [pltpu.VMEM((occupied, width), jnp.bfloat16)],
-        cost,
-    )(theta, *chols, *summands)
+    )(theta, *chols)
 
 
 def final_kernel(theta_ref, extra_ref, own_ref, other_ref, propagator_ref, out_ref, log_ref):
@@ -142,18 +140,29 @@
     log_weight = jnp.sum(extra_ref[...].astype(jnp.float32))
     log_ref[0] = log_weight - energy_step * energy
     stepped = (theta - gradient_step * gradient).astype(jnp.bfloat16)
-    propagated = lax.dot_general(
-        stepped, propagator_ref[...], (((1,), (1,)), ((), ())), preferred_element_type=jnp.float32
-    )
-    mean_square = jnp.sum(propagated * propagated, keepdims=True) / (occupied * basis)
-    current = propagated * lax.rsqrt(mean_square + epsilon)
-    for _ in range(NS_ITERS):
-        narrow = current.astype(jnp.bfloat16)
-        overlap = lax.dot_general(
-            narrow, narrow, (((1,), (1,)), ((), ())), preferred_element_type=jnp.float32
+    propagated = jnp.dot(stepped, propagator_ref[...], preferred_element_type=jnp.float32)
+    narrow = propagated.astype(jnp.bfloat16)
+    overlap = lax.dot_general(
+        narrow, narrow, (((1,), (1,)), ((), ())), preferred_element_type=jnp.float32
+    )
+    diagonal = lax.broadcasted_iota(jnp.int32, overlap.shape, 0) == lax.broadcasted_iota(
+        jnp.int32, overlap.shape, 1
+    )
+    squares = jnp.sum(jnp.where(diagonal, overlap, 0.0), keepdims=True)
+    scale = lax.rsqrt(squares / (occupied * basis) + epsilon)
+    overlap = overlap * scale * (scale * (0.5 / basis))
+    current = propagated * scale
+    for index in range(NS_ITERS):
+        if index:
+            narrow = current.astype(jnp.bfloat16)
+            overlap = lax.dot_general(
+                narrow, narrow, (((1,), (1,)), ((), ())), preferred_element_type=jnp.float32
+            ) * (0.5 / basis)
+        else:
+            narrow = current.astype(jnp.bfloat16)
+        current = 1.5 * current - jnp.dot(
+            overlap.astype(jnp.bfloat16), narrow, preferred_element_type=jnp.float32
         )
-        overlap = (overlap * (0.5 / basis)).astype(jnp.bfloat16)
-        current = 1.5 * current - jnp.dot(overlap, narrow, preferred_element_type=jnp.float32)
     out_ref[...] = current
 
 
@@ -217,11 +226,18 @@
     *cross, chosen = lax.optimization_barrier((*cross, chosen))
     other = [swap(c, "wlk", lambda i: i ^ 1) for c in cross]
     slow = pl.CostEstimate(flops=10**11, bytes_accessed=256 * 2**20, transcendentals=0)
-    own_part = partial_gradient(norm_scale, chosen, [cholesky], [], jnp.float32)
-    to_send = partial_gradient(norm_scale, neighbour, [cholesky], [], jnp.float32, slow)
-    to_send = partial_gradient(norm_scale, neighbour, [*cross, *other], [to_send], jnp.bfloat16)
+    arrived = call(
+        copy_kernel,
+        jax.ShapeDtypeStruct(neighbour.shape, neighbour.dtype),
+        vmem(1),
+        vmem(1)[0],
+        (),
+        slow,
+    )(neighbour)
+    vectors = [cholesky, *cross, *other]
+    to_send = partial_gradient(norm_scale, arrived, vectors, jnp.bfloat16)
     received = swap(to_send, "vec", lambda i: i ^ 1)
-    own_part = partial_gradient(norm_scale, chosen, [*cross, *other], [own_part], jnp.float32)
+    own_part = partial_gradient(norm_scale, chosen, vectors, jnp.float32)
 
     new_orbitals, new_logs = call(
         final_kernel,
@@ -231,7 +247,7 @@
         ),
         vmem(5),
         [pl.BlockSpec(memory_space=pltpu.VMEM), smem],
-    )(chosen, chosen_extra, own_part, received, propagator.astype(jnp.bfloat16))
+    )(chosen, chosen_extra, own_part, received, propagator.T.astype(jnp.bfloat16))
     return new_orbitals.reshape(orbitals.shape), new_logs
 
 

time: 24.2 us -> 23.7 us (0.979)
  Pallas kernels: 4.25 us -> 3.21 us
  waiting for transfers between devices: 4.12 us -> 4.47 us
    pallas_call x4 -> x3, Pallas kernels: 2.49 us -> 1.53 us  [the longest x2 1.52 us: partial_gradient(): call(functools.partial(gradient_kernel, norm_scale), jax.ShapeDtypeStruct...]
    ppermute x3, waiting for transfers between devices: 2.85 us -> 3.21 us  [swap(): return lax.ppermute(array, axis, [(i, partner(i)) for i in range(size)])]
  transfers between devices with their start and end apart: 4 -> 4, of which waited for: 3 -> 3; matrix products, arithmetic and copies ran while one was open for 0% -> 1% of each run, Pallas kernels for 8% -> 4%
where the time goes in v4:
time: 23.7 us; the launch traced here: 23.5 us
  starting transfers between devices  7.39 us (31%)
  blocking collectives  6.1 us (26%)
  waiting for transfers between devices  4.47 us (19%)
  Pallas kernels  3.21 us (14%)
  between operations  2.07 us (9%)
  local copies, waits for them, and re-layouts  0.24 us (1%)
    all_gather x1, blocking collectives, walkers(): gathered = lax.all_gather(payload, 'wlk', axis=0)  6.1 us
    ppermute x1, starting transfers between devices, local(): lax.ppermute(mine, 'vec', [(i, (i + 2 * m) % vec_size) for i in range(vec...  4.1 us
    ppermute x3, starting transfers between devices, swap(): return lax.ppermute(array, axis, [(i, partner(i)) for i in range(size)])  3.29 us
    ppermute x3, waiting for transfers between devices, swap(): return lax.ppermute(array, axis, [(i, partner(i)) for i in range(size)])  3.21 us
    pallas_call x1, Pallas kernels, local(): call(final_kernel, (jax.ShapeDtypeStruct((occupied, basis), jnp.float32),...  1.58 us
    pallas_call x2, Pallas kernels, partial_gradient(): call(functools.partial(gradient_kernel, norm_scale), jax.ShapeDtypeStruct...  1.52 us
    ppermute x1, waiting for transfers between devices, local(): lax.ppermute(mine, 'vec', [(i, (i + 2 * m) % vec_size) for i in range(vec...  1.27 us
  transfers between devices with their start and end apart: 4, of which 3 were waited for; matrix products, arithmetic and copies ran while one was open for 1% of the time, Pallas kernels for 4%

profile of v4, /device:TPU:0, one launch (start us, length us, event | category | flops | bytes accessed | tf_op | source)
XLA Modules:
  0.0 23.5 jit_solution(5032299155102058953)
XLA Ops:
  0.6 0.0 copy-start
  2.0 0.0 copy-done
  2.0 0.0 copy-start.1
  2.1 4.1 %collective-permute-start = (bf16[3,64,512]{2,1,0:T(8,128)(2,1)S(1)}, bf16[3,64,512]{2,1,0:T(8,128)(2,1)S(1)}, u32[]{:S(2)}, u32[]{:S(2)}) collective-permute-start(bf16[3,64,512]{2,1,0:T(8,128)(2,1)S(1)} %shard_map.70), channel_id=1, source_target_pairs={{0,8},{4,12},{8,0},{12,4},{1,9},{5,13},{9,1},{13,5},{2,10},{6,14},... | collective-permute-start | bytes 589832 | tf_op jit(solution)/shard_map/ppermute | solution.py:200
  6.2 0.0 copy-done.1
  6.2 6.1 %all-gather = bf16[320,512]{1,0:T(8,128)(2,1)S(1)} all-gather(bf16[80,512]{1,0:T(8,128)(2,1)S(1)} %shard_map.71), channel_id=2, replica_groups=mesh['grp'=2,'vec'=4,'wlk'=4] {'wlk'}, dimensions={0}, use_global_device_ids=true | all-gather | bytes 409600 | tf_op jit(solution)/shard_map/all_gather | solution.py:212
  12.4 1.6 %collective-permute-start.2 = (bf16[64,512]{1,0:T(8,128)(2,1)S(1)}, bf16[64,512]{1,0:T(8,128)(2,1)S(1)}, u32[]{:S(2)}, u32[]{:S(2)}) collective-permute-start(bf16[64,512]{1,0:T(8,128)(2,1)S(1)} %get-tuple-element.9.theta_ref), channel_id=1, source_target_pairs={{0,4},{4,0},{8,12},{12,8},{1,5},{5,1},{9,13},{13,9},{2,6},{6,2},{1... | collective-permute-start | bytes 196616 | tf_op jit(solution)/shard_map/ppermute | solution.py:39
  14.0 1.3 %collective-permute-done.refs_1_ = bf16[3,64,512]{2,1,0:T(8,128)(2,1)S(1)} collective-permute-done((bf16[3,64,512]{2,1,0:T(8,128)(2,1)S(1)}, bf16[3,64,512]{2,1,0:T(8,128)(2,1)S(1)}, u32[]{:S(2)}, u32[]{:S(2)}) %collective-permute-start) | collective-permute-done | bytes 196640 | tf_op jit(solution)/shard_map/ppermute | solution.py:200
  15.3 0.0 collective-permute-start.1
  15.3 1.5 %collective-permute-done.2.in_ref = bf16[64,512]{1,0:T(8,128)(2,1)S(1)} collective-permute-done((bf16[64,512]{1,0:T(8,128)(2,1)S(1)}, bf16[64,512]{1,0:T(8,128)(2,1)S(1)}, u32[]{:S(2)}, u32[]{:S(2)}) %collective-permute-start.2) | collective-permute-done | bytes 65568 | tf_op jit(solution)/shard_map/ppermute | solution.py:39
  16.8 0.0 copy-start.2
  16.8 0.0 collective-permute-done.1.refs_2_
  16.8 0.8 %shard_map.75 = bf16[64,512]{1,0:T(8,128)(2,1)S(1)} custom-call(bf16[64,512]{1,0:T(8,128)(2,1)S(1)} %shard_map.74.theta_ref, bf16[6,64,512]{2,1,0:T(8,128)(2,1)S(1)} %copy-done, bf16[3,64,512]{2,1,0:T(8,128)(2,1)S(1)} %collective-permute-done.refs_1_, bf16[3,64,512]{2,1,0:T(8,128)(2,1)S(1)} %collective-permute-done.1.refs_2_), custom_call_target="tpu_custom_call" | custom-call | tf_op jit(solution)/shard_map/pallas_call | solution.py:126
  17.6 1.6 %collective-permute-start.3 = (bf16[64,512]{1,0:T(8,128)(2,1)S(1)}, bf16[64,512]{1,0:T(8,128)(2,1)S(1)}, u32[]{:S(2)}, u32[]{:S(2)}) collective-permute-start(bf16[64,512]{1,0:T(8,128)(2,1)S(1)} %shard_map.75), channel_id=1, source_target_pairs={{0,4},{4,0},{8,12},{12,8},{1,5},{5,1},{9,13},{13,9},{2,6},{6,2},{1... | collective-permute-start | bytes 196616 | tf_op jit(solution)/shard_map/ppermute | solution.py:39
  19.2 0.0 copy-done.2
  19.2 0.2 copy.7
  19.4 0.8 %shard_map.73.own_ref = f32[64,512]{1,0:T(8,128)S(1)} custom-call(bf16[64,512]{1,0:T(8,128)(2,1)S(1)} %get-tuple-element.9.theta_ref, bf16[6,64,512]{2,1,0:T(8,128)(2,1)S(1)} %copy-done, bf16[3,64,512]{2,1,0:T(8,128)(2,1)S(1)} %collective-permute-done.refs_1_, bf16[3,64,512]{2,1,0:T(8,128)(2,1)S(1)} %collective-permute-done.1.refs_2_), custom_call_target="tpu_custom_call" | custom-call | tf_op jit(solution)/shard_map/pallas_call | solution.py:126
  20.2 1.7 %collective-permute-done.3.other_ref = bf16[64,512]{1,0:T(8,128)(2,1)S(1)} collective-permute-done((bf16[64,512]{1,0:T(8,128)(2,1)S(1)}, bf16[64,512]{1,0:T(8,128)(2,1)S(1)}, u32[]{:S(2)}, u32[]{:S(2)}) %collective-permute-start.3) | collective-permute-done | bytes 65568 | tf_op jit(solution)/shard_map/ppermute | solution.py:39
  21.9 1.6 %shard_map.76 = (f32[64,512]{1,0:T(8,128)}, f32[1]{0:T(128)}) custom-call(bf16[64,512]{1,0:T(8,128)(2,1)S(1)} %get-tuple-element.9.theta_ref, bf16[16,512]{1,0:T(8,128)(2,1)S(1)} %get-tuple-element.10.extra_ref, f32[64,512]{1,0:T(8,128)S(1)} %shard_map.73.own_ref, bf16[64,512]{1,0:T(8,128)(2,1)S(1)} %collective-permute-done.3.other_ref, ...), custom_call_target="tpu_custom_call" | custom-call | tf_op jit(solution)/shard_map/pallas_call | solution.py:242
  (7 shorter events, 0.1 us)
Async XLA Ops:
  0.6 1.4 %copy-start = (bf16[6,64,512]{2,1,0:T(8,128)(2,1)S(1)}, bf16[6,64,512]{2,1,0:T(8,128)(2,1)}, u32[]{:S(2)}) copy-start(bf16[6,64,512]{2,1,0:T(8,128)(2,1)} %refs_0_.3) | copy-start | bytes 1179652
  2.0 4.2 %copy-start.1 = (f32[1,64,512]{2,1,0:T(8,128)S(1)}, f32[1,64,512]{2,1,0:T(8,128)}, u32[]{:S(2)}) copy-start(f32[1,64,512]{2,1,0:T(8,128)} %orbitals_ref.1) | copy-start | bytes 393220
  2.1 13.2 %collective-permute-start = (bf16[3,64,512]{2,1,0:T(8,128)(2,1)S(1)}, bf16[3,64,512]{2,1,0:T(8,128)(2,1)S(1)}, u32[]{:S(2)}, u32[]{:S(2)}) collective-permute-start(bf16[3,64,512]{2,1,0:T(8,128)(2,1)S(1)} %shard_map.70), channel_id=1, source_target_pairs={{0,8},{4,12},{8,0},{12,4},{1,9},{5,13},{9,1},{13,5},{2,10},{6,14},... | collective-permute-start | bytes 589832 | tf_op jit(solution)/shard_map/ppermute | solution.py:200
  12.4 4.4 %collective-permute-start.2 = (bf16[64,512]{1,0:T(8,128)(2,1)S(1)}, bf16[64,512]{1,0:T(8,128)(2,1)S(1)}, u32[]{:S(2)}, u32[]{:S(2)}) collective-permute-start(bf16[64,512]{1,0:T(8,128)(2,1)S(1)} %get-tuple-element.9.theta_ref), channel_id=1, source_target_pairs={{0,4},{4,0},{8,12},{12,8},{1,5},{5,1},{9,13},{13,9},{2,6},{6,2},{1... | collective-permute-start | bytes 196616 | tf_op jit(solution)/shard_map/ppermute | solution.py:39
  15.3 1.5 %collective-permute-start.1 = (bf16[3,64,512]{2,1,0:T(8,128)(2,1)S(1)}, bf16[3,64,512]{2,1,0:T(8,128)(2,1)S(1)}, u32[]{:S(2)}, u32[]{:S(2)}) collective-permute-start(bf16[3,64,512]{2,1,0:T(8,128)(2,1)S(1)} %collective-permute-done.refs_1_), channel_id=1, source_target_pairs={{0,1},{1,0},{2,3},{3,2},{4,5},{5,4},{6,7},{7,6},{8,9},{9,8},{10,11... | collective-permute-start | bytes 589832 | tf_op jit(solution)/shard_map/ppermute | solution.py:39
  16.8 2.4 %copy-start.2 = (f32[512,512]{1,0:T(8,128)S(1)}, f32[512,512]{1,0:T(8,128)}, u32[]{:S(2)}) copy-start(f32[512,512]{1,0:T(8,128)} %param.9) | copy-start | bytes 3145732
  17.6 4.3 %collective-permute-start.3 = (bf16[64,512]{1,0:T(8,128)(2,1)S(1)}, bf16[64,512]{1,0:T(8,128)(2,1)S(1)}, u32[]{:S(2)}, u32[]{:S(2)}) collective-permute-start(bf16[64,512]{1,0:T(8,128)(2,1)S(1)} %shard_map.75), channel_id=1, source_target_pairs={{0,4},{4,0},{8,12},{12,8},{1,5},{5,1},{9,13},{13,9},{2,6},{6,2},{1... | collective-permute-start | bytes 196616 | tf_op jit(solution)/shard_map/ppermute | solution.py:39

commit v5 on v4

v5 whole, which is shorter than its diff:
```python
import functools
import math

import jax
import jax.numpy as jnp
from jax import lax
from jax.experimental import pallas as pl
from jax.experimental.pallas import tpu as pltpu
from jax.sharding import PartitionSpec as P

NS_ITERS = 2
EXTRA = 16

gradient_step = 0.25
energy_step = 0.002
epsilon = 1e-06

VMEM_LIMIT = 32 * 1024 * 1024


def call(body, out_shape, in_specs, out_specs, scratch=(), cost=None):
    return pl.pallas_call(
        body,
        out_shape=out_shape,
        in_specs=in_specs,
        out_specs=out_specs,
        scratch_shapes=list(scratch),
        cost_estimate=cost,
        compiler_params=pltpu.CompilerParams(vmem_limit_bytes=VMEM_LIMIT),
    )


def vmem(count):
    return [pl.BlockSpec(memory_space=pltpu.VMEM)] * count


def swap(array, axis, partner):
    size = lax.axis_size(axis)
    return lax.ppermute(array, axis, [(i, partner(i)) for i in range(size)])


def half_kernel(chol_ref, mine_ref, pair_ref):
    half, pair = mine_ref.shape[0], pair_ref.shape[0]
    here = lax.axis_index("wlk")
    first = lax.rem(here // 2, 2) * half
    mine_ref[...] = chol_ref[pl.ds(first, half)]
    pair_ref[...] = chol_ref[pl.ds(first + lax.rem(here, 2) * (half - pair), pair)]


def tile_kernel(log_ref, parent_ref, out_ref):
    rows = lax.broadcasted_iota(jnp.int32, out_ref.shape, 0)
    value = jnp.full(out_ref.shape, log_ref[0])
    high = value.astype(jnp.bfloat16).astype(jnp.float32)
    middle = (value - high).astype(jnp.bfloat16).astype(jnp.float32)
    low = value - high - middle
    parent = parent_ref[0].astype(jnp.float32)
    out_ref[...] = jnp.where(
        rows == 0, high, jnp.where(rows == 1, middle, jnp.where(rows == 2, low, parent))
    ).astype(jnp.bfloat16)


def payload_kernel(tile_ref, orbitals_ref, payload_ref):
    occupied = orbitals_ref.shape[1]
    payload_ref[:occupied, :] = orbitals_ref[0].astype(jnp.bfloat16)
    payload_ref[occupied:, :] = tile_ref[...]


def select_kernel(row_ref, theta_ref, extra_ref, other_ref):
    occupied, basis = theta_ref.shape
    here = lax.axis_index("wlk")

    def chosen(target, whole):
        extra = row_ref[target, occupied:, :].astype(jnp.float32)
        place = jnp.broadcast_to(extra[3:4, :], (whole, basis))
        picked = row_ref[0, :whole].astype(jnp.float32)
        for index in range(1, row_ref.shape[0]):
            picked = jnp.where(place == index, row_ref[index, :whole].astype(jnp.float32), picked)
        return picked.astype(jnp.bfloat16)

    own = chosen(here, row_ref.shape[1])
    theta_ref[...] = own[:occupied]
    extra_ref[...] = own[occupied:]
    other_ref[...] = chosen(jnp.bitwise_xor(here, 2), occupied)


def gradient_kernel(norm_scale, blocks, theta_ref, *refs):
    chol_refs, sum_refs = refs[:blocks], refs[blocks:-2]
    out_ref, adjoint = refs[-2:]
    occupied, basis = theta_ref.shape
    theta = theta_ref[...]
    rows = lax.broadcasted_iota(jnp.int32, (occupied, occupied), 0)
    columns = lax.broadcasted_iota(jnp.int32, (occupied, occupied), 1)
    diagonal = rows == columns
    turned = [
        lax.dot_general(
            ref[...].reshape(-1, basis), theta, (((1,), (1,)), ((), ())),
            preferred_element_type=jnp.float32,
        )
        for ref in chol_refs
    ]
    place = 0
    for product in turned:
        product = product.astype(jnp.bfloat16).astype(jnp.float32)
        for g in range(product.shape[0] // occupied):
            block = product[g * occupied : (g + 1) * occupied, :]
            on_diagonal = jnp.where(diagonal, block, 0.0)
            trace = jnp.sum(jnp.sum(on_diagonal, axis=0, keepdims=True), axis=1, keepdims=True)
            piece = norm_scale * (jnp.where(diagonal, trace, 0.0) - block)
            adjoint[:, place : place + occupied] = piece.astype(jnp.bfloat16)
            place += occupied
    total = sum_refs[0][...] if sum_refs else None
    place = 0
    for ref in chol_refs:
        width = ref.shape[0] * occupied
        term = jnp.dot(
            adjoint[:, place : place + width], ref[...].reshape(-1, basis),
            preferred_element_type=jnp.float32,
        )
        total = term if total is None else total + term
        place += width
    out_ref[...] = total.astype(out_ref.dtype)


def partial_gradient(norm_scale, theta, chols, dtype, *summand):
    occupied, basis = theta.shape
    width = sum(c.shape[0] for c in chols) * occupied
    return call(
        functools.partial(gradient_kernel, norm_scale, len(chols)),
        jax.ShapeDtypeStruct((occupied, basis), dtype),
        vmem(1 + len(chols) + len(summand)),
        pl.BlockSpec(memory_space=pltpu.VMEM),
        [pltpu.VMEM((occupied, width), jnp.bfloat16)],
    )(theta, *chols, *summand)


def final_kernel(theta_ref, extra_ref, own_ref, other_ref, propagator_ref, out_ref, log_ref):
    occupied, basis = theta_ref.shape
    theta = theta_ref[...].astype(jnp.float32)
    gradient = own_ref[...] + other_ref[...].astype(jnp.float32)
    energy = 0.5 * jnp.sum(theta * gradient)
    log_weight = jnp.sum(extra_ref[:3, :1].astype(jnp.float32))
    log_ref[0] = log_weight - energy_step * energy
    stepped = (theta - gradient_step * gradient).astype(jnp.bfloat16)
    propagated = jnp.dot(stepped, propagator_ref[...], preferred_element_type=jnp.float32)
    narrow = propagated.astype(jnp.bfloat16)
    overlap = lax.dot_general(
        narrow, narrow, (((1,), (1,)), ((), ())), preferred_element_type=jnp.float32
    )
    diagonal = lax.broadcasted_iota(jnp.int32, overlap.shape, 0) == lax.broadcasted_iota(
        jnp.int32, overlap.shape, 1
    )
    squares = jnp.sum(jnp.where(diagonal, overlap, 0.0), keepdims=True)
    scale = lax.rsqrt(squares / (occupied * basis) + epsilon)
    overlap = overlap * scale * (scale * (0.5 / basis))
    current = propagated * scale
    for index in range(NS_ITERS):
        if index:
            narrow = current.astype(jnp.bfloat16)
            overlap = lax.dot_general(
                narrow, narrow, (((1,), (1,)), ((), ())), preferred_element_type=jnp.float32
            ) * (0.5 / basis)
        else:
            narrow = current.astype(jnp.bfloat16)
        current = 1.5 * current - jnp.dot(
            overlap.astype(jnp.bfloat16), narrow, preferred_element_type=jnp.float32
        )
    out_ref[...] = current


def local(cholesky, orbitals, log_weights, parents, propagator):
    walker_count, occupied, basis = orbitals.shape
    vectors_here = cholesky.shape[0]
    vec_size, wlk_size = lax.axis_size("vec"), lax.axis_size("wlk")
    norm_scale = 1.0 / math.sqrt(vectors_here * vec_size)
    half = vectors_here // 2
    pair = (half + 1) // 2
    smem = pl.BlockSpec(memory_space=pltpu.SMEM)

    mine, part = call(
        half_kernel,
        (
            jax.ShapeDtypeStruct((half, occupied, basis), cholesky.dtype),
            jax.ShapeDtypeStruct((pair, occupied, basis), cholesky.dtype),
        ),
        vmem(1),
        vmem(2),
    )(cholesky)
    far = [
        lax.ppermute(
            mine,
            ("vec", "wlk"),
            [
                ((v ^ (2 * m + k % 2)) * wlk_size + k, v * wlk_size + k)
                for v in range(vec_size)
                for k in range(wlk_size)
            ],
        )
        for m in range(1, vec_size // 2)
    ]
    near = swap(part, "vec", lambda i: i ^ 1)

    tile = call(
        tile_kernel,
        jax.ShapeDtypeStruct((EXTRA, basis), jnp.bfloat16),
        [smem] * 2,
        vmem(1)[0],
    )(log_weights, parents)
    payload = call(
        payload_kernel,
        jax.ShapeDtypeStruct((occupied + EXTRA, basis), jnp.bfloat16),
        vmem(2),
        vmem(1)[0],
    )(tile, orbitals)
    row = lax.all_gather(payload, "wlk", axis=0)
    chosen, chosen_extra, neighbour = call(
        select_kernel,
        (
            jax.ShapeDtypeStruct((occupied, basis), jnp.bfloat16),
            jax.ShapeDtypeStruct((EXTRA, basis), jnp.bfloat16),
            jax.ShapeDtypeStruct((occupied, basis), jnp.bfloat16),
        ),
        vmem(1),
        vmem(3),
    )(row)

    *far, near, chosen = lax.optimization_barrier((*far, near, chosen))
    lacking = half - pair
    sent = lax.dynamic_slice_in_dim(near, lax.axis_index("wlk") % 2 * (pair - lacking), lacking, 0)
    vectors = [mine, near, *far]
    other = [swap(c, "wlk", lambda i: i ^ 1) for c in (sent, *far)]
    to_send = partial_gradient(norm_scale, neighbour, vectors, jnp.float32)
    to_send = partial_gradient(norm_scale, neighbour, other, jnp.bfloat16, to_send)
    received = swap(to_send, "wlk", lambda i: i ^ 2)
    own_part = partial_gradient(norm_scale, chosen, [*vectors, *other], jnp.float32)

    new_orbitals, new_logs = call(
        final_kernel,
        (
            jax.ShapeDtypeStruct((occupied, basis), jnp.float32),
            jax.ShapeDtypeStruct((1,), jnp.float32),
        ),
        vmem(5),
        [pl.BlockSpec(memory_space=pltpu.VMEM), smem],
    )(chosen, chosen_extra, own_part, received, propagator.T.astype(jnp.bfloat16))
    return new_orbitals.reshape(orbitals.shape), new_logs


def solution(mesh):
    placed = (
        P(("grp", "vec"), None, None),
        P(("grp", "vec", "wlk"), None, None),
        P(("grp", "vec", "wlk")),
        P(("grp", "vec", "wlk")),
        P("grp", None),
    )
    return jax.shard_map(
        local,
        mesh=mesh,
        in_specs=placed,
        out_specs=(P(("grp", "vec", "wlk"), None, None), P(("grp", "vec", "wlk"))),
        check_vma=False,
    )
```

time: 23.7 us -> 23.5 us (level)
  waiting for transfers between devices: 4.47 us -> 1.84 us
  Pallas kernels: 3.21 us -> 4.29 us
  local copies, waits for them, and re-layouts: 0.24 us -> 1.21 us
  starting transfers between devices: 7.39 us -> 7.68 us
    ppermute x3 -> x4, waiting for transfers between devices: 3.21 us -> 1.83 us  [swap(): return lax.ppermute(array, axis, [(i, partner(i)) for i in range(size)])]
    ppermute x1, waiting for transfers between devices: 1.27 us -> 0.01 us  [local(): lax.ppermute(mine, ('vec', 'wlk'), [((v ^ 2 * m + k % 2) * wlk_size + k,...]
    pallas_call x8 -> x7, Pallas kernels: 1.63 us -> 2.71 us  [the longest x3 2.58 us: partial_gradient(): call(functools.partial(gradient_kernel, norm_scale, len(chols)), jax.Shap...]
    unnamed x7, local copies, waits for them, and re-layouts: 0.22 us -> 1.2 us
    ppermute x3 -> x4, starting transfers between devices: 3.29 us -> 3.58 us  [swap(): return lax.ppermute(array, axis, [(i, partner(i)) for i in range(size)])]
  transfers between devices with their start and end apart: 4 -> 5, of which waited for: 3 -> 2; matrix products, arithmetic and copies ran while one was open for 1% -> 1% of each run, Pallas kernels for 4% -> 9%
where the time goes in v5:
time: 23.5 us; the launch traced here: 23.3 us
  starting transfers between devices  7.68 us (33%)
  blocking collectives  6.23 us (27%)
  Pallas kernels  4.29 us (18%)
  between operations  2.02 us (9%)
  waiting for transfers between devices  1.84 us (8%)
  local copies, waits for them, and re-layouts  1.21 us (5%)
    all_gather x1, blocking collectives, local(): row = lax.all_gather(payload, 'wlk', axis=0)  6.23 us
    ppermute x1, starting transfers between devices, local(): lax.ppermute(mine, ('vec', 'wlk'), [((v ^ 2 * m + k % 2) * wlk_size + k,...  4.1 us
    ppermute x4, starting transfers between devices, swap(): return lax.ppermute(array, axis, [(i, partner(i)) for i in range(size)])  3.58 us
    pallas_call x3, Pallas kernels, partial_gradient(): call(functools.partial(gradient_kernel, norm_scale, len(chols)), jax.Shap...  2.58 us
    ppermute x4, waiting for transfers between devices, swap(): return lax.ppermute(array, axis, [(i, partner(i)) for i in range(size)])  1.83 us
    pallas_call x1, Pallas kernels, local(): call(final_kernel, (jax.ShapeDtypeStruct((occupied, basis), jnp.float32),...  1.58 us
    unnamed x7, local copies, waits for them, and re-layouts  1.2 us
  transfers between devices with their start and end apart: 5, of which 2 were waited for; matrix products, arithmetic and copies ran while one was open for 1% of the time, Pallas kernels for 9%

profile of v5, /device:TPU:0, one launch (start us, length us, event | category | flops | bytes accessed | tf_op | source)
XLA Modules:
  0.0 23.3 jit_solution(7090757072434661732)
XLA Ops:
  0.6 0.0 copy-start
  0.6 1.0 %copy-done = bf16[6,64,512]{2,1,0:T(8,128)(2,1)S(1)} copy-done((bf16[6,64,512]{2,1,0:T(8,128)(2,1)S(1)}, bf16[6,64,512]{2,1,0:T(8,128)(2,1)}, u32[]{:S(2)}) %copy-start) | copy-done | bytes 393240
  1.6 0.0 copy-start.1
  1.7 4.1 %collective-permute-start = (bf16[3,64,512]{2,1,0:T(8,128)(2,1)S(1)}, bf16[3,64,512]{2,1,0:T(8,128)(2,1)S(1)}, u32[]{:S(2)}, u32[]{:S(2)}) collective-permute-start(bf16[3,64,512]{2,1,0:T(8,128)(2,1)S(1)} %get-tuple-element.12.refs_0_), channel_id=1, source_target_pairs={{8,0},{13,1},{10,2},{15,3},{12,4},{9,5},{14,6},{11,7},{0,8},{5,9},... | collective-permute-start | bytes 589832 | tf_op jit(solution)/shard_map/ppermute | solution.py:189
  5.8 1.6 %collective-permute-start.1 = (bf16[2,64,512]{2,1,0:T(8,128)(2,1)S(1)}, bf16[2,64,512]{2,1,0:T(8,128)(2,1)S(1)}, u32[]{:S(2)}, u32[]{:S(2)}) collective-permute-start(bf16[2,64,512]{2,1,0:T(8,128)(2,1)S(1)} %get-tuple-element.13), channel_id=1, source_target_pairs={{0,4},{4,0},{8,12},{12,8},{1,5},{5,1},{9,13},{13,9},{2,6},{6,2},{1... | collective-permute-start | bytes 393224 | tf_op jit(solution)/shard_map/ppermute | solution.py:39
  8.6 0.0 copy-done.1
  8.7 0.0 copy-start.2
  8.7 6.2 %all-gather = bf16[320,512]{1,0:T(8,128)(2,1)S(1)} all-gather(bf16[80,512]{1,0:T(8,128)(2,1)S(1)} %shard_map.70), channel_id=2, replica_groups=mesh['grp'=2,'vec'=4,'wlk'=4] {'wlk'}, dimensions={0}, use_global_device_ids=true | all-gather | bytes 409600 | tf_op jit(solution)/shard_map/all_gather | solution.py:214
  14.9 0.1 shard_map.71
  15.0 0.0 collective-permute-done.1.refs_1_
  15.0 0.0 collective-permute-done.refs_2_
  15.0 0.4 %collective-permute-start.3 = (bf16[3,64,512]{2,1,0:T(8,128)(2,1)S(1)}, bf16[3,64,512]{2,1,0:T(8,128)(2,1)S(1)}, u32[]{:S(2)}, u32[]{:S(2)}) collective-permute-start(bf16[3,64,512]{2,1,0:T(8,128)(2,1)S(1)} %collective-permute-done.refs_2_), channel_id=1, source_target_pairs={{0,1},{1,0},{2,3},{3,2},{4,5},{5,4},{6,7},{7,6},{8,9},{9,8},{10,11... | collective-permute-start | bytes 589832 | tf_op jit(solution)/shard_map/ppermute | solution.py:39
  15.5 0.2 collective-permute-start.2
  15.6 0.9 %shard_map.73.refs_2_ = f32[64,512]{1,0:T(8,128)S(1)} custom-call(bf16[64,512]{1,0:T(8,128)(2,1)S(1)} %get-tuple-element.19.theta_ref, bf16[3,64,512]{2,1,0:T(8,128)(2,1)S(1)} %get-tuple-element.12.refs_0_, bf16[2,64,512]{2,1,0:T(8,128)(2,1)S(1)} %collective-permute-done.1.refs_1_, bf16[3,64,512]{2,1,0:T(8,128)(2,1)S(1)} %collective-permute-done.refs_2_), custom_call_target="tpu_custom_call" | custom-call | tf_op jit(solution)/shard_map/pallas_call | solution.py:127
  16.5 0.2 collective-permute-done.2.refs_3_.refs_0_
  16.7 0.0 collective-permute-done.3.refs_4_.refs_1_
  16.7 0.6 %shard_map.74 = bf16[64,512]{1,0:T(8,128)(2,1)S(1)} custom-call(bf16[64,512]{1,0:T(8,128)(2,1)S(1)} %get-tuple-element.19.theta_ref, bf16[1,64,512]{2,1,0:T(8,128)(2,1)S(1)} %collective-permute-done.2.refs_3_.refs_0_, bf16[3,64,512]{2,1,0:T(8,128)(2,1)S(1)} %collective-permute-done.3.refs_4_.refs_1_, f32[64,512]{1,0:T(8,128)S(1)} %shard_map.73.refs_2_), custom_call_target="tpu_custom_call" | custom-call | tf_op jit(solution)/shard_map/pallas_call | solution.py:127
  17.3 1.4 %collective-permute-start.4 = (bf16[64,512]{1,0:T(8,128)(2,1)S(1)}, bf16[64,512]{1,0:T(8,128)(2,1)S(1)}, u32[]{:S(2)}, u32[]{:S(2)}) collective-permute-start(bf16[64,512]{1,0:T(8,128)(2,1)S(1)} %shard_map.74), channel_id=1, source_target_pairs={{0,2},{1,3},{2,0},{3,1},{4,6},{5,7},{6,4},{7,5},{8,10},{9,11},{10,... | collective-permute-start | bytes 196616 | tf_op jit(solution)/shard_map/ppermute | solution.py:39
  18.8 0.0 copy-done.2
  18.8 0.2 copy.7
  19.0 1.1 %shard_map.72.own_ref = f32[64,512]{1,0:T(8,128)S(1)} custom-call(bf16[64,512]{1,0:T(8,128)(2,1)S(1)} %get-tuple-element.15.theta_ref, bf16[3,64,512]{2,1,0:T(8,128)(2,1)S(1)} %get-tuple-element.12.refs_0_, bf16[2,64,512]{2,1,0:T(8,128)(2,1)S(1)} %collective-permute-done.1.refs_1_, bf16[3,64,512]{2,1,0:T(8,128)(2,1)S(1)} %collective-permute-done.refs_2_, ...), custom_call_target="tpu_custom_call" | custom-call | tf_op jit(solution)/shard_map/pallas_call | solution.py:127
  20.1 1.6 %collective-permute-done.4.other_ref = bf16[64,512]{1,0:T(8,128)(2,1)S(1)} collective-permute-done((bf16[64,512]{1,0:T(8,128)(2,1)S(1)}, bf16[64,512]{1,0:T(8,128)(2,1)S(1)}, u32[]{:S(2)}, u32[]{:S(2)}) %collective-permute-start.4) | collective-permute-done | bytes 65568 | tf_op jit(solution)/shard_map/ppermute | solution.py:39
  21.7 1.6 %shard_map.75 = (f32[64,512]{1,0:T(8,128)}, f32[1]{0:T(128)}) custom-call(bf16[64,512]{1,0:T(8,128)(2,1)S(1)} %get-tuple-element.15.theta_ref, bf16[16,512]{1,0:T(8,128)(2,1)S(1)} %get-tuple-element.16.extra_ref, f32[64,512]{1,0:T(8,128)S(1)} %shard_map.72.own_ref, bf16[64,512]{1,0:T(8,128)(2,1)S(1)} %collective-permute-done.4.other_ref, ...), custom_call_target="tpu_custom_call" | custom-call | tf_op jit(solution)/shard_map/pallas_call | solution.py:236
  (4 shorter events, 0.1 us)
Async XLA Ops:
  0.6 1.0 %copy-start = (bf16[6,64,512]{2,1,0:T(8,128)(2,1)S(1)}, bf16[6,64,512]{2,1,0:T(8,128)(2,1)}, u32[]{:S(2)}) copy-start(bf16[6,64,512]{2,1,0:T(8,128)(2,1)} %chol_ref.1) | copy-start | bytes 1179652
  1.6 7.0 %copy-start.1 = (f32[1,64,512]{2,1,0:T(8,128)S(1)}, f32[1,64,512]{2,1,0:T(8,128)}, u32[]{:S(2)}) copy-start(f32[1,64,512]{2,1,0:T(8,128)} %orbitals_ref.1) | copy-start | bytes 393220
  1.7 13.4 %collective-permute-start = (bf16[3,64,512]{2,1,0:T(8,128)(2,1)S(1)}, bf16[3,64,512]{2,1,0:T(8,128)(2,1)S(1)}, u32[]{:S(2)}, u32[]{:S(2)}) collective-permute-start(bf16[3,64,512]{2,1,0:T(8,128)(2,1)S(1)} %get-tuple-element.12.refs_0_), channel_id=1, source_target_pairs={{8,0},{13,1},{10,2},{15,3},{12,4},{9,5},{14,6},{11,7},{0,8},{5,9},... | collective-permute-start | bytes 589832 | tf_op jit(solution)/shard_map/ppermute | solution.py:189
  5.8 9.3 %collective-permute-start.1 = (bf16[2,64,512]{2,1,0:T(8,128)(2,1)S(1)}, bf16[2,64,512]{2,1,0:T(8,128)(2,1)S(1)}, u32[]{:S(2)}, u32[]{:S(2)}) collective-permute-start(bf16[2,64,512]{2,1,0:T(8,128)(2,1)S(1)} %get-tuple-element.13), channel_id=1, source_target_pairs={{0,4},{4,0},{8,12},{12,8},{1,5},{5,1},{9,13},{13,9},{2,6},{6,2},{1... | collective-permute-start | bytes 393224 | tf_op jit(solution)/shard_map/ppermute | solution.py:39
  8.7 10.1 %copy-start.2 = (f32[512,512]{1,0:T(8,128)S(1)}, f32[512,512]{1,0:T(8,128)}, u32[]{:S(2)}) copy-start(f32[512,512]{1,0:T(8,128)} %param.9) | copy-start | bytes 3145732
  15.0 1.7 %collective-permute-start.3 = (bf16[3,64,512]{2,1,0:T(8,128)(2,1)S(1)}, bf16[3,64,512]{2,1,0:T(8,128)(2,1)S(1)}, u32[]{:S(2)}, u32[]{:S(2)}) collective-permute-start(bf16[3,64,512]{2,1,0:T(8,128)(2,1)S(1)} %collective-permute-done.refs_2_), channel_id=1, source_target_pairs={{0,1},{1,0},{2,3},{3,2},{4,5},{5,4},{6,7},{7,6},{8,9},{9,8},{10,11... | collective-permute-start | bytes 589832 | tf_op jit(solution)/shard_map/ppermute | solution.py:39
  15.5 1.3 %collective-permute-start.2 = (bf16[1,64,512]{2,1,0:T(8,128)(2,1)S(1)}, bf16[1,64,512]{2,1,0:T(8,128)(2,1)S(1)}, u32[]{:S(2)}, u32[]{:S(2)}) collective-permute-start(bf16[1,64,512]{2,1,0:T(8,128)(2,1)S(1)} %constant_dynamic-slice_fusion), channel_id=1, source_target_pairs={{0,1},{1,0},{2,3},{3,2},{4,5},{5,4},{6,7},{7,6},{8,9},{9,8},{10,11... | collective-permute-start | bytes 196616 | tf_op jit(solution)/shard_map/ppermute | solution.py:39
  17.3 4.3 %collective-permute-start.4 = (bf16[64,512]{1,0:T(8,128)(2,1)S(1)}, bf16[64,512]{1,0:T(8,128)(2,1)S(1)}, u32[]{:S(2)}, u32[]{:S(2)}) collective-permute-start(bf16[64,512]{1,0:T(8,128)(2,1)S(1)} %shard_map.74), channel_id=1, source_target_pairs={{0,2},{1,3},{2,0},{3,1},{4,6},{5,7},{6,4},{7,5},{8,10},{9,11},{10,... | collective-permute-start | bytes 196616 | tf_op jit(solution)/shard_map/ppermute | solution.py:39

commit v6 on v5

--- a/solution.py
+++ b/solution.py
@@ -39,7 +39,7 @@
     return lax.ppermute(array, axis, [(i, partner(i)) for i in range(size)])
 
 
-def half_kernel(chol_ref, mine_ref, pair_ref):
+def half_kernel(parent_ref, chol_ref, mine_ref, pair_ref):
     half, pair = mine_ref.shape[0], pair_ref.shape[0]
     here = lax.axis_index("wlk")
     first = lax.rem(here // 2, 2) * half
@@ -47,22 +47,26 @@
     pair_ref[...] = chol_ref[pl.ds(first + lax.rem(here, 2) * (half - pair), pair)]
 
 
-def tile_kernel(log_ref, parent_ref, out_ref):
-    rows = lax.broadcasted_iota(jnp.int32, out_ref.shape, 0)
-    value = jnp.full(out_ref.shape, log_ref[0])
+def blank_kernel(out_ref):
+    out_ref[...] = jnp.zeros(out_ref.shape, out_ref.dtype)
+
+
+def parent_kernel(parent_ref, blank_ref, out_ref):
+    out_ref[...] = blank_ref[...] + parent_ref[0].astype(jnp.float32)
+
+
+def payload_kernel(log_ref, parent_ref, orbitals_ref, payload_ref):
+    occupied, basis = orbitals_ref.shape[1:]
+    payload_ref[:occupied, :] = orbitals_ref[0].astype(jnp.bfloat16)
+    rows = lax.broadcasted_iota(jnp.int32, (EXTRA, basis), 0)
+    value = jnp.full((EXTRA, basis), log_ref[0])
     high = value.astype(jnp.bfloat16).astype(jnp.float32)
     middle = (value - high).astype(jnp.bfloat16).astype(jnp.float32)
     low = value - high - middle
-    parent = parent_ref[0].astype(jnp.float32)
-    out_ref[...] = jnp.where(
+    parent = jnp.broadcast_to(parent_ref[:1, :1], value.shape)
+    payload_ref[occupied:, :] = jnp.where(
         rows == 0, high, jnp.where(rows == 1, middle, jnp.where(rows == 2, low, parent))
     ).astype(jnp.bfloat16)
-
-
-def payload_kernel(tile_ref, orbitals_ref, payload_ref):
-    occupied = orbitals_ref.shape[1]
-    payload_ref[:occupied, :] = orbitals_ref[0].astype(jnp.bfloat16)
-    payload_ref[occupied:, :] = tile_ref[...]
 
 
 def select_kernel(row_ref, theta_ref, extra_ref, other_ref):
@@ -91,33 +95,20 @@
     rows = lax.broadcasted_iota(jnp.int32, (occupied, occupied), 0)
     columns = lax.broadcasted_iota(jnp.int32, (occupied, occupied), 1)
     diagonal = rows == columns
-    turned = [
-        lax.dot_general(
-            ref[...].reshape(-1, basis), theta, (((1,), (1,)), ((), ())),
-            preferred_element_type=jnp.float32,
-        )
-        for ref in chol_refs
-    ]
-    place = 0
-    for product in turned:
-        product = product.astype(jnp.bfloat16).astype(jnp.float32)
-        for g in range(product.shape[0] // occupied):
-            block = product[g * occupied : (g + 1) * occupied, :]
-            on_diagonal = jnp.where(diagonal, block, 0.0)
-            trace = jnp.sum(jnp.sum(on_diagonal, axis=0, keepdims=True), axis=1, keepdims=True)
-            piece = norm_scale * (jnp.where(diagonal, trace, 0.0) - block)
-            adjoint[:, place : place + occupied] = piece.astype(jnp.bfloat16)
-            place += occupied
-    total = sum_refs[0][...] if sum_refs else None
-    place = 0
-    for ref in chol_refs:
-        width = ref.shape[0] * occupied
-        term = jnp.dot(
-            adjoint[:, place : place + width], ref[...].reshape(-1, basis),
-            preferred_element_type=jnp.float32,
-        )
-        total = term if total is None else total + term
-        place += width
+    chol = jnp.concatenate([ref[...].reshape(-1, basis) for ref in chol_refs], axis=0)
+    turned = lax.dot_general(
+        chol, theta, (((1,), (1,)), ((), ())), preferred_element_type=jnp.float32
+    )
+    turned = turned.astype(jnp.bfloat16).astype(jnp.float32)
+    for place in range(0, chol.shape[0], occupied):
+        block = turned[place : place + occupied, :]
+        on_diagonal = jnp.where(diagonal, block, 0.0)
+        trace = jnp.sum(jnp.sum(on_diagonal, axis=0, keepdims=True), axis=1, keepdims=True)
+        piece = norm_scale * (jnp.where(diagonal, trace, 0.0) - block)
+        adjoint[:, place : place + occupied] = piece.astype(jnp.bfloat16)
+    total = jnp.dot(adjoint[...], chol, preferred_element_type=jnp.float32)
+    if sum_refs:
+        total = total + sum_refs[0][...]
     out_ref[...] = total.astype(out_ref.dtype)
 
 
@@ -176,15 +167,29 @@
     pair = (half + 1) // 2
     smem = pl.BlockSpec(memory_space=pltpu.SMEM)
 
+    blank = call(
+        blank_kernel,
+        jax.ShapeDtypeStruct((8, 128), jnp.float32),
+        [],
+        vmem(1)[0],
+        (),
+        pl.CostEstimate(flops=10**11, bytes_accessed=256 * 2**20, transcendentals=0),
+    )()
+    parent = call(
+        parent_kernel,
+        jax.ShapeDtypeStruct((8, 128), jnp.float32),
+        [smem] + vmem(1),
+        vmem(1)[0],
+    )(parents, blank)
     mine, part = call(
         half_kernel,
         (
             jax.ShapeDtypeStruct((half, occupied, basis), cholesky.dtype),
             jax.ShapeDtypeStruct((pair, occupied, basis), cholesky.dtype),
         ),
-        vmem(1),
         vmem(2),
-    )(cholesky)
+        vmem(2),
+    )(parent, cholesky)
     far = [
         lax.ppermute(
             mine,
@@ -199,18 +204,12 @@
     ]
     near = swap(part, "vec", lambda i: i ^ 1)
 
-    tile = call(
-        tile_kernel,
-        jax.ShapeDtypeStruct((EXTRA, basis), jnp.bfloat16),
-        [smem] * 2,
-        vmem(1)[0],
-    )(log_weights, parents)
     payload = call(
         payload_kernel,
         jax.ShapeDtypeStruct((occupied + EXTRA, basis), jnp.bfloat16),
-        vmem(2),
+        [smem] + vmem(2),
         vmem(1)[0],
-    )(tile, orbitals)
+    )(log_weights, parent, orbitals)
     row = lax.all_gather(payload, "wlk", axis=0)
     chosen, chosen_extra, neighbour = call(
         select_kernel,
@@ -227,7 +226,7 @@
     lacking = half - pair
     sent = lax.dynamic_slice_in_dim(near, lax.axis_index("wlk") % 2 * (pair - lacking), lacking, 0)
     vectors = [mine, near, *far]
-    other = [swap(c, "wlk", lambda i: i ^ 1) for c in (sent, *far)]
+    other = [swap(jnp.concatenate([sent, *far], axis=0), "wlk", lambda i: i ^ 1)]
     to_send = partial_gradient(norm_scale, neighbour, vectors, jnp.float32)
     to_send = partial_gradient(norm_scale, neighbour, other, jnp.bfloat16, to_send)
     received = swap(to_send, "wlk", lambda i: i ^ 2)

time: 23.5 us -> 23.3 us (level)
  waiting for transfers between devices: 1.84 us -> 3.31 us
  local copies, waits for them, and re-layouts: 1.21 us -> 0.5 us
  Pallas kernels: 4.29 us -> 3.85 us
  starting transfers between devices: 7.68 us -> 7.31 us
    ppermute x1, waiting for transfers between devices: 0.01 us -> 0.78 us  [local(): lax.ppermute(mine, ('vec', 'wlk'), [((v ^ 2 * m + k % 2) * wlk_size + k,...]
    unnamed x7, local copies, waits for them, and re-layouts: 1.2 us -> 0.5 us
    ppermute x4 -> x3, waiting for transfers between devices: 1.83 us -> 2.53 us  [swap(): return lax.ppermute(array, axis, [(i, partner(i)) for i in range(size)])]
    pallas_call x3, Pallas kernels: 2.58 us -> 2.11 us  [partial_gradient(): call(functools.partial(gradient_kernel, norm_scale, len(chols)), jax.Shap...]
    ppermute x4 -> x3, starting transfers between devices: 3.58 us -> 3.2 us  [swap(): return lax.ppermute(array, axis, [(i, partner(i)) for i in range(size)])]
  transfers between devices with their start and end apart: 5 -> 4, of which waited for: 2 -> 3; matrix products, arithmetic and copies ran while one was open for 1% -> 1% of each run, Pallas kernels for 9% -> 7%
where the time goes in v6:
time: 23.3 us; the launch traced here: 23.2 us
  starting transfers between devices  7.31 us (31%)
  blocking collectives  6.1 us (26%)
  Pallas kernels  3.85 us (17%)
  waiting for transfers between devices  3.31 us (14%)
  between operations  2.08 us (9%)
  local copies, waits for them, and re-layouts  0.5 us (2%)
    all_gather x1, blocking collectives, local(): row = lax.all_gather(payload, 'wlk', axis=0)  6.1 us
    ppermute x1, starting transfers between devices, local(): lax.ppermute(mine, ('vec', 'wlk'), [((v ^ 2 * m + k % 2) * wlk_size + k,...  4.1 us
    ppermute x3, starting transfers between devices, swap(): return lax.ppermute(array, axis, [(i, partner(i)) for i in range(size)])  3.2 us
    ppermute x3, waiting for transfers between devices, swap(): return lax.ppermute(array, axis, [(i, partner(i)) for i in range(size)])  2.53 us
    pallas_call x3, Pallas kernels, partial_gradient(): call(functools.partial(gradient_kernel, norm_scale, len(chols)), jax.Shap...  2.11 us
    pallas_call x1, Pallas kernels, local(): call(final_kernel, (jax.ShapeDtypeStruct((occupied, basis), jnp.float32),...  1.58 us
    ppermute x1, waiting for transfers between devices, local(): lax.ppermute(mine, ('vec', 'wlk'), [((v ^ 2 * m + k % 2) * wlk_size + k,...  0.78 us
    unnamed x7, local copies, waits for them, and re-layouts  0.5 us
  transfers between devices with their start and end apart: 4, of which 3 were waited for; matrix products, arithmetic and copies ran while one was open for 1% of the time, Pallas kernels for 7%

profile of v6, /device:TPU:0, one launch (start us, length us, event | category | flops | bytes accessed | tf_op | source)
XLA Modules:
  0.0 23.2 jit_solution(6020993724046500514)
XLA Ops:
  0.6 0.0 copy-start
  1.4 0.3 %copy-done = bf16[6,64,512]{2,1,0:T(8,128)(2,1)S(1)} copy-done((bf16[6,64,512]{2,1,0:T(8,128)(2,1)S(1)}, bf16[6,64,512]{2,1,0:T(8,128)(2,1)}, u32[]{:S(2)}) %copy-start) | copy-done | bytes 393240
  1.6 0.0 copy-start.1
  1.7 4.1 %collective-permute-start = (bf16[3,64,512]{2,1,0:T(8,128)(2,1)S(1)}, bf16[3,64,512]{2,1,0:T(8,128)(2,1)S(1)}, u32[]{:S(2)}, u32[]{:S(2)}) collective-permute-start(bf16[3,64,512]{2,1,0:T(8,128)(2,1)S(1)} %get-tuple-element.12.refs_0_), channel_id=1, source_target_pairs={{8,0},{13,1},{10,2},{15,3},{12,4},{9,5},{14,6},{11,7},{0,8},{5,9},... | collective-permute-start | bytes 589832 | tf_op jit(solution)/shard_map/ppermute | solution.py:194
  5.8 1.6 %collective-permute-start.1 = (bf16[2,64,512]{2,1,0:T(8,128)(2,1)S(1)}, bf16[2,64,512]{2,1,0:T(8,128)(2,1)S(1)}, u32[]{:S(2)}, u32[]{:S(2)}) collective-permute-start(bf16[2,64,512]{2,1,0:T(8,128)(2,1)S(1)} %get-tuple-element.13), channel_id=1, source_target_pairs={{0,4},{4,0},{8,12},{12,8},{1,5},{5,1},{9,13},{13,9},{2,6},{6,2},{1... | collective-permute-start | bytes 393224 | tf_op jit(solution)/shard_map/ppermute | solution.py:39
  8.0 0.0 copy-done.1
  8.1 6.1 %all-gather = bf16[320,512]{1,0:T(8,128)(2,1)S(1)} all-gather(bf16[80,512]{1,0:T(8,128)(2,1)S(1)} %shard_map.71), channel_id=2, replica_groups=mesh['grp'=2,'vec'=4,'wlk'=4] {'wlk'}, dimensions={0}, use_global_device_ids=true | all-gather | bytes 409600 | tf_op jit(solution)/shard_map/all_gather | solution.py:213
  14.2 0.0 copy-start.2
  14.2 0.1 shard_map.72
  14.3 0.0 collective-permute-done.1.refs_1_
  14.3 0.8 %collective-permute-done.refs_2_ = bf16[3,64,512]{2,1,0:T(8,128)(2,1)S(1)} collective-permute-done((bf16[3,64,512]{2,1,0:T(8,128)(2,1)S(1)}, bf16[3,64,512]{2,1,0:T(8,128)(2,1)S(1)}, u32[]{:S(2)}, u32[]{:S(2)}) %collective-permute-start) | collective-permute-done | bytes 196640 | tf_op jit(solution)/shard_map/ppermute | solution.py:194
  15.1 0.1 collective-permute-start.2
  15.2 0.7 %shard_map.74.refs_1_ = f32[64,512]{1,0:T(8,128)S(1)} custom-call(bf16[64,512]{1,0:T(8,128)(2,1)S(1)} %get-tuple-element.19.theta_ref, bf16[3,64,512]{2,1,0:T(8,128)(2,1)S(1)} %get-tuple-element.12.refs_0_, bf16[2,64,512]{2,1,0:T(8,128)(2,1)S(1)} %collective-permute-done.1.refs_1_, bf16[3,64,512]{2,1,0:T(8,128)(2,1)S(1)} %collective-permute-done.refs_2_), custom_call_target="tpu_custom_call" | custom-call | tf_op jit(solution)/shard_map/pallas_call | solution.py:118
  15.9 0.8 %collective-permute-done.2.refs_3_.refs_0_ = bf16[4,64,512]{2,1,0:T(8,128)(2,1)S(1)} collective-permute-done((bf16[4,64,512]{2,1,0:T(8,128)(2,1)S(1)}, bf16[4,64,512]{2,1,0:T(8,128)(2,1)S(1)}, u32[]{:S(2)}, u32[]{:S(2)}) %collective-permute-start.2) | collective-permute-done | bytes 262176 | tf_op jit(solution)/shard_map/ppermute | solution.py:39
  16.7 0.6 %shard_map.75 = bf16[64,512]{1,0:T(8,128)(2,1)S(1)} custom-call(bf16[64,512]{1,0:T(8,128)(2,1)S(1)} %get-tuple-element.19.theta_ref, bf16[4,64,512]{2,1,0:T(8,128)(2,1)S(1)} %collective-permute-done.2.refs_3_.refs_0_, f32[64,512]{1,0:T(8,128)S(1)} %shard_map.74.refs_1_), custom_call_target="tpu_custom_call" | custom-call | tf_op jit(solution)/shard_map/pallas_call | solution.py:118
  17.3 1.6 %collective-permute-start.3 = (bf16[64,512]{1,0:T(8,128)(2,1)S(1)}, bf16[64,512]{1,0:T(8,128)(2,1)S(1)}, u32[]{:S(2)}, u32[]{:S(2)}) collective-permute-start(bf16[64,512]{1,0:T(8,128)(2,1)S(1)} %shard_map.75), channel_id=1, source_target_pairs={{0,2},{1,3},{2,0},{3,1},{4,6},{5,7},{6,4},{7,5},{8,10},{9,11},{10,... | collective-permute-start | bytes 196616 | tf_op jit(solution)/shard_map/ppermute | solution.py:39
  18.8 0.0 copy-done.2
  18.8 0.2 copy.7
  19.0 0.8 %shard_map.73.own_ref = f32[64,512]{1,0:T(8,128)S(1)} custom-call(bf16[64,512]{1,0:T(8,128)(2,1)S(1)} %get-tuple-element.15.theta_ref, bf16[3,64,512]{2,1,0:T(8,128)(2,1)S(1)} %get-tuple-element.12.refs_0_, bf16[2,64,512]{2,1,0:T(8,128)(2,1)S(1)} %collective-permute-done.1.refs_1_, bf16[3,64,512]{2,1,0:T(8,128)(2,1)S(1)} %collective-permute-done.refs_2_, ...), custom_call_target="tpu_custom_call" | custom-call | tf_op jit(solution)/shard_map/pallas_call | solution.py:118
  19.9 1.7 %collective-permute-done.3.other_ref = bf16[64,512]{1,0:T(8,128)(2,1)S(1)} collective-permute-done((bf16[64,512]{1,0:T(8,128)(2,1)S(1)}, bf16[64,512]{1,0:T(8,128)(2,1)S(1)}, u32[]{:S(2)}, u32[]{:S(2)}) %collective-permute-start.3) | collective-permute-done | bytes 65568 | tf_op jit(solution)/shard_map/ppermute | solution.py:39
  21.6 1.6 %shard_map.76 = (f32[64,512]{1,0:T(8,128)}, f32[1]{0:T(128)}) custom-call(bf16[64,512]{1,0:T(8,128)(2,1)S(1)} %get-tuple-element.15.theta_ref, bf16[16,512]{1,0:T(8,128)(2,1)S(1)} %get-tuple-element.16.extra_ref, f32[64,512]{1,0:T(8,128)S(1)} %shard_map.73.own_ref, bf16[64,512]{1,0:T(8,128)(2,1)S(1)} %collective-permute-done.3.other_ref, ...), custom_call_target="tpu_custom_call" | custom-call | tf_op jit(solution)/shard_map/pallas_call | solution.py:235
  (6 shorter events, 0.1 us)
Async XLA Ops:
  0.6 1.0 %copy-start = (bf16[6,64,512]{2,1,0:T(8,128)(2,1)S(1)}, bf16[6,64,512]{2,1,0:T(8,128)(2,1)}, u32[]{:S(2)}) copy-start(bf16[6,64,512]{2,1,0:T(8,128)(2,1)} %chol_ref.1) | copy-start | bytes 1179652
  1.6 6.4 %copy-start.1 = (f32[1,64,512]{2,1,0:T(8,128)S(1)}, f32[1,64,512]{2,1,0:T(8,128)}, u32[]{:S(2)}) copy-start(f32[1,64,512]{2,1,0:T(8,128)} %orbitals_ref.1) | copy-start | bytes 393220
  1.7 13.4 %collective-permute-start = (bf16[3,64,512]{2,1,0:T(8,128)(2,1)S(1)}, bf16[3,64,512]{2,1,0:T(8,128)(2,1)S(1)}, u32[]{:S(2)}, u32[]{:S(2)}) collective-permute-start(bf16[3,64,512]{2,1,0:T(8,128)(2,1)S(1)} %get-tuple-element.12.refs_0_), channel_id=1, source_target_pairs={{8,0},{13,1},{10,2},{15,3},{12,4},{9,5},{14,6},{11,7},{0,8},{5,9},... | collective-permute-start | bytes 589832 | tf_op jit(solution)/shard_map/ppermute | solution.py:194
  5.8 8.5 %collective-permute-start.1 = (bf16[2,64,512]{2,1,0:T(8,128)(2,1)S(1)}, bf16[2,64,512]{2,1,0:T(8,128)(2,1)S(1)}, u32[]{:S(2)}, u32[]{:S(2)}) collective-permute-start(bf16[2,64,512]{2,1,0:T(8,128)(2,1)S(1)} %get-tuple-element.13), channel_id=1, source_target_pairs={{0,4},{4,0},{8,12},{12,8},{1,5},{5,1},{9,13},{13,9},{2,6},{6,2},{1... | collective-permute-start | bytes 393224 | tf_op jit(solution)/shard_map/ppermute | solution.py:39
  14.2 4.7 %copy-start.2 = (f32[512,512]{1,0:T(8,128)S(1)}, f32[512,512]{1,0:T(8,128)}, u32[]{:S(2)}) copy-start(f32[512,512]{1,0:T(8,128)} %param.9) | copy-start | bytes 3145732
  15.1 1.6 %collective-permute-start.2 = (bf16[4,64,512]{2,1,0:T(8,128)(2,1)S(1)}, bf16[4,64,512]{2,1,0:T(8,128)(2,1)S(1)}, u32[]{:S(2)}, u32[]{:S(2)}) collective-permute-start(bf16[4,64,512]{2,1,0:T(8,128)(2,1)S(1)} %pad_maximum_fusion), channel_id=1, source_target_pairs={{0,1},{1,0},{2,3},{3,2},{4,5},{5,4},{6,7},{7,6},{8,9},{9,8},{10,11... | collective-permute-start | bytes 786440 | tf_op jit(solution)/shard_map/ppermute | solution.py:39
  17.3 4.3 %collective-permute-start.3 = (bf16[64,512]{1,0:T(8,128)(2,1)S(1)}, bf16[64,512]{1,0:T(8,128)(2,1)S(1)}, u32[]{:S(2)}, u32[]{:S(2)}) collective-permute-start(bf16[64,512]{1,0:T(8,128)(2,1)S(1)} %shard_map.75), channel_id=1, source_target_pairs={{0,2},{1,3},{2,0},{3,1},{4,6},{5,7},{6,4},{7,5},{8,10},{9,11},{10,... | collective-permute-start | bytes 196616 | tf_op jit(solution)/shard_map/ppermute | solution.py:39

commit v7 on v6

--- a/solution.py
+++ b/solution.py
@@ -129,7 +129,7 @@
     theta = theta_ref[...].astype(jnp.float32)
     gradient = own_ref[...] + other_ref[...].astype(jnp.float32)
     energy = 0.5 * jnp.sum(theta * gradient)
-    log_weight = jnp.sum(extra_ref[:3, :1].astype(jnp.float32))
+    log_weight = jnp.sum(extra_ref[...].astype(jnp.float32)[:3, :1])
     log_ref[0] = log_weight - energy_step * energy
     stepped = (theta - gradient_step * gradient).astype(jnp.bfloat16)
     propagated = jnp.dot(stepped, propagator_ref[...], preferred_element_type=jnp.float32)

time: 23.3 us -> 23.3 us (level)
  no operation moved by 1% of the time
where the time goes in v7:
time: 23.3 us; the launch traced here: 23.2 us
  starting transfers between devices  7.31 us (31%)
  blocking collectives  6.1 us (26%)
  Pallas kernels  3.85 us (17%)
  waiting for transfers between devices  3.31 us (14%)
  between operations  2.08 us (9%)
  local copies, waits for them, and re-layouts  0.5 us (2%)
    all_gather x1, blocking collectives, local(): row = lax.all_gather(payload, 'wlk', axis=0)  6.1 us
    ppermute x1, starting transfers between devices, local(): lax.ppermute(mine, ('vec', 'wlk'), [((v ^ 2 * m + k % 2) * wlk_size + k,...  4.1 us
    ppermute x3, starting transfers between devices, swap(): return lax.ppermute(array, axis, [(i, partner(i)) for i in range(size)])  3.2 us
    ppermute x3, waiting for transfers between devices, swap(): return lax.ppermute(array, axis, [(i, partner(i)) for i in range(size)])  2.53 us
    pallas_call x3, Pallas kernels, partial_gradient(): call(functools.partial(gradient_kernel, norm_scale, len(chols)), jax.Shap...  2.11 us
    pallas_call x1, Pallas kernels, local(): call(final_kernel, (jax.ShapeDtypeStruct((occupied, basis), jnp.float32),...  1.58 us
    ppermute x1, waiting for transfers between devices, local(): lax.ppermute(mine, ('vec', 'wlk'), [((v ^ 2 * m + k % 2) * wlk_size + k,...  0.78 us
    unnamed x7, local copies, waits for them, and re-layouts  0.5 us
  transfers between devices with their start and end apart: 4, of which 3 were waited for; matrix products, arithmetic and copies ran while one was open for 1% of the time, Pallas kernels for 7%

profile of v7, /device:TPU:0, one launch (start us, length us, event | category | flops | bytes accessed | tf_op | source)
XLA Modules:
  0.0 23.2 jit_solution(15994174517351317979)
XLA Ops:
  0.6 0.0 copy-start
  1.4 0.3 %copy-done = bf16[6,64,512]{2,1,0:T(8,128)(2,1)S(1)} copy-done((bf16[6,64,512]{2,1,0:T(8,128)(2,1)S(1)}, bf16[6,64,512]{2,1,0:T(8,128)(2,1)}, u32[]{:S(2)}) %copy-start) | copy-done | bytes 393240
  1.6 0.0 copy-start.1
  1.7 4.1 %collective-permute-start = (bf16[3,64,512]{2,1,0:T(8,128)(2,1)S(1)}, bf16[3,64,512]{2,1,0:T(8,128)(2,1)S(1)}, u32[]{:S(2)}, u32[]{:S(2)}) collective-permute-start(bf16[3,64,512]{2,1,0:T(8,128)(2,1)S(1)} %get-tuple-element.12.refs_0_), channel_id=1, source_target_pairs={{8,0},{13,1},{10,2},{15,3},{12,4},{9,5},{14,6},{11,7},{0,8},{5,9},... | collective-permute-start | bytes 589832 | tf_op jit(solution)/shard_map/ppermute | solution.py:194
  5.8 1.6 %collective-permute-start.1 = (bf16[2,64,512]{2,1,0:T(8,128)(2,1)S(1)}, bf16[2,64,512]{2,1,0:T(8,128)(2,1)S(1)}, u32[]{:S(2)}, u32[]{:S(2)}) collective-permute-start(bf16[2,64,512]{2,1,0:T(8,128)(2,1)S(1)} %get-tuple-element.13), channel_id=1, source_target_pairs={{0,4},{4,0},{8,12},{12,8},{1,5},{5,1},{9,13},{13,9},{2,6},{6,2},{1... | collective-permute-start | bytes 393224 | tf_op jit(solution)/shard_map/ppermute | solution.py:39
  8.0 0.0 copy-done.1
  8.1 6.1 %all-gather = bf16[320,512]{1,0:T(8,128)(2,1)S(1)} all-gather(bf16[80,512]{1,0:T(8,128)(2,1)S(1)} %shard_map.71), channel_id=2, replica_groups=mesh['grp'=2,'vec'=4,'wlk'=4] {'wlk'}, dimensions={0}, use_global_device_ids=true | all-gather | bytes 409600 | tf_op jit(solution)/shard_map/all_gather | solution.py:213
  14.2 0.0 copy-start.2
  14.2 0.1 shard_map.72
  14.3 0.0 collective-permute-done.1.refs_1_
  14.3 0.8 %collective-permute-done.refs_2_ = bf16[3,64,512]{2,1,0:T(8,128)(2,1)S(1)} collective-permute-done((bf16[3,64,512]{2,1,0:T(8,128)(2,1)S(1)}, bf16[3,64,512]{2,1,0:T(8,128)(2,1)S(1)}, u32[]{:S(2)}, u32[]{:S(2)}) %collective-permute-start) | collective-permute-done | bytes 196640 | tf_op jit(solution)/shard_map/ppermute | solution.py:194
  15.1 0.1 collective-permute-start.2
  15.2 0.7 %shard_map.74.refs_1_ = f32[64,512]{1,0:T(8,128)S(1)} custom-call(bf16[64,512]{1,0:T(8,128)(2,1)S(1)} %get-tuple-element.19.theta_ref, bf16[3,64,512]{2,1,0:T(8,128)(2,1)S(1)} %get-tuple-element.12.refs_0_, bf16[2,64,512]{2,1,0:T(8,128)(2,1)S(1)} %collective-permute-done.1.refs_1_, bf16[3,64,512]{2,1,0:T(8,128)(2,1)S(1)} %collective-permute-done.refs_2_), custom_call_target="tpu_custom_call" | custom-call | tf_op jit(solution)/shard_map/pallas_call | solution.py:118
  15.9 0.8 %collective-permute-done.2.refs_3_.refs_0_ = bf16[4,64,512]{2,1,0:T(8,128)(2,1)S(1)} collective-permute-done((bf16[4,64,512]{2,1,0:T(8,128)(2,1)S(1)}, bf16[4,64,512]{2,1,0:T(8,128)(2,1)S(1)}, u32[]{:S(2)}, u32[]{:S(2)}) %collective-permute-start.2) | collective-permute-done | bytes 262176 | tf_op jit(solution)/shard_map/ppermute | solution.py:39
  16.7 0.6 %shard_map.75 = bf16[64,512]{1,0:T(8,128)(2,1)S(1)} custom-call(bf16[64,512]{1,0:T(8,128)(2,1)S(1)} %get-tuple-element.19.theta_ref, bf16[4,64,512]{2,1,0:T(8,128)(2,1)S(1)} %collective-permute-done.2.refs_3_.refs_0_, f32[64,512]{1,0:T(8,128)S(1)} %shard_map.74.refs_1_), custom_call_target="tpu_custom_call" | custom-call | tf_op jit(solution)/shard_map/pallas_call | solution.py:118
  17.3 1.6 %collective-permute-start.3 = (bf16[64,512]{1,0:T(8,128)(2,1)S(1)}, bf16[64,512]{1,0:T(8,128)(2,1)S(1)}, u32[]{:S(2)}, u32[]{:S(2)}) collective-permute-start(bf16[64,512]{1,0:T(8,128)(2,1)S(1)} %shard_map.75), channel_id=1, source_target_pairs={{0,2},{1,3},{2,0},{3,1},{4,6},{5,7},{6,4},{7,5},{8,10},{9,11},{10,... | collective-permute-start | bytes 196616 | tf_op jit(solution)/shard_map/ppermute | solution.py:39
  18.8 0.0 copy-done.2
  18.8 0.2 copy.7
  19.0 0.8 %shard_map.73.own_ref = f32[64,512]{1,0:T(8,128)S(1)} custom-call(bf16[64,512]{1,0:T(8,128)(2,1)S(1)} %get-tuple-element.15.theta_ref, bf16[3,64,512]{2,1,0:T(8,128)(2,1)S(1)} %get-tuple-element.12.refs_0_, bf16[2,64,512]{2,1,0:T(8,128)(2,1)S(1)} %collective-permute-done.1.refs_1_, bf16[3,64,512]{2,1,0:T(8,128)(2,1)S(1)} %collective-permute-done.refs_2_, ...), custom_call_target="tpu_custom_call" | custom-call | tf_op jit(solution)/shard_map/pallas_call | solution.py:118
  19.9 1.7 %collective-permute-done.3.other_ref = bf16[64,512]{1,0:T(8,128)(2,1)S(1)} collective-permute-done((bf16[64,512]{1,0:T(8,128)(2,1)S(1)}, bf16[64,512]{1,0:T(8,128)(2,1)S(1)}, u32[]{:S(2)}, u32[]{:S(2)}) %collective-permute-start.3) | collective-permute-done | bytes 65568 | tf_op jit(solution)/shard_map/ppermute | solution.py:39
  21.6 1.6 %shard_map.76 = (f32[64,512]{1,0:T(8,128)}, f32[1]{0:T(128)}) custom-call(bf16[64,512]{1,0:T(8,128)(2,1)S(1)} %get-tuple-element.15.theta_ref, bf16[16,512]{1,0:T(8,128)(2,1)S(1)} %get-tuple-element.16.extra_ref, f32[64,512]{1,0:T(8,128)S(1)} %shard_map.73.own_ref, bf16[64,512]{1,0:T(8,128)(2,1)S(1)} %collective-permute-done.3.other_ref, ...), custom_call_target="tpu_custom_call" | custom-call | tf_op jit(solution)/shard_map/pallas_call | solution.py:235
  (6 shorter events, 0.1 us)
Async XLA Ops:
  0.6 1.0 %copy-start = (bf16[6,64,512]{2,1,0:T(8,128)(2,1)S(1)}, bf16[6,64,512]{2,1,0:T(8,128)(2,1)}, u32[]{:S(2)}) copy-start(bf16[6,64,512]{2,1,0:T(8,128)(2,1)} %chol_ref.1) | copy-start | bytes 1179652
  1.6 6.4 %copy-start.1 = (f32[1,64,512]{2,1,0:T(8,128)S(1)}, f32[1,64,512]{2,1,0:T(8,128)}, u32[]{:S(2)}) copy-start(f32[1,64,512]{2,1,0:T(8,128)} %orbitals_ref.1) | copy-start | bytes 393220
  1.7 13.4 %collective-permute-start = (bf16[3,64,512]{2,1,0:T(8,128)(2,1)S(1)}, bf16[3,64,512]{2,1,0:T(8,128)(2,1)S(1)}, u32[]{:S(2)}, u32[]{:S(2)}) collective-permute-start(bf16[3,64,512]{2,1,0:T(8,128)(2,1)S(1)} %get-tuple-element.12.refs_0_), channel_id=1, source_target_pairs={{8,0},{13,1},{10,2},{15,3},{12,4},{9,5},{14,6},{11,7},{0,8},{5,9},... | collective-permute-start | bytes 589832 | tf_op jit(solution)/shard_map/ppermute | solution.py:194
  5.8 8.5 %collective-permute-start.1 = (bf16[2,64,512]{2,1,0:T(8,128)(2,1)S(1)}, bf16[2,64,512]{2,1,0:T(8,128)(2,1)S(1)}, u32[]{:S(2)}, u32[]{:S(2)}) collective-permute-start(bf16[2,64,512]{2,1,0:T(8,128)(2,1)S(1)} %get-tuple-element.13), channel_id=1, source_target_pairs={{0,4},{4,0},{8,12},{12,8},{1,5},{5,1},{9,13},{13,9},{2,6},{6,2},{1... | collective-permute-start | bytes 393224 | tf_op jit(solution)/shard_map/ppermute | solution.py:39
  14.2 4.7 %copy-start.2 = (f32[512,512]{1,0:T(8,128)S(1)}, f32[512,512]{1,0:T(8,128)}, u32[]{:S(2)}) copy-start(f32[512,512]{1,0:T(8,128)} %param.9) | copy-start | bytes 3145732
  15.1 1.6 %collective-permute-start.2 = (bf16[4,64,512]{2,1,0:T(8,128)(2,1)S(1)}, bf16[4,64,512]{2,1,0:T(8,128)(2,1)S(1)}, u32[]{:S(2)}, u32[]{:S(2)}) collective-permute-start(bf16[4,64,512]{2,1,0:T(8,128)(2,1)S(1)} %pad_maximum_fusion), channel_id=1, source_target_pairs={{0,1},{1,0},{2,3},{3,2},{4,5},{5,4},{6,7},{7,6},{8,9},{9,8},{10,11... | collective-permute-start | bytes 786440 | tf_op jit(solution)/shard_map/ppermute | solution.py:39
  17.3 4.3 %collective-permute-start.3 = (bf16[64,512]{1,0:T(8,128)(2,1)S(1)}, bf16[64,512]{1,0:T(8,128)(2,1)S(1)}, u32[]{:S(2)}, u32[]{:S(2)}) collective-permute-start(bf16[64,512]{1,0:T(8,128)(2,1)S(1)} %shard_map.75), channel_id=1, source_target_pairs={{0,2},{1,3},{2,0},{3,1},{4,6},{5,7},{6,4},{7,5},{8,10},{9,11},{10,... | collective-permute-start | bytes 196616 | tf_op jit(solution)/shard_map/ppermute | solution.py:39

commit v8 on v7

--- a/solution.py
+++ b/solution.py
@@ -195,7 +195,7 @@
             mine,
             ("vec", "wlk"),
             [
-                ((v ^ (2 * m + k % 2)) * wlk_size + k, v * wlk_size + k)
+                ((v ^ (2 * m + 1 - k % 2)) * wlk_size + k, v * wlk_size + k)
                 for v in range(vec_size)
                 for k in range(wlk_size)
             ],

time: 23.3 us -> 22.1 us (0.948)
  waiting for transfers between devices: 3.31 us -> 2.28 us
    ppermute x3, starting transfers between devices: 3.2 us -> 2.02 us  [swap(): return lax.ppermute(array, axis, [(i, partner(i)) for i in range(size)])]
    ppermute x1, starting transfers between devices: 4.1 us -> 5.11 us  [local(): lax.ppermute(mine, ('vec', 'wlk'), [((v ^ 2 * m + 1 - k % 2) * wlk_size +...]
    ppermute x1, waiting for transfers between devices: 0.78 us -> 0.01 us  [local(): lax.ppermute(mine, ('vec', 'wlk'), [((v ^ 2 * m + 1 - k % 2) * wlk_size +...]
    ppermute x3, waiting for transfers between devices: 2.53 us -> 2.28 us  [swap(): return lax.ppermute(array, axis, [(i, partner(i)) for i in range(size)])]
  transfers between devices with their start and end apart: 4 -> 4, of which waited for: 3 -> 3; matrix products, arithmetic and copies ran while one was open for 1% -> 1% of each run, Pallas kernels for 7% -> 8%
where the time goes in v8:
time: 22.1 us; the launch traced here: 22 us
  starting transfers between devices  7.13 us (32%)
  blocking collectives  6.1 us (28%)
  Pallas kernels  3.84 us (17%)
  waiting for transfers between devices  2.28 us (10%)
  between operations  2.07 us (9%)
  local copies, waits for them, and re-layouts  0.5 us (2%)
    all_gather x1, blocking collectives, local(): row = lax.all_gather(payload, 'wlk', axis=0)  6.1 us
    ppermute x1, starting transfers between devices, local(): lax.ppermute(mine, ('vec', 'wlk'), [((v ^ 2 * m + 1 - k % 2) * wlk_size +...  5.11 us
    ppermute x3, waiting for transfers between devices, swap(): return lax.ppermute(array, axis, [(i, partner(i)) for i in range(size)])  2.28 us
    pallas_call x3, Pallas kernels, partial_gradient(): call(functools.partial(gradient_kernel, norm_scale, len(chols)), jax.Shap...  2.11 us
    ppermute x3, starting transfers between devices, swap(): return lax.ppermute(array, axis, [(i, partner(i)) for i in range(size)])  2.02 us
    pallas_call x1, Pallas kernels, local(): call(final_kernel, (jax.ShapeDtypeStruct((occupied, basis), jnp.float32),...  1.58 us
    unnamed x7, local copies, waits for them, and re-layouts  0.5 us
  transfers between devices with their start and end apart: 4, of which 3 were waited for; matrix products, arithmetic and copies ran while one was open for 1% of the time, Pallas kernels for 8%

profile of v8, /device:TPU:0, one launch (start us, length us, event | category | flops | bytes accessed | tf_op | source)
XLA Modules:
  0.0 22.0 jit_solution(15367790701391146760)
XLA Ops:
  0.6 0.0 copy-start
  1.4 0.3 %copy-done = bf16[6,64,512]{2,1,0:T(8,128)(2,1)S(1)} copy-done((bf16[6,64,512]{2,1,0:T(8,128)(2,1)S(1)}, bf16[6,64,512]{2,1,0:T(8,128)(2,1)}, u32[]{:S(2)}) %copy-start) | copy-done | bytes 393240
  1.6 0.0 copy-start.1
  1.7 5.1 %collective-permute-start = (bf16[3,64,512]{2,1,0:T(8,128)(2,1)S(1)}, bf16[3,64,512]{2,1,0:T(8,128)(2,1)S(1)}, u32[]{:S(2)}, u32[]{:S(2)}) collective-permute-start(bf16[3,64,512]{2,1,0:T(8,128)(2,1)S(1)} %get-tuple-element.12.refs_0_), channel_id=1, source_target_pairs={{12,0},{9,1},{14,2},{11,3},{8,4},{13,5},{10,6},{15,7},{4,8},{1,9},... | collective-permute-start | bytes 589832 | tf_op jit(solution)/shard_map/ppermute | solution.py:194
  6.8 0.0 collective-permute-start.1
  7.4 0.0 copy-done.1
  7.5 6.1 %all-gather = bf16[320,512]{1,0:T(8,128)(2,1)S(1)} all-gather(bf16[80,512]{1,0:T(8,128)(2,1)S(1)} %shard_map.71), channel_id=2, replica_groups=mesh['grp'=2,'vec'=4,'wlk'=4] {'wlk'}, dimensions={0}, use_global_device_ids=true | all-gather | bytes 409600 | tf_op jit(solution)/shard_map/all_gather | solution.py:213
  13.6 0.0 copy-start.2
  13.6 0.1 shard_map.72
  13.7 0.1 collective-permute-done.1.refs_1_
  13.8 0.0 collective-permute-done.refs_2_
  13.9 0.3 %collective-permute-start.2 = (bf16[4,64,512]{2,1,0:T(8,128)(2,1)S(1)}, bf16[4,64,512]{2,1,0:T(8,128)(2,1)S(1)}, u32[]{:S(2)}, u32[]{:S(2)}) collective-permute-start(bf16[4,64,512]{2,1,0:T(8,128)(2,1)S(1)} %pad_maximum_fusion), channel_id=1, source_target_pairs={{0,1},{1,0},{2,3},{3,2},{4,5},{5,4},{6,7},{7,6},{8,9},{9,8},{10,11... | collective-permute-start | bytes 786440 | tf_op jit(solution)/shard_map/ppermute | solution.py:39
  14.2 0.7 %shard_map.74.refs_1_ = f32[64,512]{1,0:T(8,128)S(1)} custom-call(bf16[64,512]{1,0:T(8,128)(2,1)S(1)} %get-tuple-element.19.theta_ref, bf16[3,64,512]{2,1,0:T(8,128)(2,1)S(1)} %get-tuple-element.12.refs_0_, bf16[2,64,512]{2,1,0:T(8,128)(2,1)S(1)} %collective-permute-done.1.refs_1_, bf16[3,64,512]{2,1,0:T(8,128)(2,1)S(1)} %collective-permute-done.refs_2_), custom_call_target="tpu_custom_call" | custom-call | tf_op jit(solution)/shard_map/pallas_call | solution.py:118
  14.9 0.6 %collective-permute-done.2.refs_3_.refs_0_ = bf16[4,64,512]{2,1,0:T(8,128)(2,1)S(1)} collective-permute-done((bf16[4,64,512]{2,1,0:T(8,128)(2,1)S(1)}, bf16[4,64,512]{2,1,0:T(8,128)(2,1)S(1)}, u32[]{:S(2)}, u32[]{:S(2)}) %collective-permute-start.2) | collective-permute-done | bytes 262176 | tf_op jit(solution)/shard_map/ppermute | solution.py:39
  15.5 0.6 %shard_map.75 = bf16[64,512]{1,0:T(8,128)(2,1)S(1)} custom-call(bf16[64,512]{1,0:T(8,128)(2,1)S(1)} %get-tuple-element.19.theta_ref, bf16[4,64,512]{2,1,0:T(8,128)(2,1)S(1)} %collective-permute-done.2.refs_3_.refs_0_, f32[64,512]{1,0:T(8,128)S(1)} %shard_map.74.refs_1_), custom_call_target="tpu_custom_call" | custom-call | tf_op jit(solution)/shard_map/pallas_call | solution.py:118
  16.1 1.7 %collective-permute-start.3 = (bf16[64,512]{1,0:T(8,128)(2,1)S(1)}, bf16[64,512]{1,0:T(8,128)(2,1)S(1)}, u32[]{:S(2)}, u32[]{:S(2)}) collective-permute-start(bf16[64,512]{1,0:T(8,128)(2,1)S(1)} %shard_map.75), channel_id=1, source_target_pairs={{0,2},{1,3},{2,0},{3,1},{4,6},{5,7},{6,4},{7,5},{8,10},{9,11},{10,... | collective-permute-start | bytes 196616 | tf_op jit(solution)/shard_map/ppermute | solution.py:39
  17.8 0.0 copy-done.2
  17.8 0.2 copy.7
  18.0 0.8 %shard_map.73.own_ref = f32[64,512]{1,0:T(8,128)S(1)} custom-call(bf16[64,512]{1,0:T(8,128)(2,1)S(1)} %get-tuple-element.15.theta_ref, bf16[3,64,512]{2,1,0:T(8,128)(2,1)S(1)} %get-tuple-element.12.refs_0_, bf16[2,64,512]{2,1,0:T(8,128)(2,1)S(1)} %collective-permute-done.1.refs_1_, bf16[3,64,512]{2,1,0:T(8,128)(2,1)S(1)} %collective-permute-done.refs_2_, ...), custom_call_target="tpu_custom_call" | custom-call | tf_op jit(solution)/shard_map/pallas_call | solution.py:118
  18.8 1.6 %collective-permute-done.3.other_ref = bf16[64,512]{1,0:T(8,128)(2,1)S(1)} collective-permute-done((bf16[64,512]{1,0:T(8,128)(2,1)S(1)}, bf16[64,512]{1,0:T(8,128)(2,1)S(1)}, u32[]{:S(2)}, u32[]{:S(2)}) %collective-permute-start.3) | collective-permute-done | bytes 65568 | tf_op jit(solution)/shard_map/ppermute | solution.py:39
  20.4 1.6 %shard_map.76 = (f32[64,512]{1,0:T(8,128)}, f32[1]{0:T(128)}) custom-call(bf16[64,512]{1,0:T(8,128)(2,1)S(1)} %get-tuple-element.15.theta_ref, bf16[16,512]{1,0:T(8,128)(2,1)S(1)} %get-tuple-element.16.extra_ref, f32[64,512]{1,0:T(8,128)S(1)} %shard_map.73.own_ref, bf16[64,512]{1,0:T(8,128)(2,1)S(1)} %collective-permute-done.3.other_ref, ...), custom_call_target="tpu_custom_call" | custom-call | tf_op jit(solution)/shard_map/pallas_call | solution.py:235
  (6 shorter events, 0.1 us)
Async XLA Ops:
  0.6 1.0 %copy-start = (bf16[6,64,512]{2,1,0:T(8,128)(2,1)S(1)}, bf16[6,64,512]{2,1,0:T(8,128)(2,1)}, u32[]{:S(2)}) copy-start(bf16[6,64,512]{2,1,0:T(8,128)(2,1)} %chol_ref.1) | copy-start | bytes 1179652
  1.6 5.8 %copy-start.1 = (f32[1,64,512]{2,1,0:T(8,128)S(1)}, f32[1,64,512]{2,1,0:T(8,128)}, u32[]{:S(2)}) copy-start(f32[1,64,512]{2,1,0:T(8,128)} %orbitals_ref.1) | copy-start | bytes 393220
  1.7 12.2 %collective-permute-start = (bf16[3,64,512]{2,1,0:T(8,128)(2,1)S(1)}, bf16[3,64,512]{2,1,0:T(8,128)(2,1)S(1)}, u32[]{:S(2)}, u32[]{:S(2)}) collective-permute-start(bf16[3,64,512]{2,1,0:T(8,128)(2,1)S(1)} %get-tuple-element.12.refs_0_), channel_id=1, source_target_pairs={{12,0},{9,1},{14,2},{11,3},{8,4},{13,5},{10,6},{15,7},{4,8},{1,9},... | collective-permute-start | bytes 589832 | tf_op jit(solution)/shard_map/ppermute | solution.py:194
  6.8 7.0 %collective-permute-start.1 = (bf16[2,64,512]{2,1,0:T(8,128)(2,1)S(1)}, bf16[2,64,512]{2,1,0:T(8,128)(2,1)S(1)}, u32[]{:S(2)}, u32[]{:S(2)}) collective-permute-start(bf16[2,64,512]{2,1,0:T(8,128)(2,1)S(1)} %get-tuple-element.13), channel_id=1, source_target_pairs={{0,4},{4,0},{8,12},{12,8},{1,5},{5,1},{9,13},{13,9},{2,6},{6,2},{1... | collective-permute-start | bytes 393224 | tf_op jit(solution)/shard_map/ppermute | solution.py:39
  13.6 4.2 %copy-start.2 = (f32[512,512]{1,0:T(8,128)S(1)}, f32[512,512]{1,0:T(8,128)}, u32[]{:S(2)}) copy-start(f32[512,512]{1,0:T(8,128)} %param.9) | copy-start | bytes 3145732
  13.9 1.6 %collective-permute-start.2 = (bf16[4,64,512]{2,1,0:T(8,128)(2,1)S(1)}, bf16[4,64,512]{2,1,0:T(8,128)(2,1)S(1)}, u32[]{:S(2)}, u32[]{:S(2)}) collective-permute-start(bf16[4,64,512]{2,1,0:T(8,128)(2,1)S(1)} %pad_maximum_fusion), channel_id=1, source_target_pairs={{0,1},{1,0},{2,3},{3,2},{4,5},{5,4},{6,7},{7,6},{8,9},{9,8},{10,11... | collective-permute-start | bytes 786440 | tf_op jit(solution)/shard_map/ppermute | solution.py:39
  16.1 4.3 %collective-permute-start.3 = (bf16[64,512]{1,0:T(8,128)(2,1)S(1)}, bf16[64,512]{1,0:T(8,128)(2,1)S(1)}, u32[]{:S(2)}, u32[]{:S(2)}) collective-permute-start(bf16[64,512]{1,0:T(8,128)(2,1)S(1)} %shard_map.75), channel_id=1, source_target_pairs={{0,2},{1,3},{2,0},{3,1},{4,6},{5,7},{6,4},{7,5},{8,10},{9,11},{10,... | collective-permute-start | bytes 196616 | tf_op jit(solution)/shard_map/ppermute | solution.py:39

commit v9 on v8

--- a/solution.py
+++ b/solution.py
@@ -84,7 +84,7 @@
     own = chosen(here, row_ref.shape[1])
     theta_ref[...] = own[:occupied]
     extra_ref[...] = own[occupied:]
-    other_ref[...] = chosen(jnp.bitwise_xor(here, 2), occupied)
+    other_ref[...] = chosen(jnp.bitwise_xor(here, 3), occupied)
 
 
 def gradient_kernel(norm_scale, blocks, theta_ref, *refs):
@@ -229,7 +229,7 @@
     other = [swap(jnp.concatenate([sent, *far], axis=0), "wlk", lambda i: i ^ 1)]
     to_send = partial_gradient(norm_scale, neighbour, vectors, jnp.float32)
     to_send = partial_gradient(norm_scale, neighbour, other, jnp.bfloat16, to_send)
-    received = swap(to_send, "wlk", lambda i: i ^ 2)
+    received = swap(to_send, "wlk", lambda i: i ^ 3)
     own_part = partial_gradient(norm_scale, chosen, [*vectors, *other], jnp.float32)
 
     new_orbitals, new_logs = call(

time: 22.1 us -> 21.9 us (level)
  starting transfers between devices: 7.13 us -> 6.87 us
    ppermute x3, starting transfers between devices: 2.02 us -> 1.76 us  [swap(): return lax.ppermute(array, axis, [(i, partner(i)) for i in range(size)])]
where the time goes in v9:
time: 21.9 us; the launch traced here: 21.7 us
  starting transfers between devices  6.87 us (31%)
  blocking collectives  6.1 us (28%)
  Pallas kernels  3.84 us (18%)
  waiting for transfers between devices  2.32 us (11%)
  between operations  2.07 us (9%)
  local copies, waits for them, and re-layouts  0.5 us (2%)
    all_gather x1, blocking collectives, local(): row = lax.all_gather(payload, 'wlk', axis=0)  6.1 us
    ppermute x1, starting transfers between devices, local(): lax.ppermute(mine, ('vec', 'wlk'), [((v ^ 2 * m + 1 - k % 2) * wlk_size +...  5.11 us
    ppermute x3, waiting for transfers between devices, swap(): return lax.ppermute(array, axis, [(i, partner(i)) for i in range(size)])  2.32 us
    pallas_call x3, Pallas kernels, partial_gradient(): call(functools.partial(gradient_kernel, norm_scale, len(chols)), jax.Shap...  2.11 us
    ppermute x3, starting transfers between devices, swap(): return lax.ppermute(array, axis, [(i, partner(i)) for i in range(size)])  1.76 us
    pallas_call x1, Pallas kernels, local(): call(final_kernel, (jax.ShapeDtypeStruct((occupied, basis), jnp.float32),...  1.58 us
    unnamed x7, local copies, waits for them, and re-layouts  0.5 us
  transfers between devices with their start and end apart: 4, of which 3 were waited for; matrix products, arithmetic and copies ran while one was open for 1% of the time, Pallas kernels for 8%

profile of v9, /device:TPU:0, one launch (start us, length us, event | category | flops | bytes accessed | tf_op | source)
XLA Modules:
  0.0 21.7 jit_solution(16554541657487659897)
XLA Ops:
  0.6 0.0 copy-start
  1.4 0.3 %copy-done = bf16[6,64,512]{2,1,0:T(8,128)(2,1)S(1)} copy-done((bf16[6,64,512]{2,1,0:T(8,128)(2,1)S(1)}, bf16[6,64,512]{2,1,0:T(8,128)(2,1)}, u32[]{:S(2)}) %copy-start) | copy-done | bytes 393240
  1.6 0.0 copy-start.1
  1.7 5.1 %collective-permute-start = (bf16[3,64,512]{2,1,0:T(8,128)(2,1)S(1)}, bf16[3,64,512]{2,1,0:T(8,128)(2,1)S(1)}, u32[]{:S(2)}, u32[]{:S(2)}) collective-permute-start(bf16[3,64,512]{2,1,0:T(8,128)(2,1)S(1)} %get-tuple-element.12.refs_0_), channel_id=1, source_target_pairs={{12,0},{9,1},{14,2},{11,3},{8,4},{13,5},{10,6},{15,7},{4,8},{1,9},... | collective-permute-start | bytes 589832 | tf_op jit(solution)/shard_map/ppermute | solution.py:194
  6.8 0.0 collective-permute-start.1
  7.4 0.0 copy-done.1
  7.5 6.1 %all-gather = bf16[320,512]{1,0:T(8,128)(2,1)S(1)} all-gather(bf16[80,512]{1,0:T(8,128)(2,1)S(1)} %shard_map.71), channel_id=2, replica_groups=mesh['grp'=2,'vec'=4,'wlk'=4] {'wlk'}, dimensions={0}, use_global_device_ids=true | all-gather | bytes 409600 | tf_op jit(solution)/shard_map/all_gather | solution.py:213
  13.6 0.0 copy-start.2
  13.6 0.1 shard_map.72
  13.7 0.1 collective-permute-done.1.refs_1_
  13.8 0.0 collective-permute-done.refs_2_
  13.9 0.3 %collective-permute-start.2 = (bf16[4,64,512]{2,1,0:T(8,128)(2,1)S(1)}, bf16[4,64,512]{2,1,0:T(8,128)(2,1)S(1)}, u32[]{:S(2)}, u32[]{:S(2)}) collective-permute-start(bf16[4,64,512]{2,1,0:T(8,128)(2,1)S(1)} %pad_maximum_fusion), channel_id=1, source_target_pairs={{0,1},{1,0},{2,3},{3,2},{4,5},{5,4},{6,7},{7,6},{8,9},{9,8},{10,11... | collective-permute-start | bytes 786440 | tf_op jit(solution)/shard_map/ppermute | solution.py:39
  14.2 0.7 %shard_map.74.refs_1_ = f32[64,512]{1,0:T(8,128)S(1)} custom-call(bf16[64,512]{1,0:T(8,128)(2,1)S(1)} %get-tuple-element.19.theta_ref, bf16[3,64,512]{2,1,0:T(8,128)(2,1)S(1)} %get-tuple-element.12.refs_0_, bf16[2,64,512]{2,1,0:T(8,128)(2,1)S(1)} %collective-permute-done.1.refs_1_, bf16[3,64,512]{2,1,0:T(8,128)(2,1)S(1)} %collective-permute-done.refs_2_), custom_call_target="tpu_custom_call" | custom-call | tf_op jit(solution)/shard_map/pallas_call | solution.py:118
  14.9 0.6 %collective-permute-done.2.refs_3_.refs_0_ = bf16[4,64,512]{2,1,0:T(8,128)(2,1)S(1)} collective-permute-done((bf16[4,64,512]{2,1,0:T(8,128)(2,1)S(1)}, bf16[4,64,512]{2,1,0:T(8,128)(2,1)S(1)}, u32[]{:S(2)}, u32[]{:S(2)}) %collective-permute-start.2) | collective-permute-done | bytes 262176 | tf_op jit(solution)/shard_map/ppermute | solution.py:39
  15.5 0.6 %shard_map.75 = bf16[64,512]{1,0:T(8,128)(2,1)S(1)} custom-call(bf16[64,512]{1,0:T(8,128)(2,1)S(1)} %get-tuple-element.19.theta_ref, bf16[4,64,512]{2,1,0:T(8,128)(2,1)S(1)} %collective-permute-done.2.refs_3_.refs_0_, f32[64,512]{1,0:T(8,128)S(1)} %shard_map.74.refs_1_), custom_call_target="tpu_custom_call" | custom-call | tf_op jit(solution)/shard_map/pallas_call | solution.py:118
  16.1 1.4 %collective-permute-start.3 = (bf16[64,512]{1,0:T(8,128)(2,1)S(1)}, bf16[64,512]{1,0:T(8,128)(2,1)S(1)}, u32[]{:S(2)}, u32[]{:S(2)}) collective-permute-start(bf16[64,512]{1,0:T(8,128)(2,1)S(1)} %shard_map.75), channel_id=1, source_target_pairs={{0,3},{1,2},{2,1},{3,0},{4,7},{5,6},{6,5},{7,4},{8,11},{9,10},{10,... | collective-permute-start | bytes 196616 | tf_op jit(solution)/shard_map/ppermute | solution.py:39
  17.5 0.0 copy-done.2
  17.5 0.2 copy.7
  17.7 0.8 %shard_map.73.own_ref = f32[64,512]{1,0:T(8,128)S(1)} custom-call(bf16[64,512]{1,0:T(8,128)(2,1)S(1)} %get-tuple-element.15.theta_ref, bf16[3,64,512]{2,1,0:T(8,128)(2,1)S(1)} %get-tuple-element.12.refs_0_, bf16[2,64,512]{2,1,0:T(8,128)(2,1)S(1)} %collective-permute-done.1.refs_1_, bf16[3,64,512]{2,1,0:T(8,128)(2,1)S(1)} %collective-permute-done.refs_2_, ...), custom_call_target="tpu_custom_call" | custom-call | tf_op jit(solution)/shard_map/pallas_call | solution.py:118
  18.6 1.6 %collective-permute-done.3.other_ref = bf16[64,512]{1,0:T(8,128)(2,1)S(1)} collective-permute-done((bf16[64,512]{1,0:T(8,128)(2,1)S(1)}, bf16[64,512]{1,0:T(8,128)(2,1)S(1)}, u32[]{:S(2)}, u32[]{:S(2)}) %collective-permute-start.3) | collective-permute-done | bytes 65568 | tf_op jit(solution)/shard_map/ppermute | solution.py:39
  20.2 1.6 %shard_map.76 = (f32[64,512]{1,0:T(8,128)}, f32[1]{0:T(128)}) custom-call(bf16[64,512]{1,0:T(8,128)(2,1)S(1)} %get-tuple-element.15.theta_ref, bf16[16,512]{1,0:T(8,128)(2,1)S(1)} %get-tuple-element.16.extra_ref, f32[64,512]{1,0:T(8,128)S(1)} %shard_map.73.own_ref, bf16[64,512]{1,0:T(8,128)(2,1)S(1)} %collective-permute-done.3.other_ref, ...), custom_call_target="tpu_custom_call" | custom-call | tf_op jit(solution)/shard_map/pallas_call | solution.py:235
  (6 shorter events, 0.1 us)
Async XLA Ops:
  0.6 1.0 %copy-start = (bf16[6,64,512]{2,1,0:T(8,128)(2,1)S(1)}, bf16[6,64,512]{2,1,0:T(8,128)(2,1)}, u32[]{:S(2)}) copy-start(bf16[6,64,512]{2,1,0:T(8,128)(2,1)} %chol_ref.1) | copy-start | bytes 1179652
  1.6 5.8 %copy-start.1 = (f32[1,64,512]{2,1,0:T(8,128)S(1)}, f32[1,64,512]{2,1,0:T(8,128)}, u32[]{:S(2)}) copy-start(f32[1,64,512]{2,1,0:T(8,128)} %orbitals_ref.1) | copy-start | bytes 393220
  1.7 12.2 %collective-permute-start = (bf16[3,64,512]{2,1,0:T(8,128)(2,1)S(1)}, bf16[3,64,512]{2,1,0:T(8,128)(2,1)S(1)}, u32[]{:S(2)}, u32[]{:S(2)}) collective-permute-start(bf16[3,64,512]{2,1,0:T(8,128)(2,1)S(1)} %get-tuple-element.12.refs_0_), channel_id=1, source_target_pairs={{12,0},{9,1},{14,2},{11,3},{8,4},{13,5},{10,6},{15,7},{4,8},{1,9},... | collective-permute-start | bytes 589832 | tf_op jit(solution)/shard_map/ppermute | solution.py:194
  6.8 7.0 %collective-permute-start.1 = (bf16[2,64,512]{2,1,0:T(8,128)(2,1)S(1)}, bf16[2,64,512]{2,1,0:T(8,128)(2,1)S(1)}, u32[]{:S(2)}, u32[]{:S(2)}) collective-permute-start(bf16[2,64,512]{2,1,0:T(8,128)(2,1)S(1)} %get-tuple-element.13), channel_id=1, source_target_pairs={{0,4},{4,0},{8,12},{12,8},{1,5},{5,1},{9,13},{13,9},{2,6},{6,2},{1... | collective-permute-start | bytes 393224 | tf_op jit(solution)/shard_map/ppermute | solution.py:39
  13.6 3.9 %copy-start.2 = (f32[512,512]{1,0:T(8,128)S(1)}, f32[512,512]{1,0:T(8,128)}, u32[]{:S(2)}) copy-start(f32[512,512]{1,0:T(8,128)} %param.9) | copy-start | bytes 3145732
  13.9 1.6 %collective-permute-start.2 = (bf16[4,64,512]{2,1,0:T(8,128)(2,1)S(1)}, bf16[4,64,512]{2,1,0:T(8,128)(2,1)S(1)}, u32[]{:S(2)}, u32[]{:S(2)}) collective-permute-start(bf16[4,64,512]{2,1,0:T(8,128)(2,1)S(1)} %pad_maximum_fusion), channel_id=1, source_target_pairs={{0,1},{1,0},{2,3},{3,2},{4,5},{5,4},{6,7},{7,6},{8,9},{9,8},{10,11... | collective-permute-start | bytes 786440 | tf_op jit(solution)/shard_map/ppermute | solution.py:39
  16.1 4.1 %collective-permute-start.3 = (bf16[64,512]{1,0:T(8,128)(2,1)S(1)}, bf16[64,512]{1,0:T(8,128)(2,1)S(1)}, u32[]{:S(2)}, u32[]{:S(2)}) collective-permute-start(bf16[64,512]{1,0:T(8,128)(2,1)S(1)} %shard_map.75), channel_id=1, source_target_pairs={{0,3},{1,2},{2,1},{3,0},{4,7},{5,6},{6,5},{7,4},{8,11},{9,10},{10,... | collective-permute-start | bytes 196616 | tf_op jit(solution)/shard_map/ppermute | solution.py:39

commit v10 on v9

--- a/solution.py
+++ b/solution.py
@@ -39,12 +39,14 @@
     return lax.ppermute(array, axis, [(i, partner(i)) for i in range(size)])
 
 
-def half_kernel(parent_ref, chol_ref, mine_ref, pair_ref):
-    half, pair = mine_ref.shape[0], pair_ref.shape[0]
+def half_kernel(parent_ref, chol_ref, mine_ref, part_ref):
+    half, _, basis = mine_ref.shape
     here = lax.axis_index("wlk")
-    first = lax.rem(here // 2, 2) * half
-    mine_ref[...] = chol_ref[pl.ds(first, half)]
-    pair_ref[...] = chol_ref[pl.ds(first + lax.rem(here, 2) * (half - pair), pair)]
+    mine = chol_ref[pl.ds(lax.rem(here // 2, 2) * half, half)]
+    mine_ref[...] = mine
+    mine = mine.reshape(-1, basis)
+    rows = part_ref.shape[0]
+    part_ref[...] = jnp.where(lax.rem(here, 2) == 0, mine[:rows], mine[rows:])
 
 
 def blank_kernel(out_ref):
@@ -87,41 +89,62 @@
     other_ref[...] = chosen(jnp.bitwise_xor(here, 3), occupied)
 
 
-def gradient_kernel(norm_scale, blocks, theta_ref, *refs):
-    chol_refs, sum_refs = refs[:blocks], refs[blocks:-2]
-    out_ref, adjoint = refs[-2:]
+def gradient_kernel(norm_scale, blocks, exchanged, theta_ref, *refs):
+    *in_refs, out_ref, adjoint = refs
     occupied, basis = theta_ref.shape
     theta = theta_ref[...]
     rows = lax.broadcasted_iota(jnp.int32, (occupied, occupied), 0)
     columns = lax.broadcasted_iota(jnp.int32, (occupied, occupied), 1)
     diagonal = rows == columns
-    chol = jnp.concatenate([ref[...].reshape(-1, basis) for ref in chol_refs], axis=0)
-    turned = lax.dot_general(
-        chol, theta, (((1,), (1,)), ((), ())), preferred_element_type=jnp.float32
-    )
-    turned = turned.astype(jnp.bfloat16).astype(jnp.float32)
-    for place in range(0, chol.shape[0], occupied):
-        block = turned[place : place + occupied, :]
-        on_diagonal = jnp.where(diagonal, block, 0.0)
-        trace = jnp.sum(jnp.sum(on_diagonal, axis=0, keepdims=True), axis=1, keepdims=True)
-        piece = norm_scale * (jnp.where(diagonal, trace, 0.0) - block)
-        adjoint[:, place : place + occupied] = piece.astype(jnp.bfloat16)
-    total = jnp.dot(adjoint[...], chol, preferred_element_type=jnp.float32)
-    if sum_refs:
-        total = total + sum_refs[0][...]
+    chols = [ref[...].reshape(-1, basis) for ref in in_refs[:blocks]]
+    if exchanged:
+        part_ref, other_ref = in_refs[blocks : blocks + 2]
+        part, other = part_ref[...], other_ref[: part_ref.shape[0], :]
+        is_first = lax.rem(lax.axis_index("wlk"), 2) == 0
+        chols.append(
+            jnp.concatenate(
+                [jnp.where(is_first, part, other), jnp.where(is_first, other, part)], axis=0
+            )
+        )
+        chols.append(other_ref[part_ref.shape[0] :, :])
+    sum_refs = in_refs[blocks + 2 * exchanged :]
+    turned = [
+        lax.dot_general(chol, theta, (((1,), (1,)), ((), ())), preferred_element_type=jnp.float32)
+        for chol in chols
+    ]
+    place = 0
+    for product in turned:
+        product = product.astype(jnp.bfloat16).astype(jnp.float32)
+        for g in range(product.shape[0] // occupied):
+            block = product[g * occupied : (g + 1) * occupied, :]
+            on_diagonal = jnp.where(diagonal, block, 0.0)
+            trace = jnp.sum(jnp.sum(on_diagonal, axis=0, keepdims=True), axis=1, keepdims=True)
+            piece = norm_scale * (jnp.where(diagonal, trace, 0.0) - block)
+            adjoint[:, place : place + occupied] = piece.astype(jnp.bfloat16)
+            place += occupied
+    total = sum_refs[0][...] if sum_refs else None
+    place = 0
+    for chol in chols:
+        width = chol.shape[0]
+        term = jnp.dot(
+            adjoint[:, place : place + width], chol, preferred_element_type=jnp.float32
+        )
+        total = term if total is None else total + term
+        place += width
     out_ref[...] = total.astype(out_ref.dtype)
 
 
-def partial_gradient(norm_scale, theta, chols, dtype, *summand):
+def partial_gradient(norm_scale, theta, chols, exchanged, dtype, *summand):
     occupied, basis = theta.shape
-    width = sum(c.shape[0] for c in chols) * occupied
+    arrays = [*chols, *exchanged]
+    width = sum(math.prod(a.shape[:-1]) for a in arrays)
     return call(
-        functools.partial(gradient_kernel, norm_scale, len(chols)),
+        functools.partial(gradient_kernel, norm_scale, len(chols), len(exchanged) // 2),
         jax.ShapeDtypeStruct((occupied, basis), dtype),
-        vmem(1 + len(chols) + len(summand)),
+        vmem(1 + len(arrays) + len(summand)),
         pl.BlockSpec(memory_space=pltpu.VMEM),
         [pltpu.VMEM((occupied, width), jnp.bfloat16)],
-    )(theta, *chols, *summand)
+    )(theta, *arrays, *summand)
 
 
 def final_kernel(theta_ref, extra_ref, own_ref, other_ref, propagator_ref, out_ref, log_ref):
@@ -164,7 +187,6 @@
     vec_size, wlk_size = lax.axis_size("vec"), lax.axis_size("wlk")
     norm_scale = 1.0 / math.sqrt(vectors_here * vec_size)
     half = vectors_here // 2
-    pair = (half + 1) // 2
     smem = pl.BlockSpec(memory_space=pltpu.SMEM)
 
     blank = call(
@@ -185,7 +207,7 @@
         half_kernel,
         (
             jax.ShapeDtypeStruct((half, occupied, basis), cholesky.dtype),
-            jax.ShapeDtypeStruct((pair, occupied, basis), cholesky.dtype),
+            jax.ShapeDtypeStruct((half * occupied // 2, basis), cholesky.dtype),
         ),
         vmem(2),
         vmem(2),
@@ -223,14 +245,13 @@
     )(row)
 
     *far, near, chosen = lax.optimization_barrier((*far, near, chosen))
-    lacking = half - pair
-    sent = lax.dynamic_slice_in_dim(near, lax.axis_index("wlk") % 2 * (pair - lacking), lacking, 0)
-    vectors = [mine, near, *far]
-    other = [swap(jnp.concatenate([sent, *far], axis=0), "wlk", lambda i: i ^ 1)]
-    to_send = partial_gradient(norm_scale, neighbour, vectors, jnp.float32)
-    to_send = partial_gradient(norm_scale, neighbour, other, jnp.bfloat16, to_send)
+    fetched = jnp.concatenate([near, *[c.reshape(-1, basis) for c in far]], axis=0)
+    exchanged = [near, swap(fetched, "wlk", lambda i: i ^ 1)]
+    vectors = [mine, *far]
+    to_send = partial_gradient(norm_scale, neighbour, vectors, [], jnp.float32)
+    to_send = partial_gradient(norm_scale, neighbour, [], exchanged, jnp.bfloat16, to_send)
     received = swap(to_send, "wlk", lambda i: i ^ 3)
-    own_part = partial_gradient(norm_scale, chosen, [*vectors, *other], jnp.float32)
+    own_part = partial_gradient(norm_scale, chosen, vectors, exchanged, jnp.float32)
 
     new_orbitals, new_logs = call(
         final_kernel,

time: 21.9 us -> 22 us (level); the launches traced: 21.7 us -> 21.6 us
  transfers between devices with their start and end apart: 4 -> 4, of which waited for: 3 -> 2; matrix products, arithmetic and copies ran while one was open for 1% -> 1% of each run, Pallas kernels for 8% -> 7%
where the time goes in v10:
time: 22 us; the launch traced here: 21.6 us
  starting transfers between devices  6.89 us (31%)
  blocking collectives  6.1 us (28%)
  Pallas kernels  3.75 us (17%)
  waiting for transfers between devices  2.27 us (10%)
  between operations  2.08 us (9%)
  local copies, waits for them, and re-layouts  0.5 us (2%)
    all_gather x1, blocking collectives, local(): row = lax.all_gather(payload, 'wlk', axis=0)  6.1 us
    ppermute x1, starting transfers between devices, local(): lax.ppermute(mine, ('vec', 'wlk'), [((v ^ 2 * m + 1 - k % 2) * wlk_size +...  5.11 us
    ppermute x3, waiting for transfers between devices, swap(): return lax.ppermute(array, axis, [(i, partner(i)) for i in range(size)])  2.26 us
    pallas_call x3, Pallas kernels, partial_gradient(): call(functools.partial(gradient_kernel, norm_scale, len(chols), len(excha...  2.01 us
    ppermute x3, starting transfers between devices, swap(): return lax.ppermute(array, axis, [(i, partner(i)) for i in range(size)])  1.78 us
    pallas_call x1, Pallas kernels, local(): call(final_kernel, (jax.ShapeDtypeStruct((occupied, basis), jnp.float32),...  1.58 us
    unnamed x7, local copies, waits for them, and re-layouts  0.5 us
  transfers between devices with their start and end apart: 4, of which 2 were waited for; matrix products, arithmetic and copies ran while one was open for 1% of the time, Pallas kernels for 7%

profile of v10, /device:TPU:0, one launch (start us, length us, event | category | flops | bytes accessed | tf_op | source)
XLA Modules:
  0.0 21.6 jit_solution(4598898240604972203)
XLA Ops:
  0.6 0.0 copy-start
  1.4 0.3 %copy-done = bf16[6,64,512]{2,1,0:T(8,128)(2,1)S(1)} copy-done((bf16[6,64,512]{2,1,0:T(8,128)(2,1)S(1)}, bf16[6,64,512]{2,1,0:T(8,128)(2,1)}, u32[]{:S(2)}) %copy-start) | copy-done | bytes 393240
  1.6 0.0 copy-start.1
  1.7 5.1 %collective-permute-start = (bf16[3,64,512]{2,1,0:T(8,128)(2,1)S(1)}, bf16[3,64,512]{2,1,0:T(8,128)(2,1)S(1)}, u32[]{:S(2)}, u32[]{:S(2)}) collective-permute-start(bf16[3,64,512]{2,1,0:T(8,128)(2,1)S(1)} %get-tuple-element.12.refs_0_), channel_id=1, source_target_pairs={{12,0},{9,1},{14,2},{11,3},{8,4},{13,5},{10,6},{15,7},{4,8},{1,9},... | collective-permute-start | bytes 589832 | tf_op jit(solution)/shard_map/ppermute | solution.py:216
  6.8 0.0 collective-permute-start.1
  7.4 0.0 copy-done.1
  7.5 6.1 %all-gather = bf16[320,512]{1,0:T(8,128)(2,1)S(1)} all-gather(bf16[80,512]{1,0:T(8,128)(2,1)S(1)} %shard_map.71), channel_id=2, replica_groups=mesh['grp'=2,'vec'=4,'wlk'=4] {'wlk'}, dimensions={0}, use_global_device_ids=true | all-gather | bytes 409600 | tf_op jit(solution)/shard_map/all_gather | solution.py:235
  13.6 0.0 copy-start.2
  13.6 0.1 shard_map.72
  13.7 0.0 collective-permute-done.1.refs_2_.refs_0_
  13.7 0.0 collective-permute-done.refs_1_
  13.7 0.4 %collective-permute-start.2 = (bf16[288,512]{1,0:T(8,128)(2,1)S(1)}, bf16[288,512]{1,0:T(8,128)(2,1)S(1)}, u32[]{:S(2)}, u32[]{:S(2)}) collective-permute-start(bf16[288,512]{1,0:T(8,128)(2,1)S(1)} %pad_maximum_fusion), channel_id=1, source_target_pairs={{0,1},{1,0},{2,3},{3,2},{4,5},{5,4},{6,7},{7,6},{8,9},{9,8},{10,11... | collective-permute-start | bytes 884744 | tf_op jit(solution)/shard_map/ppermute | solution.py:39
  14.2 0.7 %shard_map.74.refs_2_ = f32[64,512]{1,0:T(8,128)S(1)} custom-call(bf16[64,512]{1,0:T(8,128)(2,1)S(1)} %get-tuple-element.19.theta_ref, bf16[3,64,512]{2,1,0:T(8,128)(2,1)S(1)} %get-tuple-element.12.refs_0_, bf16[3,64,512]{2,1,0:T(8,128)(2,1)S(1)} %collective-permute-done.refs_1_), custom_call_target="tpu_custom_call" | custom-call | tf_op jit(solution)/shard_map/pallas_call | solution.py:141
  14.8 0.6 %collective-permute-done.2.refs_3_.refs_1_ = bf16[288,512]{1,0:T(8,128)(2,1)S(1)} collective-permute-done((bf16[288,512]{1,0:T(8,128)(2,1)S(1)}, bf16[288,512]{1,0:T(8,128)(2,1)S(1)}, u32[]{:S(2)}, u32[]{:S(2)}) %collective-permute-start.2) | collective-permute-done | bytes 294944 | tf_op jit(solution)/shard_map/ppermute | solution.py:39
  15.4 0.6 %shard_map.75 = bf16[64,512]{1,0:T(8,128)(2,1)S(1)} custom-call(bf16[64,512]{1,0:T(8,128)(2,1)S(1)} %get-tuple-element.19.theta_ref, bf16[96,512]{1,0:T(8,128)(2,1)S(1)} %collective-permute-done.1.refs_2_.refs_0_, bf16[288,512]{1,0:T(8,128)(2,1)S(1)} %collective-permute-done.2.refs_3_.refs_1_, f32[64,512]{1,0:T(8,128)S(1)} %shard_map.74.refs_2_), custom_call_target="tpu_custom_call" | custom-call | tf_op jit(solution)/shard_map/pallas_call | solution.py:141
  16.0 1.4 %collective-permute-start.3 = (bf16[64,512]{1,0:T(8,128)(2,1)S(1)}, bf16[64,512]{1,0:T(8,128)(2,1)S(1)}, u32[]{:S(2)}, u32[]{:S(2)}) collective-permute-start(bf16[64,512]{1,0:T(8,128)(2,1)S(1)} %shard_map.75), channel_id=1, source_target_pairs={{0,3},{1,2},{2,1},{3,0},{4,7},{5,6},{6,5},{7,4},{8,11},{9,10},{10,... | collective-permute-start | bytes 196616 | tf_op jit(solution)/shard_map/ppermute | solution.py:39
  17.4 0.0 copy-done.2
  17.4 0.2 copy.7
  17.6 0.7 %shard_map.73.own_ref = f32[64,512]{1,0:T(8,128)S(1)} custom-call(bf16[64,512]{1,0:T(8,128)(2,1)S(1)} %get-tuple-element.15.theta_ref, bf16[3,64,512]{2,1,0:T(8,128)(2,1)S(1)} %get-tuple-element.12.refs_0_, bf16[3,64,512]{2,1,0:T(8,128)(2,1)S(1)} %collective-permute-done.refs_1_, bf16[96,512]{1,0:T(8,128)(2,1)S(1)} %collective-permute-done.1.refs_2_.refs_0_, ...), custom_call_target="tpu_custom_call" | custom-call | tf_op jit(solution)/shard_map/pallas_call | solution.py:141
  18.3 1.7 %collective-permute-done.3.other_ref = bf16[64,512]{1,0:T(8,128)(2,1)S(1)} collective-permute-done((bf16[64,512]{1,0:T(8,128)(2,1)S(1)}, bf16[64,512]{1,0:T(8,128)(2,1)S(1)}, u32[]{:S(2)}, u32[]{:S(2)}) %collective-permute-start.3) | collective-permute-done | bytes 65568 | tf_op jit(solution)/shard_map/ppermute | solution.py:39
  20.0 1.6 %shard_map.76 = (f32[64,512]{1,0:T(8,128)}, f32[1]{0:T(128)}) custom-call(bf16[64,512]{1,0:T(8,128)(2,1)S(1)} %get-tuple-element.15.theta_ref, bf16[16,512]{1,0:T(8,128)(2,1)S(1)} %get-tuple-element.16.extra_ref, f32[64,512]{1,0:T(8,128)S(1)} %shard_map.73.own_ref, bf16[64,512]{1,0:T(8,128)(2,1)S(1)} %collective-permute-done.3.other_ref, ...), custom_call_target="tpu_custom_call" | custom-call | tf_op jit(solution)/shard_map/pallas_call | solution.py:256
  (5 shorter events, 0.1 us)
Async XLA Ops:
  0.6 1.0 %copy-start = (bf16[6,64,512]{2,1,0:T(8,128)(2,1)S(1)}, bf16[6,64,512]{2,1,0:T(8,128)(2,1)}, u32[]{:S(2)}) copy-start(bf16[6,64,512]{2,1,0:T(8,128)(2,1)} %chol_ref.1) | copy-start | bytes 1179652
  1.6 5.8 %copy-start.1 = (f32[1,64,512]{2,1,0:T(8,128)S(1)}, f32[1,64,512]{2,1,0:T(8,128)}, u32[]{:S(2)}) copy-start(f32[1,64,512]{2,1,0:T(8,128)} %orbitals_ref.1) | copy-start | bytes 393220
  1.7 12.0 %collective-permute-start = (bf16[3,64,512]{2,1,0:T(8,128)(2,1)S(1)}, bf16[3,64,512]{2,1,0:T(8,128)(2,1)S(1)}, u32[]{:S(2)}, u32[]{:S(2)}) collective-permute-start(bf16[3,64,512]{2,1,0:T(8,128)(2,1)S(1)} %get-tuple-element.12.refs_0_), channel_id=1, source_target_pairs={{12,0},{9,1},{14,2},{11,3},{8,4},{13,5},{10,6},{15,7},{4,8},{1,9},... | collective-permute-start | bytes 589832 | tf_op jit(solution)/shard_map/ppermute | solution.py:216
  6.8 6.9 %collective-permute-start.1 = (bf16[96,512]{1,0:T(8,128)(2,1)S(1)}, bf16[96,512]{1,0:T(8,128)(2,1)S(1)}, u32[]{:S(2)}, u32[]{:S(2)}) collective-permute-start(bf16[96,512]{1,0:T(8,128)(2,1)S(1)} %get-tuple-element.13), channel_id=1, source_target_pairs={{0,4},{4,0},{8,12},{12,8},{1,5},{5,1},{9,13},{13,9},{2,6},{6,2},{1... | collective-permute-start | bytes 294920 | tf_op jit(solution)/shard_map/ppermute | solution.py:39
  13.6 3.8 %copy-start.2 = (f32[512,512]{1,0:T(8,128)S(1)}, f32[512,512]{1,0:T(8,128)}, u32[]{:S(2)}) copy-start(f32[512,512]{1,0:T(8,128)} %param.9) | copy-start | bytes 3145732
  13.7 1.6 %collective-permute-start.2 = (bf16[288,512]{1,0:T(8,128)(2,1)S(1)}, bf16[288,512]{1,0:T(8,128)(2,1)S(1)}, u32[]{:S(2)}, u32[]{:S(2)}) collective-permute-start(bf16[288,512]{1,0:T(8,128)(2,1)S(1)} %pad_maximum_fusion), channel_id=1, source_target_pairs={{0,1},{1,0},{2,3},{3,2},{4,5},{5,4},{6,7},{7,6},{8,9},{9,8},{10,11... | collective-permute-start | bytes 884744 | tf_op jit(solution)/shard_map/ppermute | solution.py:39
  16.0 4.0 %collective-permute-start.3 = (bf16[64,512]{1,0:T(8,128)(2,1)S(1)}, bf16[64,512]{1,0:T(8,128)(2,1)S(1)}, u32[]{:S(2)}, u32[]{:S(2)}) collective-permute-start(bf16[64,512]{1,0:T(8,128)(2,1)S(1)} %shard_map.75), channel_id=1, source_target_pairs={{0,3},{1,2},{2,1},{3,0},{4,7},{5,6},{6,5},{7,4},{8,11},{9,10},{10,... | collective-permute-start | bytes 196616 | tf_op jit(solution)/shard_map/ppermute | solution.py:39
